TPU v7x, 128 devices: a whole 4x4x4 slice. The times are simulated.
128 devices in a mesh: sx: 16 (over x, z_lo, core), sy: 8 (over y, z_hi).
Axes of the slice: x: 4, y: 4, z: 4 (z_hi: 2, z_lo: 2; z = z_hi * 2 + z_lo), core: 2. Of those that a mesh axis runs over, the one named last changes fastest.
Arguments:
- volume: bfloat16 [64, 64, 256, 64], P('sx', 'sy'), may hold values from -6 to 6
- first_kernel: bfloat16 [3, 3, 3, 64, 128], replicated, may hold values from -0.15625 to 0.15625
- second_kernel: bfloat16 [3, 3, 3, 128, 128], P(None, None, None, None, 'sx'), may hold values from -0.109375 to 0.109375
- third_kernel: bfloat16 [3, 3, 3, 128, 128], P(None, None, None, 'sx'), may hold values from -0.109375 to 0.109375
- cotangent: bfloat16 [32, 32, 128, 128], P('sy', None, None, 'sx'), may hold values from -0.119628906 to 0.119628906
Outputs:
- output: bfloat16 [32, 32, 128, 128], P('sy', None, None, 'sx')
- first_grad: float32 [3, 3, 3, 64, 128], replicated
- second_grad: float32 [3, 3, 3, 128, 128], P(None, None, None, None, 'sx')
- third_grad: float32 [3, 3, 3, 128, 128], P(None, None, None, 'sx')
All inputs are finite; a program needn't handle non-finite values.
Results may differ from a plain program's by a relative error of at most 0.034.
The roundings to bfloat16 on the way count: a program that leaves them out, or rounds other values in their place, can miss the bound.
Values may be sent and summed in bfloat16 or wider, within the bound.
No kernel may reach another device: no remote copies, remote signals or barrier semaphores. Data moves between devices by JAX's collectives and lax.ppermute only.
A program may use at most 192 MiB of HBM per device.

v0:
```python
import jax
import jax.numpy as jnp
from jax import lax
from jax.sharding import PartitionSpec as P

leak_slope = 0.2


def as_sent(shard):
    return jax.tree.map(lambda a: a.astype(jnp.bfloat16) if a.dtype == jnp.float32 else a, shard)


def padded_2(cells, sides, width):
    for axis, dim in sides:
        count = lax.axis_size(axis)
        ends = count - 1
        head = lax.slice_in_dim(cells, 0, width, axis=dim)
        tail = lax.slice_in_dim(cells, cells.shape[dim] - width, cells.shape[dim], axis=dim)
        cells = jnp.concatenate(
            [
                lax.ppermute(tail, axis, [(i, (i + 1) % count) for i in range(ends)]),
                cells,
                lax.ppermute(head, axis, [((i + 1) % count, i) for i in range(ends)]),
            ],
            axis=dim,
        )
    return cells


def conv_valid(padded, kernel):
    return lax.conv_general_dilated(
        padded[None],
        kernel,
        (1, 1, 1),
        "VALID",
        dimension_numbers=("NDHWC", "DHWIO", "NDHWC"),
        preferred_element_type=jnp.float32,
    )[0]


def flipped(kernel):
    return jnp.swapaxes(kernel[::-1, ::-1, ::-1], 3, 4)


def kernel_grad(padded, cotangent):
    depth_cells, height_cells, width_cells, out_width = cotangent.shape
    inner_width = padded.shape[3]
    flat_cot = cotangent.reshape(-1, out_width)
    tap_list = []
    for a in range(3):
        for b in range(3):
            for c in range(3):
                window = padded[
                    a : a + depth_cells, b : b + height_cells, c : c + width_cells
                ].reshape(-1, inner_width)
                tap_list.append(
                    lax.dot_general(
                        window,
                        flat_cot,
                        (((0,), (0,)), ((), ())),
                        preferred_element_type=jnp.float32,
                    )
                )
    return jnp.stack(tap_list).reshape(3, 3, 3, inner_width, out_width)


def leaky_relu(values):
    return jnp.where(values > 0, values, leak_slope * values)


def leaky_slope(values):
    return jnp.where(values > 0, 1.0, leak_slope)


def pad_width(values):
    return jnp.pad(values, ((0, 0), (0, 0), (1, 1), (0, 0)))


def to_channels(values):
    return jax.tree.map(
        lambda part, own: part.astype(own.dtype),
        lax.all_to_all(
            lax.all_to_all(as_sent(values), "sx", split_axis=3, concat_axis=0, tiled=True),
            "sy",
            split_axis=0,
            concat_axis=1,
            tiled=True,
        ),
        values,
    )


def to_space(values):
    return lax.all_to_all(
        lax.all_to_all(values, "sy", split_axis=1, concat_axis=0, tiled=True),
        "sx",
        split_axis=0,
        concat_axis=3,
        tiled=True,
    )


def mid_faces(values):
    return pad_width(padded_2(values, (("sx", 0), ("sy", 1)), 1))


def finish_grads(second_grad, third_grad):
    return (
        lax.psum(second_grad.astype(jnp.bfloat16), "sy").astype(jnp.float32),
        lax.psum(third_grad.astype(jnp.bfloat16), "sy").astype(jnp.float32),
    )


def on_device(volume, first_kernel, second_kernel, third_kernel, cotangent):
    volume_pad = pad_width(padded_2(volume, (("sx", 0), ("sy", 1)), 1))
    first_pre = conv_valid(volume_pad, first_kernel)
    depth_cells, height_cells, width_cells, channels = first_pre.shape
    pooled = (
        leaky_relu(first_pre)
        .reshape(depth_cells // 2, 2, height_cells // 2, 2, width_cells // 2, 2, channels)
        .mean(axis=(1, 3, 5))
        .astype(jnp.bfloat16)
    )
    second_full, third_turned = (
        lax.all_gather(second_kernel, "sx", axis=4, tiled=True),
        lax.all_gather(jnp.swapaxes(third_kernel, 3, 4), "sx", axis=4, tiled=True),
    )
    third_full = jnp.swapaxes(third_turned, 3, 4)
    pooled_pad = mid_faces(pooled)
    second_pre = conv_valid(pooled_pad, second_full)
    hidden = leaky_relu(second_pre).astype(jnp.bfloat16)
    hidden_pad = mid_faces(hidden)
    output = to_channels(conv_valid(hidden_pad, third_full).astype(jnp.bfloat16))
    cot_space = to_space(cotangent)
    hidden_grad = conv_valid(mid_faces(cot_space), flipped(third_full))
    third_whole = kernel_grad(hidden_pad, cot_space)
    second_pre_grad = (hidden_grad * leaky_slope(second_pre)).astype(jnp.bfloat16)
    second_whole = kernel_grad(pooled_pad, second_pre_grad)
    pooled_grad = conv_valid(mid_faces(second_pre_grad), flipped(second_full)).astype(jnp.bfloat16)
    second_share, third_share = (
        lax.psum_scatter(
            second_whole.astype(jnp.bfloat16), "sx", scatter_dimension=4, tiled=True
        ).astype(jnp.float32),
        lax.psum_scatter(
            jnp.swapaxes(third_whole, 3, 4).astype(jnp.bfloat16),
            "sx",
            scatter_dimension=4,
            tiled=True,
        ).astype(jnp.float32),
    )
    second_grad, third_grad = finish_grads(second_share, jnp.swapaxes(third_share, 3, 4))
    spread = (
        jnp.broadcast_to(
            pooled_grad.astype(jnp.float32)[:, None, :, None, :, None, :],
            (depth_cells // 2, 2, height_cells // 2, 2, width_cells // 2, 2, channels),
        ).reshape(depth_cells, height_cells, width_cells, channels)
        / 8.0
    )
    first_pre_grad = (spread * leaky_slope(first_pre)).astype(jnp.bfloat16)
    first_grad = lax.psum(kernel_grad(volume_pad, first_pre_grad), ("sx", "sy"))
    return (output, first_grad, second_grad, third_grad)


def solution(mesh):
    in_specs = (
        P("sx", "sy", None, None),
        P(),
        P(None, None, None, None, "sx"),
        P(None, None, None, "sx", None),
        P("sy", None, None, "sx"),
    )
    out_specs = (
        P("sy", None, None, "sx"),
        P(),
        P(None, None, None, None, "sx"),
        P(None, None, None, "sx", None),
    )
    return jax.shard_map(
        on_device, mesh=mesh, in_specs=in_specs, out_specs=out_specs, check_vma=False
    )
```

profile of v0, /device:TPU:1, one launch (start us, length us, event | category | flops | bytes accessed | tf_op | source)
XLA Modules:
  0.0 665.1 jit_solution(17984334955329709036)
XLA Ops:
  9.1 4.9 collective-permute-start
  17.7 7.2 %all-to-all-start.2 = ((bf16[4,32,128,8]{2,3,0,1:T(8,128)(2,1)}), bf16[4,32,128,8]{2,3,0,1:T(8,128)(2,1)S(1)}, u32[]{:S(2)}, u32[]{:S(2)}) async-start(bf16[4,32,128,8]{2,3,0,1:T(8,128)(2,1)} %copy.447), calls=%async_computation.2 | async-start | bytes 524288 | tf_op jit(solution)/shard_map/all_to_all | solution.py:95
  24.9 25.7 %all_gather.6 = bf16[3,3,3,128,128]{3,4,2,1,0:T(8,128)(2,1)} all-gather(bf16[3,3,3,128,8]{3,4,2,1,0:T(8,128)(2,1)S(1)} %copy-done.59), channel_id=1, replica_groups=mesh['sx'=16,'sy'=8] {'sx'}, dimensions={4}, use_global_device_ids=true | all-gather | bytes 940032 | tf_op jit(solution)/shard_map/all_gather | solution.py:125
  53.4 5.2 collective-permute-start.2
  59.9 27.5 %all_gather.7 = bf16[3,3,3,128,128]{3,4,2,1,0:T(8,128)(2,1)} all-gather(bf16[3,3,3,128,8]{3,4,2,1,0:T(8,128)(2,1)S(1)} %bitcast.1015), channel_id=1, replica_groups=mesh['sx'=16,'sy'=8] {'sx'}, dimensions={4}, use_global_device_ids=true | all-gather | bytes 940032 | tf_op jit(solution)/shard_map/all_gather | solution.py:126
  91.5 3.5 all-to-all-start.3
  95.0 3.0 fusion.446
  100.1 11.3 %reshape.347 = bf16[6,10,1,8,33,64]{4,3,5,1,0,2:T(8,128)(2,1)} reshape(bf16[6,10,1,264,64]{3,4,1,0,2:T(8,128)(2,1)} %pad.22) | data formatting | bytes 4055040 | tf_op jit(solution)/shard_map/conv_general_dilated | solution.py:31
  111.4 10.9 %copy.431 = bf16[6,10,1,8,33,64]{5,3,4,1,0,2:T(8,128)(2,1)} copy(bf16[6,10,1,8,33,64]{4,3,5,1,0,2:T(8,128)(2,1)} %reshape.347) | data formatting | bytes 4055040 | tf_op jit(solution)/shard_map/conv_general_dilated | solution.py:31
  123.4 11.6 %compare_select_fusion.1 = (f32[4,8,8,33,128]{4,2,3,1,0:T(8,128)}, f32[4,8,8,33,128]{4,2,3,1,0:T(8,128)S(1)}) fusion(bf16[3,3,3,64,128]{4,3,2,1,0:T(8,128)(2,1)S(1)} %copy-done, bf16[6,10,1,7,2,64]{5,3,4,1,0,2:T(8,128)(2,1)S(1)} %slice.477, bf16[6,10,1,8,33,64]{5,3,4,1,0,2:T(8,128)(2,1)} %copy.431, pred[8,33]{0,1:T(8,128)(4,1)S(1)} %copy-done.62), kind=kOutput, calls=%fused_computation.8 | convolution fusion | flops 3746820096 | bytes 11228424 | tf_op jit(solution)/shard_map/conv_general_dilated | solution.py:31
  136.0 3.9 fusion.11
  140.3 3.6 collective-permute-start.4
  145.8 3.6 collective-permute-start.12
  151.5 2.7 collective-permute-start.6
  155.6 4.2 fusion.17
  159.7 5.0 copy.460
  165.6 6.1 collective-permute-start.14
  174.3 2.8 fusion.445
  187.2 3.3 fusion.26
  198.4 3.9 collective-permute-start.8
  211.4 3.6 collective-permute-start.16
  220.8 6.4 collective-permute-start.10
  229.3 5.5 collective-permute-start.18
  239.8 3.6 collective-permute-done.19
  274.0 9.7 %all-to-all-start = ((bf16[2,4,128,128]{2,1,0,3:T(4,128)(2,1)}), bf16[2,4,128,128]{2,1,0,3:T(4,128)(2,1)}, u32[]{:S(2)}, u32[]{:S(2)}) async-start(bf16[2,4,128,128]{2,1,0,3:T(4,128)(2,1)} %copy.443), calls=%async_computation | async-start | bytes 524288 | tf_op jit(solution)/shard_map/all_to_all | solution.py:83
  295.4 2.9 fusion.100
  298.3 2.9 fusion.109
  307.6 111.4 %all-reduce.15.cloned.1.call-done = (bf16[3,3,3,128,128]{3,4,2,1,0:T(8,128)(2,1)}, bf16[3,3,3,128,128]{3,4,2,1,0:T(8,128)(2,1)}) async-done(((bf16[3,3,3,128,128]{3,4,2,1,0:T(8,128)(2,1)}, bf16[3,3,3,128,128]{3,4,2,1,0:T(8,128)(2,1)}), (bf16[3,3,3,128,128]{3,4,2,1,0:T(8,128)(2,1)}, bf16[3,3,3,128,128]{3,4,2,1,0:T(8,128)(2,1)})) %all-reduce.15.cloned.1.call-update) | async-done | bytes 1769488
  421.9 3.4 fusion.105
  426.4 13.6 %all_to_all.72 = bf16[32,4,128,8]{2,3,1,0:T(8,128)(2,1)S(1)} all-to-all(bf16[32,4,128,8]{2,3,1,0:T(8,128)(2,1)S(1)} %bitcast.1007), channel_id=1, replica_groups=mesh['sx'=16,'sy'=8] {'sy'}, dimensions={0} | all-to-all | bytes 524288 | tf_op jit(solution)/shard_map/all_to_all | solution.py:82
  440.7 60.3 %all-reduce.17.cloned.1.call-done = (bf16[3,3,3,128,8]{3,4,2,1,0:T(8,128)(2,1)}, bf16[3,3,3,8,128]{4,3,2,1,0:T(8,128)(2,1)}) async-done(((bf16[3,3,3,128,8]{3,4,2,1,0:T(8,128)(2,1)}, bf16[3,3,3,8,128]{4,3,2,1,0:T(8,128)(2,1)}), (bf16[3,3,3,128,8]{3,4,2,1,0:T(8,128)(2,1)}, bf16[3,3,3,8,128]{4,3,2,1,0:T(8,128)(2,1)})) %all-reduce.17.cloned.1.call-update) | async-done | bytes 110608 | tf_op jit(solution)/shard_map/psum | solution.py:109
  504.0 152.0 %all-reduce.13.cloned.1.call-done = f32[3,3,3,64,128]{4,3,2,1,0:T(8,128)} async-done(((f32[3,3,3,64,128]{4,3,2,1,0:T(8,128)}), f32[3,3,3,64,128]{4,3,2,1,0:T(8,128)}) %all-reduce.13.cloned.1.call-update) | async-done | bytes 884752 | tf_op jit(solution)/shard_map/psum | solution.py:160
  (325 shorter events, 123.3 us)
Async XLA Ops:
  7.2 116.2 %copy-start = (bf16[3,3,3,64,128]{4,3,2,1,0:T(8,128)(2,1)S(1)}, bf16[3,3,3,64,128]{4,3,2,1,0:T(8,128)(2,1)}, u32[]{:S(2)}) copy-start(bf16[3,3,3,64,128]{4,3,2,1,0:T(8,128)(2,1)} %param.6) | copy-start | bytes 1327108
  7.2 44.4 %copy-start.5 = (bf16[4,8,256,64]{2,3,1,0:T(8,128)(2,1)S(1)}, bf16[4,8,256,64]{2,3,1,0:T(8,128)(2,1)}, u32[]{:S(2)}) copy-start(bf16[4,8,256,64]{2,3,1,0:T(8,128)(2,1)} %param.5) | copy-start | bytes 3145732
  9.1 41.5 %collective-permute-start = (bf16[1,8,256,64]{2,3,1,0:T(8,128)(2,1)S(1)}, bf16[1,8,256,64]{2,3,1,0:T(8,128)(2,1)}, u32[]{:S(2)}, u32[]{:S(2)}) collective-permute-start(bf16[1,8,256,64]{2,3,1,0:T(8,128)(2,1)S(1)} %get-tuple-element.11), channel_id=1, source_target_pairs={{0,8},{8,16},{16,24},{24,32},{32,40},{40,48},{48,56},{56,64},{64,7... | collective-permute-start | bytes 786440 | tf_op jit(solution)/shard_map/ppermute | solution.py:21
  14.0 37.6 %collective-permute-start.1 = (bf16[1,8,256,64]{2,3,1,0:T(8,128)(2,1)}, bf16[1,8,256,64]{2,3,1,0:T(8,128)(2,1)}, u32[]{:S(2)}, u32[]{:S(2)}) collective-permute-start(bf16[1,8,256,64]{2,3,1,0:T(8,128)(2,1)} %get-tuple-element.10), channel_id=1, source_target_pairs={{8,0},{16,8},{24,16},{32,24},{40,32},{48,40},{56,48},{64,56},{72,6... | collective-permute-start | bytes 786440 | tf_op jit(solution)/shard_map/ppermute | solution.py:23
  17.7 73.1 %all-to-all-start.2 = ((bf16[4,32,128,8]{2,3,0,1:T(8,128)(2,1)}), bf16[4,32,128,8]{2,3,0,1:T(8,128)(2,1)S(1)}, u32[]{:S(2)}, u32[]{:S(2)}) async-start(bf16[4,32,128,8]{2,3,0,1:T(8,128)(2,1)} %copy.447), calls=%async_computation.2 | async-start | bytes 524288 | tf_op jit(solution)/shard_map/all_to_all | solution.py:95
  53.4 36.1 %copy-start.61 = (u32[128]{0:T(128)S(1)}, u32[128]{0:T(128)}, u32[]{:S(2)}) copy-start(u32[128]{0:T(128)} %constant.59) | copy-start | bytes 1540
  53.4 41.6 %collective-permute-start.2 = (bf16[6,1,256,64]{2,3,1,0:T(8,128)(2,1)}, bf16[6,1,256,64]{2,3,1,0:T(8,128)(2,1)}, u32[]{:S(2)}, u32[]{:S(2)}) collective-permute-start(bf16[6,1,256,64]{2,3,1,0:T(8,128)(2,1)} %get-tuple-element.8), channel_id=1, source_target_pairs={{0,1},{1,2},{2,3},{3,4},{4,5},{5,6},{6,7},{8,9},{9,10},{10,11},{11... | collective-permute-start | bytes 589832 | tf_op jit(solution)/shard_map/ppermute | solution.py:21
  58.6 36.4 %collective-permute-start.3 = (bf16[6,1,256,64]{2,3,1,0:T(8,128)(2,1)}, bf16[6,1,256,64]{2,3,1,0:T(8,128)(2,1)S(1)}, u32[]{:S(2)}, u32[]{:S(2)}) collective-permute-start(bf16[6,1,256,64]{2,3,1,0:T(8,128)(2,1)} %get-tuple-element.9), channel_id=1, source_target_pairs={{1,0},{2,1},{3,2},{4,3},{5,4},{6,5},{7,6},{9,8},{10,9},{11,10},{12... | collective-permute-start | bytes 589832 | tf_op jit(solution)/shard_map/ppermute | solution.py:23
  91.5 54.3 %all-to-all-start.3 = ((bf16[32,4,128,8]{2,3,1,0:T(8,128)(2,1)}), bf16[32,4,128,8]{2,3,1,0:T(8,128)(2,1)S(1)}, u32[]{:S(2)}, u32[]{:S(2)}) async-start(bf16[32,4,128,8]{2,3,1,0:T(8,128)(2,1)} %bitcast.24), calls=%async_computation.3 | async-start | bytes 524288 | tf_op jit(solution)/shard_map/all_to_all | solution.py:94
  140.3 11.2 %collective-permute-start.4 = (bf16[1,4,128,128]{2,3,1,0:T(8,128)(2,1)S(1)}, bf16[1,4,128,128]{2,3,1,0:T(8,128)(2,1)S(1)}, u32[]{:S(2)}, u32[]{:S(2)}) collective-permute-start(bf16[1,4,128,128]{2,3,1,0:T(8,128)(2,1)S(1)} %get-tuple-element.58), channel_id=1, source_target_pairs={{0,8},{8,16},{16,24},{24,32},{32,40},{40,48},{48,56},{56,64},{64,7... | collective-permute-start | bytes 393224 | tf_op jit(solution)/shard_map/ppermute | solution.py:21
  143.8 7.6 %collective-permute-start.5 = (bf16[1,4,128,128]{2,3,1,0:T(8,128)(2,1)S(1)}, bf16[1,4,128,128]{2,3,1,0:T(8,128)(2,1)S(1)}, u32[]{:S(2)}, u32[]{:S(2)}) collective-permute-start(bf16[1,4,128,128]{2,3,1,0:T(8,128)(2,1)S(1)} %get-tuple-element.59), channel_id=1, source_target_pairs={{8,0},{16,8},{24,16},{32,24},{40,32},{48,40},{56,48},{64,56},{72,6... | collective-permute-start | bytes 393224 | tf_op jit(solution)/shard_map/ppermute | solution.py:23
  145.8 18.9 %collective-permute-start.12 = (bf16[1,4,128,128]{2,3,1,0:T(8,128)(2,1)S(1)}, bf16[1,4,128,128]{2,3,1,0:T(8,128)(2,1)S(1)}, u32[]{:S(2)}, u32[]{:S(2)}) collective-permute-start(bf16[1,4,128,128]{2,3,1,0:T(8,128)(2,1)S(1)} %get-tuple-element.52), channel_id=1, source_target_pairs={{0,8},{8,16},{16,24},{24,32},{32,40},{40,48},{48,56},{56,64},{64,7... | collective-permute-start | bytes 393224 | tf_op jit(solution)/shard_map/ppermute | solution.py:21
  149.5 15.3 %collective-permute-start.13 = (bf16[1,4,128,128]{2,3,1,0:T(8,128)(2,1)S(1)}, bf16[1,4,128,128]{2,3,1,0:T(8,128)(2,1)S(1)}, u32[]{:S(2)}, u32[]{:S(2)}) collective-permute-start(bf16[1,4,128,128]{2,3,1,0:T(8,128)(2,1)S(1)} %get-tuple-element.53), channel_id=1, source_target_pairs={{8,0},{16,8},{24,16},{32,24},{40,32},{48,40},{56,48},{64,56},{72,6... | collective-permute-start | bytes 393224 | tf_op jit(solution)/shard_map/ppermute | solution.py:23
  151.5 21.5 %collective-permute-start.6 = (bf16[4,1,128,128]{2,3,1,0:T(8,128)(2,1)S(1)}, bf16[4,1,128,128]{2,3,1,0:T(8,128)(2,1)S(1)}, u32[]{:S(2)}, u32[]{:S(2)}) collective-permute-start(bf16[4,1,128,128]{2,3,1,0:T(8,128)(2,1)S(1)} %get-tuple-element.46), channel_id=1, source_target_pairs={{0,1},{1,2},{2,3},{3,4},{4,5},{5,6},{6,7},{8,9},{9,10},{10,11},{11... | collective-permute-start | bytes 393224 | tf_op jit(solution)/shard_map/ppermute | solution.py:21
  154.3 18.8 %collective-permute-start.7 = (bf16[4,1,128,128]{2,3,1,0:T(8,128)(2,1)S(1)}, bf16[4,1,128,128]{2,3,1,0:T(8,128)(2,1)S(1)}, u32[]{:S(2)}, u32[]{:S(2)}) collective-permute-start(bf16[4,1,128,128]{2,3,1,0:T(8,128)(2,1)S(1)} %get-tuple-element.47), channel_id=1, source_target_pairs={{1,0},{2,1},{3,2},{4,3},{5,4},{6,5},{7,6},{9,8},{10,9},{11,10},{12... | collective-permute-start | bytes 393224 | tf_op jit(solution)/shard_map/ppermute | solution.py:23
  165.6 21.6 %collective-permute-start.14 = (bf16[4,1,128,128]{2,3,1,0:T(8,128)(2,1)}, bf16[4,1,128,128]{2,3,1,0:T(8,128)(2,1)}, u32[]{:S(2)}, u32[]{:S(2)}) collective-permute-start(bf16[4,1,128,128]{2,3,1,0:T(8,128)(2,1)} %get-tuple-element.42), channel_id=1, source_target_pairs={{0,1},{1,2},{2,3},{3,4},{4,5},{5,6},{6,7},{8,9},{9,10},{10,11},{11... | collective-permute-start | bytes 393224 | tf_op jit(solution)/shard_map/ppermute | solution.py:21
  171.7 15.5 %collective-permute-start.15 = (bf16[4,1,128,128]{2,3,1,0:T(8,128)(2,1)}, bf16[4,1,128,128]{2,3,1,0:T(8,128)(2,1)}, u32[]{:S(2)}, u32[]{:S(2)}) collective-permute-start(bf16[4,1,128,128]{2,3,1,0:T(8,128)(2,1)} %get-tuple-element.43), channel_id=1, source_target_pairs={{1,0},{2,1},{3,2},{4,3},{5,4},{6,5},{7,6},{9,8},{10,9},{11,10},{12... | collective-permute-start | bytes 393224 | tf_op jit(solution)/shard_map/ppermute | solution.py:23
  198.4 22.4 %collective-permute-start.8 = (bf16[1,4,128,128]{3,2,1,0:T(8,128)(2,1)}, bf16[1,4,128,128]{3,2,1,0:T(8,128)(2,1)S(1)}, u32[]{:S(2)}, u32[]{:S(2)}) collective-permute-start(bf16[1,4,128,128]{3,2,1,0:T(8,128)(2,1)} %get-tuple-element.56), channel_id=1, source_target_pairs={{0,8},{8,16},{16,24},{24,32},{32,40},{40,48},{48,56},{56,64},{64,7... | collective-permute-start | bytes 393224 | tf_op jit(solution)/shard_map/ppermute | solution.py:21
  202.2 18.5 %collective-permute-start.9 = (bf16[1,4,128,128]{3,2,1,0:T(8,128)(2,1)}, bf16[1,4,128,128]{3,2,1,0:T(8,128)(2,1)S(1)}, u32[]{:S(2)}, u32[]{:S(2)}) collective-permute-start(bf16[1,4,128,128]{3,2,1,0:T(8,128)(2,1)} %get-tuple-element.57), channel_id=1, source_target_pairs={{8,0},{16,8},{24,16},{32,24},{40,32},{48,40},{56,48},{64,56},{72,6... | collective-permute-start | bytes 393224 | tf_op jit(solution)/shard_map/ppermute | solution.py:23
  211.4 17.1 %collective-permute-start.16 = (bf16[1,4,128,128]{3,2,1,0:T(8,128)(2,1)}, bf16[1,4,128,128]{3,2,1,0:T(8,128)(2,1)S(1)}, u32[]{:S(2)}, u32[]{:S(2)}) collective-permute-start(bf16[1,4,128,128]{3,2,1,0:T(8,128)(2,1)} %get-tuple-element.50), channel_id=1, source_target_pairs={{0,8},{8,16},{16,24},{24,32},{32,40},{40,48},{48,56},{56,64},{64,7... | collective-permute-start | bytes 393224 | tf_op jit(solution)/shard_map/ppermute | solution.py:21
  215.1 13.4 %collective-permute-start.17 = (bf16[1,4,128,128]{3,2,1,0:T(8,128)(2,1)}, bf16[1,4,128,128]{3,2,1,0:T(8,128)(2,1)}, u32[]{:S(2)}, u32[]{:S(2)}) collective-permute-start(bf16[1,4,128,128]{3,2,1,0:T(8,128)(2,1)} %get-tuple-element.51), channel_id=1, source_target_pairs={{8,0},{16,8},{24,16},{32,24},{40,32},{48,40},{56,48},{64,56},{72,6... | collective-permute-start | bytes 393224 | tf_op jit(solution)/shard_map/ppermute | solution.py:23
  220.8 16.3 %collective-permute-start.10 = (bf16[4,1,128,128]{3,2,1,0:T(8,128)(2,1)S(1)}, bf16[4,1,128,128]{3,2,1,0:T(8,128)(2,1)S(1)}, u32[]{:S(2)}, u32[]{:S(2)}) collective-permute-start(bf16[4,1,128,128]{3,2,1,0:T(8,128)(2,1)S(1)} %get-tuple-element.44), channel_id=1, source_target_pairs={{0,1},{1,2},{2,3},{3,4},{4,5},{5,6},{6,7},{8,9},{9,10},{10,11},{11... | collective-permute-start | bytes 393224 | tf_op jit(solution)/shard_map/ppermute | solution.py:21
  227.2 9.9 %collective-permute-start.11 = (bf16[4,1,128,128]{3,2,1,0:T(8,128)(2,1)S(1)}, bf16[4,1,128,128]{3,2,1,0:T(8,128)(2,1)S(1)}, u32[]{:S(2)}, u32[]{:S(2)}) collective-permute-start(bf16[4,1,128,128]{3,2,1,0:T(8,128)(2,1)S(1)} %get-tuple-element.45), channel_id=1, source_target_pairs={{1,0},{2,1},{3,2},{4,3},{5,4},{6,5},{7,6},{9,8},{10,9},{11,10},{12... | collective-permute-start | bytes 393224 | tf_op jit(solution)/shard_map/ppermute | solution.py:23
  229.3 10.5 %collective-permute-start.18 = (bf16[4,1,128,128]{3,2,1,0:T(8,128)(2,1)S(1)}, bf16[4,1,128,128]{3,2,1,0:T(8,128)(2,1)S(1)}, u32[]{:S(2)}, u32[]{:S(2)}) collective-permute-start(bf16[4,1,128,128]{3,2,1,0:T(8,128)(2,1)S(1)} %get-tuple-element.38), channel_id=1, source_target_pairs={{0,1},{1,2},{2,3},{3,4},{4,5},{5,6},{6,7},{8,9},{9,10},{10,11},{11... | collective-permute-start | bytes 393224 | tf_op jit(solution)/shard_map/ppermute | solution.py:21
  234.8 8.6 %collective-permute-start.19 = (bf16[4,1,128,128]{3,2,1,0:T(8,128)(2,1)S(1)}, bf16[4,1,128,128]{3,2,1,0:T(8,128)(2,1)S(1)}, u32[]{:S(2)}, u32[]{:S(2)}) collective-permute-start(bf16[4,1,128,128]{3,2,1,0:T(8,128)(2,1)S(1)} %get-tuple-element.39), channel_id=1, source_target_pairs={{1,0},{2,1},{3,2},{4,3},{5,4},{6,5},{7,6},{9,8},{10,9},{11,10},{12... | collective-permute-start | bytes 393224 | tf_op jit(solution)/shard_map/ppermute | solution.py:23
  237.1 30.2 %copy-start.11 = (bf16[4,1,128,128]{3,2,1,0:T(8,128)(2,1)}, bf16[4,1,128,128]{3,2,1,0:T(8,128)(2,1)S(1)}, u32[]{:S(2)}) copy-start(bf16[4,1,128,128]{3,2,1,0:T(8,128)(2,1)S(1)} %collective-permute-done.10) | copy-start | bytes 393220
  237.1 30.2 %copy-start.12 = (bf16[4,1,128,128]{3,2,1,0:T(8,128)(2,1)}, bf16[4,1,128,128]{3,2,1,0:T(8,128)(2,1)S(1)}, u32[]{:S(2)}) copy-start(bf16[4,1,128,128]{3,2,1,0:T(8,128)(2,1)S(1)} %collective-permute-done.11) | copy-start | bytes 393220
  274.0 151.3 %all-to-all-start = ((bf16[2,4,128,128]{2,1,0,3:T(4,128)(2,1)}), bf16[2,4,128,128]{2,1,0,3:T(4,128)(2,1)}, u32[]{:S(2)}, u32[]{:S(2)}) async-start(bf16[2,4,128,128]{2,1,0,3:T(4,128)(2,1)} %copy.443), calls=%async_computation | async-start | bytes 524288 | tf_op jit(solution)/shard_map/all_to_all | solution.py:83
  283.8 135.2 %all-reduce.15.cloned.1.call-start = ((), (), s32[]{:S(2)}) async-start(), calls=%async_computation.5 | async-start | bytes 3538944
  295.4 205.7 %all-reduce.17.cloned.1.call-start = ((), (), s32[]{:S(2)}) async-start(), calls=%async_computation.6 | async-start | bytes 221184 | tf_op jit(solution)/shard_map/psum | solution.py:109
  421.9 234.1 %all-reduce.13.cloned.1.call-start = ((), (), s32[]{:S(2)}) async-start(), calls=%async_computation.4 | async-start | bytes 1769472 | tf_op jit(solution)/shard_map/psum | solution.py:160
  425.3 232.9 %copy-start.1 = (bf16[3,3,3,64,128]{4,3,2,1,0:T(8,128)(2,1)S(1)}, bf16[3,3,3,64,128]{4,3,2,1,0:T(8,128)(2,1)}, u32[]{:S(2)}) copy-start(bf16[3,3,3,64,128]{4,3,2,1,0:T(8,128)(2,1)} %param.6) | copy-start | bytes 1327108
  (60 other events, 266.4 us)
Sparse Core Ops, SparseCore 0:
  295.5 123.4 all-reduce.14
  422.3 78.7 all-reduce.16
  506.4 149.5 all-reduce.12
where the time goes:
time: 675 us; the launch traced here: 665 us
  waiting for transfers between devices  327 us (48%)
  starting transfers between devices  82.6 us (12%)
  local copies, waits for them, and re-layouts  79.5 us (12%)
  blocking collectives  66.8 us (10%)
  matrix products  63.8 us (9%)
  other arithmetic  28.4 us (4%)
  between operations  16.6 us (2%)
    psum x1, waiting for transfers between devices, on_device(): first_grad = lax.psum(kernel_grad(volume_pad, first_pre_grad), ('sx', 'sy'))  152 us
    unnamed x4, waiting for transfers between devices  111 us
    psum x1, waiting for transfers between devices, finish_grads(): lax.psum(second_grad.astype(jnp.bfloat16), 'sy').astype(jnp.float32)  60.3 us
    ppermute x10, starting transfers between devices, padded_2(): lax.ppermute(tail, axis, [(i, (i + 1) % count) for i in range(ends)])  45.6 us
    dot_general x81, matrix products, kernel_grad(): lax.dot_general(window, flat_cot, (((0,), (0,)), ((), ())), preferred_ele...  43.7 us
    all_gather x1, blocking collectives, on_device(): lax.all_gather(jnp.swapaxes(third_kernel, 3, 4), 'sx', axis=4, tiled=True)  27.5 us
    conv_general_dilated x17, local copies, waits for them, and re-layouts, conv_valid(): lax.conv_general_dilated(padded[None], kernel, (1, 1, 1), 'VALID', dimens...  25.9 us
    unnamed x143, local copies, waits for them, and re-layouts  25.9 us
  transfers between devices with their start and end apart: 26, of which 4 were waited for; matrix products, arithmetic and copies ran while one was open for 18% of the time, Pallas kernels for 0%

commit v1 on v0

--- a/solution.py
+++ b/solution.py
@@ -4,10 +4,6 @@
 from jax.sharding import PartitionSpec as P
 
 leak_slope = 0.2
-
-
-def as_sent(shard):
-    return jax.tree.map(lambda a: a.astype(jnp.bfloat16) if a.dtype == jnp.float32 else a, shard)
 
 
 def padded_2(cells, sides, width):
@@ -76,39 +72,47 @@
     return jnp.pad(values, ((0, 0), (0, 0), (1, 1), (0, 0)))
 
 
+def swap_places(ways):
+    return [
+        (a * 8 + b, (2 * b + a % 2) * 8 + a // 2)
+        if ways > 0
+        else ((2 * b + a % 2) * 8 + a // 2, a * 8 + b)
+        for a in range(16)
+        for b in range(8)
+    ]
+
+
 def to_channels(values):
-    return jax.tree.map(
-        lambda part, own: part.astype(own.dtype),
-        lax.all_to_all(
-            lax.all_to_all(as_sent(values), "sx", split_axis=3, concat_axis=0, tiled=True),
-            "sy",
-            split_axis=0,
-            concat_axis=1,
-            tiled=True,
-        ),
-        values,
-    )
+    moved = lax.ppermute(jnp.swapaxes(values, 2, 3), ("sx", "sy"), swap_places(1))
+    parts = jnp.swapaxes(moved.reshape(8, 16, 8, 128), 0, 1)
+    parts = lax.all_to_all(parts, "sx", 0, 0, tiled=True)
+    parts = parts.reshape(8, 2, 2, 4, 8, 128).transpose(1, 2, 0, 3, 4, 5)
+    return jnp.swapaxes(parts.reshape(4, 32, 8, 128), 2, 3)
 
 
 def to_space(values):
-    return lax.all_to_all(
-        lax.all_to_all(values, "sy", split_axis=1, concat_axis=0, tiled=True),
-        "sx",
-        split_axis=0,
-        concat_axis=3,
-        tiled=True,
+    parts = jnp.swapaxes(values, 2, 3).reshape(2, 2, 8, 4, 8, 128)
+    parts = parts.transpose(2, 0, 1, 3, 4, 5).reshape(16, 8, 8, 128)
+    parts = lax.all_to_all(parts, "sx", 0, 0, tiled=True)
+    cells = jnp.swapaxes(parts, 0, 1).reshape(2, 4, 128, 128)
+    return jnp.swapaxes(lax.ppermute(cells, ("sx", "sy"), swap_places(-1)), 2, 3)
+
+
+def sum_parts(parts, axis):
+    got = lax.all_to_all(parts.astype(jnp.bfloat16), axis, 0, 0, tiled=True)
+    return got.astype(jnp.float32).sum(0)
+
+
+def spread_part(part, axis, count):
+    part = part.astype(jnp.bfloat16)
+    got = lax.all_to_all(
+        jnp.broadcast_to(part[None], (count,) + part.shape), axis, 0, 0, tiled=True
     )
+    return got.reshape((-1,) + part.shape[1:])
 
 
 def mid_faces(values):
     return pad_width(padded_2(values, (("sx", 0), ("sy", 1)), 1))
-
-
-def finish_grads(second_grad, third_grad):
-    return (
-        lax.psum(second_grad.astype(jnp.bfloat16), "sy").astype(jnp.float32),
-        lax.psum(third_grad.astype(jnp.bfloat16), "sy").astype(jnp.float32),
-    )
 
 
 def on_device(volume, first_kernel, second_kernel, third_kernel, cotangent):
@@ -121,11 +125,16 @@
         .mean(axis=(1, 3, 5))
         .astype(jnp.bfloat16)
     )
-    second_full, third_turned = (
-        lax.all_gather(second_kernel, "sx", axis=4, tiled=True),
-        lax.all_gather(jnp.swapaxes(third_kernel, 3, 4), "sx", axis=4, tiled=True),
+    shares = jnp.concatenate(
+        [
+            jnp.swapaxes(second_kernel, 3, 4).reshape(216, 128),
+            third_kernel.reshape(216, 128),
+        ]
     )
-    third_full = jnp.swapaxes(third_turned, 3, 4)
+    filters = lax.all_gather(shares, "sx", axis=0, tiled=True).reshape(16, 2, 27, 8, 128)
+    filters = filters.transpose(1, 2, 0, 3, 4).reshape(2, 3, 3, 3, 128, 128)
+    second_full = jnp.swapaxes(filters[0], 3, 4)
+    third_full = filters[1]
     pooled_pad = mid_faces(pooled)
     second_pre = conv_valid(pooled_pad, second_full)
     hidden = leaky_relu(second_pre).astype(jnp.bfloat16)
@@ -137,18 +146,12 @@
     second_pre_grad = (hidden_grad * leaky_slope(second_pre)).astype(jnp.bfloat16)
     second_whole = kernel_grad(pooled_pad, second_pre_grad)
     pooled_grad = conv_valid(mid_faces(second_pre_grad), flipped(second_full)).astype(jnp.bfloat16)
-    second_share, third_share = (
-        lax.psum_scatter(
-            second_whole.astype(jnp.bfloat16), "sx", scatter_dimension=4, tiled=True
-        ).astype(jnp.float32),
-        lax.psum_scatter(
-            jnp.swapaxes(third_whole, 3, 4).astype(jnp.bfloat16),
-            "sx",
-            scatter_dimension=4,
-            tiled=True,
-        ).astype(jnp.float32),
-    )
-    second_grad, third_grad = finish_grads(second_share, jnp.swapaxes(third_share, 3, 4))
+    grads = jnp.stack([jnp.swapaxes(second_whole, 3, 4), third_whole]).astype(jnp.bfloat16)
+    grads = grads.reshape(54, 16, 8, 128).swapaxes(0, 1).reshape(16, 432, 128)
+    share = sum_parts(grads, "sx")
+    share = sum_parts(jnp.pad(share, ((0, 80), (0, 0))).reshape(8, 64, 128), "sy")
+    share = spread_part(share, "sy", 8)[:432].astype(jnp.float32).reshape(2, 3, 3, 3, 8, 128)
+    second_grad, third_grad = jnp.swapaxes(share[0], 3, 4), share[1]
     spread = (
         jnp.broadcast_to(
             pooled_grad.astype(jnp.float32)[:, None, :, None, :, None, :],
@@ -157,7 +160,10 @@
         / 8.0
     )
     first_pre_grad = (spread * leaky_slope(first_pre)).astype(jnp.bfloat16)
-    first_grad = lax.psum(kernel_grad(volume_pad, first_pre_grad), ("sx", "sy"))
+    first_part = kernel_grad(volume_pad, first_pre_grad).reshape(1728, 128)
+    first_part = jnp.pad(first_part, ((0, 320), (0, 0))).reshape(128, 16, 128)
+    first_sum = spread_part(sum_parts(first_part, ("sx", "sy")), ("sx", "sy"), 128)
+    first_grad = first_sum[:1728].astype(jnp.float32).reshape(3, 3, 3, 64, 128)
     return (output, first_grad, second_grad, third_grad)
 
 

time: 675 us -> 389 us (0.58)
  waiting for transfers between devices: 327 us -> 61.7 us
  blocking collectives: 66.8 us -> 0 us
  starting transfers between devices: 82.6 us -> 123 us
  matrix products: 63.8 us -> 84.6 us
  local copies, waits for them, and re-layouts: 79.5 us -> 70.1 us
    psum x2 -> x0, waiting for transfers between devices: 212 us -> none  [the longest x1 152 us: on_device(): first_grad = lax.psum(kernel_grad(volume_pad, first_pre_grad), ('sx', 'sy'))]
    unnamed x4 -> x1, waiting for transfers between devices: 111 us -> 0.02 us
    all_to_all x3 -> x7, waiting for transfers between devices: 0.01 us -> 57.3 us  [the longest x3 34.2 us: sum_parts(): got = lax.all_to_all(parts.astype(jnp.bfloat16), axis, 0, 0, tiled=True)]
    all_gather x2 -> x0, blocking collectives: 53.2 us -> none  [the longest x1 27.5 us: on_device(): lax.all_gather(jnp.swapaxes(third_kernel, 3, 4), 'sx', axis=4, tiled=True)]
    all_to_all x3 -> x7, starting transfers between devices: 20.4 us -> 53.1 us  [the longest x1 23.4 us: to_channels(): parts = lax.all_to_all(parts, 'sx', 0, 0, tiled=True)]
    dot_general x81, matrix products: 43.7 us -> 64.4 us  [kernel_grad(): lax.dot_general(window, flat_cot, (((0,), (0,)), ((), ())), preferred_ele...]
    all_to_all x1 -> x0, blocking collectives: 13.6 us -> none  [to_channels(): lax.all_to_all(lax.all_to_all(as_sent(values), 'sx', split_axis=3, concat...]
    unnamed x143 -> x81, local copies, waits for them, and re-layouts: 25.9 us -> 21.3 us
  transfers between devices with their start and end apart: 26 -> 30, of which waited for: 4 -> 8; matrix products, arithmetic and copies ran while one was open for 18% -> 30% of each run, Pallas kernels for 0% -> 0%
where the time goes in v1:
time: 389 us; the launch traced here: 382 us
  starting transfers between devices  123 us (32%)
  matrix products  84.6 us (22%)
  local copies, waits for them, and re-layouts  70.1 us (18%)
  waiting for transfers between devices  61.7 us (16%)
  other arithmetic  26.9 us (7%)
  between operations  15.7 us (4%)
    dot_general x81, matrix products, kernel_grad(): lax.dot_general(window, flat_cot, (((0,), (0,)), ((), ())), preferred_ele...  64.4 us
    ppermute x10, starting transfers between devices, padded_2(): lax.ppermute(tail, axis, [(i, (i + 1) % count) for i in range(ends)])  48.7 us
    all_to_all x3, waiting for transfers between devices, sum_parts(): got = lax.all_to_all(parts.astype(jnp.bfloat16), axis, 0, 0, tiled=True)  34.2 us
    conv_general_dilated x17, local copies, waits for them, and re-layouts, conv_valid(): lax.conv_general_dilated(padded[None], kernel, (1, 1, 1), 'VALID', dimens...  24.2 us
    all_to_all x1, starting transfers between devices, to_channels(): parts = lax.all_to_all(parts, 'sx', 0, 0, tiled=True)  23.4 us
    unnamed x81, local copies, waits for them, and re-layouts  21.3 us
    conv_general_dilated x5, matrix products, conv_valid(): lax.conv_general_dilated(padded[None], kernel, (1, 1, 1), 'VALID', dimens...  20.2 us
    all_to_all x2, waiting for transfers between devices, spread_part(): lax.all_to_all(jnp.broadcast_to(part[None], (count,) + part.shape), axis,...  19.1 us
  transfers between devices with their start and end apart: 30, of which 8 were waited for; matrix products, arithmetic and copies ran while one was open for 30% of the time, Pallas kernels for 0%

profile of v1, /device:TPU:1, one launch (start us, length us, event | category | flops | bytes accessed | tf_op | source)
XLA Modules:
  0.0 382.2 jit_solution(5229171208098223853)
XLA Ops:
  9.1 4.9 %collective-permute-start = (bf16[1,8,256,64]{2,3,1,0:T(8,128)(2,1)S(1)}, bf16[1,8,256,64]{2,3,1,0:T(8,128)(2,1)}, u32[]{:S(2)}, u32[]{:S(2)}) collective-permute-start(bf16[1,8,256,64]{2,3,1,0:T(8,128)(2,1)S(1)} %get-tuple-element.9), channel_id=1, source_target_pairs={{0,8},{8,16},{16,24},{24,32},{32,40},{40,48},{48,56},{56,64},{64,7... | collective-permute-start | bytes 786440 | tf_op jit(solution)/shard_map/ppermute | solution.py:17
  17.6 5.9 %all-to-all-start.1 = ((bf16[16,8,8,128]{3,2,1,0:T(8,128)(2,1)}), bf16[16,8,8,128]{3,2,1,0:T(8,128)(2,1)S(1)}, u32[]{:S(2)}, u32[]{:S(2)}) async-start(bf16[16,8,8,128]{3,2,1,0:T(8,128)(2,1)} %bitcast.32), calls=%async_computation.1 | async-start | bytes 524288 | tf_op jit(solution)/shard_map/all_to_all | solution.py:96
  26.6 5.9 %collective-permute-start.2 = (bf16[6,1,256,64]{2,3,1,0:T(8,128)(2,1)}, bf16[6,1,256,64]{2,3,1,0:T(8,128)(2,1)}, u32[]{:S(2)}, u32[]{:S(2)}) collective-permute-start(bf16[6,1,256,64]{2,3,1,0:T(8,128)(2,1)} %get-tuple-element.6), channel_id=1, source_target_pairs={{0,1},{1,2},{2,3},{3,4},{4,5},{5,6},{6,7},{8,9},{9,10},{10,11},{11... | collective-permute-start | bytes 589832 | tf_op jit(solution)/shard_map/ppermute | solution.py:17
  37.5 3.6 collective-permute-start.13
  46.3 8.5 %reshape.344 = bf16[6,10,1,8,33,64]{4,3,5,1,0,2:T(8,128)(2,1)} reshape(bf16[6,10,1,264,64]{3,4,1,0,2:T(8,128)(2,1)S(1)} %pad.34) | data formatting | bytes 4055040 | tf_op jit(solution)/shard_map/conv_general_dilated | solution.py:27
  54.8 11.1 %copy.186 = bf16[6,10,1,8,33,64]{5,3,4,1,0,2:T(8,128)(2,1)} copy(bf16[6,10,1,8,33,64]{4,3,5,1,0,2:T(8,128)(2,1)} %reshape.344) | data formatting | bytes 4055040 | tf_op jit(solution)/shard_map/conv_general_dilated | solution.py:27
  67.0 10.3 %compare_select_fusion.1 = (f32[4,8,8,33,128]{4,2,3,1,0:T(8,128)S(1)}, f32[4,8,8,33,128]{4,2,3,1,0:T(8,128)S(1)}) fusion(bf16[3,3,3,64,128]{4,3,2,1,0:T(8,128)(2,1)S(1)} %copy-done, bf16[6,10,1,7,2,64]{5,3,4,1,0,2:T(8,128)(2,1)S(1)} %slice.497, bf16[6,10,1,8,33,64]{5,3,4,1,0,2:T(8,128)(2,1)} %copy.186, pred[8,33]{0,1:T(8,128)(4,1)S(1)} %copy-done.32), kind=kOutput, calls=%fused_computation.8 | convolution fusion | flops 3746820096 | bytes 11228424 | tf_op jit(solution)/shard_map/conv_general_dilated | solution.py:27
  78.4 4.4 %fusion.11 = f32[2,4,128,128]{3,1,2,0:T(4,128)S(1)} fusion(f32[2,2,4,2,128,2,128]{6,3,2,5,4,1,0:T(2,128)S(1)} %bitcast.1343), kind=kLoop, calls=%fused_computation.18 | loop fusion | flops 4063232 | bytes 4718592 | tf_op jit(solution)/shard_map/reduce_sum | solution.py:125
  82.9 3.9 %collective-permute-start.4 = (bf16[1,4,128,128]{3,2,1,0:T(8,128)(2,1)S(1)}, bf16[1,4,128,128]{3,2,1,0:T(8,128)(2,1)S(1)}, u32[]{:S(2)}, u32[]{:S(2)}) collective-permute-start(bf16[1,4,128,128]{3,2,1,0:T(8,128)(2,1)S(1)} %get-tuple-element.28), channel_id=1, source_target_pairs={{0,8},{8,16},{16,24},{24,32},{32,40},{40,48},{48,56},{56,64},{64,7... | collective-permute-start | bytes 393224 | tf_op jit(solution)/shard_map/ppermute | solution.py:17
  89.7 3.6 collective-permute-start.14
  95.4 4.7 %collective-permute-start.6 = (bf16[4,1,128,128]{3,2,1,0:T(8,128)(2,1)S(1)}, bf16[4,1,128,128]{3,2,1,0:T(8,128)(2,1)S(1)}, u32[]{:S(2)}, u32[]{:S(2)}) collective-permute-start(bf16[4,1,128,128]{3,2,1,0:T(8,128)(2,1)S(1)} %get-tuple-element.20), channel_id=1, source_target_pairs={{0,1},{1,2},{2,3},{3,4},{4,5},{5,6},{6,7},{8,9},{9,10},{10,11},{11... | collective-permute-start | bytes 393224 | tf_op jit(solution)/shard_map/ppermute | solution.py:17
  101.4 4.1 %fusion.17 = bf16[6,10,258,64]{2,3,1,0:T(8,128)(2,1)} fusion(bf16[6,1,256,64]{2,3,1,0:T(8,128)(2,1)S(1)} %copy-done.22, bf16[6,8,256,64]{2,3,1,0:T(8,128)(2,1)S(1)} %copy-done.3, bf16[6,1,256,64]{2,3,1,0:T(8,128)(2,1)} %collective-permute-done.2), kind=kLoop, calls=%fused_computation.24 | loop fusion | flops 11888640 | bytes 3947520 | tf_op jit(solution)/shard_map/concatenate | solution.py:15
  109.3 5.5 %collective-permute-start.16 = (bf16[4,1,128,128]{3,2,1,0:T(8,128)(2,1)S(1)}, bf16[4,1,128,128]{3,2,1,0:T(8,128)(2,1)S(1)}, u32[]{:S(2)}, u32[]{:S(2)}) collective-permute-start(bf16[4,1,128,128]{3,2,1,0:T(8,128)(2,1)S(1)} %get-tuple-element.16), channel_id=1, source_target_pairs={{0,1},{1,2},{2,3},{3,4},{4,5},{5,6},{6,7},{8,9},{9,10},{10,11},{11... | collective-permute-start | bytes 393224 | tf_op jit(solution)/shard_map/ppermute | solution.py:17
  133.1 3.6 convolution_select_fusion.1
  146.2 4.3 %collective-permute-start.8 = (bf16[1,4,128,128]{2,3,1,0:T(8,128)(2,1)S(1)}, bf16[1,4,128,128]{2,3,1,0:T(8,128)(2,1)S(1)}, u32[]{:S(2)}, u32[]{:S(2)}) collective-permute-start(bf16[1,4,128,128]{2,3,1,0:T(8,128)(2,1)S(1)} %get-tuple-element.26), channel_id=1, source_target_pairs={{0,8},{8,16},{16,24},{24,32},{32,40},{40,48},{48,56},{56,64},{64,7... | collective-permute-start | bytes 393224 | tf_op jit(solution)/shard_map/ppermute | solution.py:17
  152.5 3.6 collective-permute-start.18
  158.4 6.6 %collective-permute-start.10 = (bf16[4,1,128,128]{2,3,1,0:T(8,128)(2,1)S(1)}, bf16[4,1,128,128]{2,3,1,0:T(8,128)(2,1)S(1)}, u32[]{:S(2)}, u32[]{:S(2)}) collective-permute-start(bf16[4,1,128,128]{2,3,1,0:T(8,128)(2,1)S(1)} %get-tuple-element.18), channel_id=1, source_target_pairs={{0,1},{1,2},{2,3},{3,4},{4,5},{5,6},{6,7},{8,9},{9,10},{10,11},{11... | collective-permute-start | bytes 393224 | tf_op jit(solution)/shard_map/ppermute | solution.py:17
  166.6 5.5 %collective-permute-start.20 = (bf16[4,1,128,128]{2,3,1,0:T(8,128)(2,1)S(1)}, bf16[4,1,128,128]{2,3,1,0:T(8,128)(2,1)S(1)}, u32[]{:S(2)}, u32[]{:S(2)}) collective-permute-start(bf16[4,1,128,128]{2,3,1,0:T(8,128)(2,1)S(1)} %get-tuple-element.12), channel_id=1, source_target_pairs={{0,1},{1,2},{2,3},{3,4},{4,5},{5,6},{6,7},{8,9},{9,10},{10,11},{11... | collective-permute-start | bytes 393224 | tf_op jit(solution)/shard_map/ppermute | solution.py:17
  240.1 3.4 copy.330
  252.8 23.4 %all-to-all-start = ((bf16[16,8,8,128]{3,2,1,0:T(8,128)(2,1)}), bf16[16,8,8,128]{3,2,1,0:T(8,128)(2,1)S(1)}, u32[]{:S(2)}, u32[]{:S(2)}) async-start(bf16[16,8,8,128]{3,2,1,0:T(8,128)(2,1)} %copy.201), calls=%async_computation | async-start | bytes 524288 | tf_op jit(solution)/shard_map/all_to_all | solution.py:88
  276.2 3.4 fusion.276
  279.6 4.0 %all-to-all-done = bf16[16,8,8,128]{3,2,1,0:T(8,128)(2,1)S(1)} async-done(((bf16[16,8,8,128]{3,2,1,0:T(8,128)(2,1)}), bf16[16,8,8,128]{3,2,1,0:T(8,128)(2,1)S(1)}, u32[]{:S(2)}, u32[]{:S(2)}) %all-to-all-start) | async-done | bytes 262176 | tf_op jit(solution)/shard_map/all_to_all | solution.py:88
  283.6 4.6 %all-to-all-start.4 = ((bf16[16,432,128]{2,1,0:T(8,128)(2,1)}), bf16[16,432,128]{2,1,0:T(8,128)(2,1)}, u32[]{:S(2)}, u32[]{:S(2)}) async-start(bf16[16,432,128]{2,1,0:T(8,128)(2,1)} %bitcast.1344), calls=%async_computation.4 | async-start | bytes 3538944 | tf_op jit(solution)/shard_map/all_to_all | solution.py:102
  295.8 16.0 %all-to-all-done.4 = bf16[16,432,128]{2,1,0:T(8,128)(2,1)} async-done(((bf16[16,432,128]{2,1,0:T(8,128)(2,1)}), bf16[16,432,128]{2,1,0:T(8,128)(2,1)}, u32[]{:S(2)}, u32[]{:S(2)}) %all-to-all-start.4) | async-done | bytes 1769504 | tf_op jit(solution)/shard_map/all_to_all | solution.py:102
  311.8 7.4 %all-to-all-start.2 = ((bf16[128,16,128]{2,1,0:T(8,128)(2,1)}), bf16[128,16,128]{2,1,0:T(8,128)(2,1)S(1)}, u32[]{:S(2)}, u32[]{:S(2)}) async-start(bf16[128,16,128]{2,1,0:T(8,128)(2,1)} %bitcast.132), calls=%async_computation.2 | async-start | bytes 1048576 | tf_op jit(solution)/shard_map/all_to_all | solution.py:102
  321.6 11.6 %all-to-all-done.2 = bf16[128,16,128]{2,1,0:T(8,128)(2,1)S(1)} async-done(((bf16[128,16,128]{2,1,0:T(8,128)(2,1)}), bf16[128,16,128]{2,1,0:T(8,128)(2,1)S(1)}, u32[]{:S(2)}, u32[]{:S(2)}) %all-to-all-start.2) | async-done | bytes 524320 | tf_op jit(solution)/shard_map/all_to_all | solution.py:102
  333.3 3.4 all-to-all-start.5
  336.8 6.6 %all-to-all-done.5 = bf16[8,64,128]{2,1,0:T(8,128)(2,1)S(1)} async-done(((bf16[8,64,128]{2,1,0:T(8,128)(2,1)}), bf16[8,64,128]{2,1,0:T(8,128)(2,1)S(1)}, u32[]{:S(2)}, u32[]{:S(2)}) %all-to-all-start.5) | async-done | bytes 131104 | tf_op jit(solution)/shard_map/all_to_all | solution.py:102
  344.2 5.1 %all-to-all-start.3 = ((bf16[128,16,128]{2,1,0:T(8,128)(2,1)}), bf16[128,16,128]{2,1,0:T(8,128)(2,1)S(1)}, u32[]{:S(2)}, u32[]{:S(2)}) async-start(bf16[128,16,128]{2,1,0:T(8,128)(2,1)} %broadcast_in_dim.53), calls=%async_computation.3 | async-start | bytes 1048576 | tf_op jit(solution)/shard_map/all_to_all | solution.py:108
  349.3 14.1 %all-to-all-done.3 = bf16[128,16,128]{2,1,0:T(8,128)(2,1)S(1)} async-done(((bf16[128,16,128]{2,1,0:T(8,128)(2,1)}), bf16[128,16,128]{2,1,0:T(8,128)(2,1)S(1)}, u32[]{:S(2)}, u32[]{:S(2)}) %all-to-all-start.3) | async-done | bytes 524320 | tf_op jit(solution)/shard_map/all_to_all | solution.py:108
  364.1 3.4 all-to-all-start.6
  369.3 4.9 %all-to-all-done.6 = bf16[8,64,128]{2,1,0:T(8,128)(2,1)S(1)} async-done(((bf16[8,64,128]{2,1,0:T(8,128)(2,1)}), bf16[8,64,128]{2,1,0:T(8,128)(2,1)S(1)}, u32[]{:S(2)}, u32[]{:S(2)}) %all-to-all-start.6) | async-done | bytes 131104 | tf_op jit(solution)/shard_map/all_to_all | solution.py:108
  (272 shorter events, 154.9 us)
Async XLA Ops:
  7.2 59.8 %copy-start = (bf16[3,3,3,64,128]{4,3,2,1,0:T(8,128)(2,1)S(1)}, bf16[3,3,3,64,128]{4,3,2,1,0:T(8,128)(2,1)}, u32[]{:S(2)}) copy-start(bf16[3,3,3,64,128]{4,3,2,1,0:T(8,128)(2,1)} %param.6) | copy-start | bytes 1327108
  9.1 14.5 %collective-permute-start = (bf16[1,8,256,64]{2,3,1,0:T(8,128)(2,1)S(1)}, bf16[1,8,256,64]{2,3,1,0:T(8,128)(2,1)}, u32[]{:S(2)}, u32[]{:S(2)}) collective-permute-start(bf16[1,8,256,64]{2,3,1,0:T(8,128)(2,1)S(1)} %get-tuple-element.9), channel_id=1, source_target_pairs={{0,8},{8,16},{16,24},{24,32},{32,40},{40,48},{48,56},{56,64},{64,7... | collective-permute-start | bytes 786440 | tf_op jit(solution)/shard_map/ppermute | solution.py:17
  14.0 10.7 %collective-permute-start.1 = (bf16[1,8,256,64]{2,3,1,0:T(8,128)(2,1)}, bf16[1,8,256,64]{2,3,1,0:T(8,128)(2,1)}, u32[]{:S(2)}, u32[]{:S(2)}) collective-permute-start(bf16[1,8,256,64]{2,3,1,0:T(8,128)(2,1)} %get-tuple-element.8), channel_id=1, source_target_pairs={{8,0},{16,8},{24,16},{32,24},{40,32},{48,40},{56,48},{64,56},{72,6... | collective-permute-start | bytes 786440 | tf_op jit(solution)/shard_map/ppermute | solution.py:19
  17.6 19.0 %all-to-all-start.1 = ((bf16[16,8,8,128]{3,2,1,0:T(8,128)(2,1)}), bf16[16,8,8,128]{3,2,1,0:T(8,128)(2,1)S(1)}, u32[]{:S(2)}, u32[]{:S(2)}) async-start(bf16[16,8,8,128]{3,2,1,0:T(8,128)(2,1)} %bitcast.32), calls=%async_computation.1 | async-start | bytes 524288 | tf_op jit(solution)/shard_map/all_to_all | solution.py:96
  23.5 101.4 %all-gather.2.cloned.1.call-start = ((), (), s32[]{:S(2)}) async-start(), calls=%async_computation.7 | async-start | bytes 1880064 | tf_op jit(solution)/shard_map/all_gather | solution.py:134
  26.6 14.5 %collective-permute-start.2 = (bf16[6,1,256,64]{2,3,1,0:T(8,128)(2,1)}, bf16[6,1,256,64]{2,3,1,0:T(8,128)(2,1)}, u32[]{:S(2)}, u32[]{:S(2)}) collective-permute-start(bf16[6,1,256,64]{2,3,1,0:T(8,128)(2,1)} %get-tuple-element.6), channel_id=1, source_target_pairs={{0,1},{1,2},{2,3},{3,4},{4,5},{5,6},{6,7},{8,9},{9,10},{10,11},{11... | collective-permute-start | bytes 589832 | tf_op jit(solution)/shard_map/ppermute | solution.py:17
  32.5 9.7 %collective-permute-start.3 = (bf16[6,1,256,64]{2,3,1,0:T(8,128)(2,1)}, bf16[6,1,256,64]{2,3,1,0:T(8,128)(2,1)S(1)}, u32[]{:S(2)}, u32[]{:S(2)}) collective-permute-start(bf16[6,1,256,64]{2,3,1,0:T(8,128)(2,1)} %get-tuple-element.7), channel_id=1, source_target_pairs={{1,0},{2,1},{3,2},{4,3},{5,4},{6,5},{7,6},{9,8},{10,9},{11,10},{12... | collective-permute-start | bytes 589832 | tf_op jit(solution)/shard_map/ppermute | solution.py:19
  37.5 51.2 %collective-permute-start.13 = (bf16[2,4,128,128]{2,3,1,0:T(8,128)(2,1)}, bf16[2,4,128,128]{2,3,1,0:T(8,128)(2,1)}, u32[]{:S(2)}, u32[]{:S(2)}) collective-permute-start(bf16[2,4,128,128]{2,3,1,0:T(8,128)(2,1)} %copy.205), channel_id=1, source_target_pairs={{0,0},{16,1},{32,2},{48,3},{64,4},{80,5},{96,6},{112,7},{8,8},{24,... | collective-permute-start | bytes 786440 | tf_op jit(solution)/shard_map/ppermute | solution.py:98
  82.9 12.4 %collective-permute-start.4 = (bf16[1,4,128,128]{3,2,1,0:T(8,128)(2,1)S(1)}, bf16[1,4,128,128]{3,2,1,0:T(8,128)(2,1)S(1)}, u32[]{:S(2)}, u32[]{:S(2)}) collective-permute-start(bf16[1,4,128,128]{3,2,1,0:T(8,128)(2,1)S(1)} %get-tuple-element.28), channel_id=1, source_target_pairs={{0,8},{8,16},{16,24},{24,32},{32,40},{40,48},{48,56},{56,64},{64,7... | collective-permute-start | bytes 393224 | tf_op jit(solution)/shard_map/ppermute | solution.py:17
  86.8 8.5 %collective-permute-start.5 = (bf16[1,4,128,128]{3,2,1,0:T(8,128)(2,1)S(1)}, bf16[1,4,128,128]{3,2,1,0:T(8,128)(2,1)S(1)}, u32[]{:S(2)}, u32[]{:S(2)}) collective-permute-start(bf16[1,4,128,128]{3,2,1,0:T(8,128)(2,1)S(1)} %get-tuple-element.29), channel_id=1, source_target_pairs={{8,0},{16,8},{24,16},{32,24},{40,32},{48,40},{56,48},{64,56},{72,6... | collective-permute-start | bytes 393224 | tf_op jit(solution)/shard_map/ppermute | solution.py:19
  89.7 18.7 %collective-permute-start.14 = (bf16[1,4,128,128]{3,2,1,0:T(8,128)(2,1)S(1)}, bf16[1,4,128,128]{3,2,1,0:T(8,128)(2,1)S(1)}, u32[]{:S(2)}, u32[]{:S(2)}) collective-permute-start(bf16[1,4,128,128]{3,2,1,0:T(8,128)(2,1)S(1)} %get-tuple-element.24), channel_id=1, source_target_pairs={{0,8},{8,16},{16,24},{24,32},{32,40},{40,48},{48,56},{56,64},{64,7... | collective-permute-start | bytes 393224 | tf_op jit(solution)/shard_map/ppermute | solution.py:17
  93.4 15.0 %collective-permute-start.15 = (bf16[1,4,128,128]{3,2,1,0:T(8,128)(2,1)S(1)}, bf16[1,4,128,128]{3,2,1,0:T(8,128)(2,1)S(1)}, u32[]{:S(2)}, u32[]{:S(2)}) collective-permute-start(bf16[1,4,128,128]{3,2,1,0:T(8,128)(2,1)S(1)} %get-tuple-element.25), channel_id=1, source_target_pairs={{8,0},{16,8},{24,16},{32,24},{40,32},{48,40},{56,48},{64,56},{72,6... | collective-permute-start | bytes 393224 | tf_op jit(solution)/shard_map/ppermute | solution.py:19
  95.4 20.8 %collective-permute-start.6 = (bf16[4,1,128,128]{3,2,1,0:T(8,128)(2,1)S(1)}, bf16[4,1,128,128]{3,2,1,0:T(8,128)(2,1)S(1)}, u32[]{:S(2)}, u32[]{:S(2)}) collective-permute-start(bf16[4,1,128,128]{3,2,1,0:T(8,128)(2,1)S(1)} %get-tuple-element.20), channel_id=1, source_target_pairs={{0,1},{1,2},{2,3},{3,4},{4,5},{5,6},{6,7},{8,9},{9,10},{10,11},{11... | collective-permute-start | bytes 393224 | tf_op jit(solution)/shard_map/ppermute | solution.py:17
  100.1 16.0 %collective-permute-start.7 = (bf16[4,1,128,128]{3,2,1,0:T(8,128)(2,1)S(1)}, bf16[4,1,128,128]{3,2,1,0:T(8,128)(2,1)S(1)}, u32[]{:S(2)}, u32[]{:S(2)}) collective-permute-start(bf16[4,1,128,128]{3,2,1,0:T(8,128)(2,1)S(1)} %get-tuple-element.21), channel_id=1, source_target_pairs={{1,0},{2,1},{3,2},{4,3},{5,4},{6,5},{7,6},{9,8},{10,9},{11,10},{12... | collective-permute-start | bytes 393224 | tf_op jit(solution)/shard_map/ppermute | solution.py:19
  109.3 10.3 %collective-permute-start.16 = (bf16[4,1,128,128]{3,2,1,0:T(8,128)(2,1)S(1)}, bf16[4,1,128,128]{3,2,1,0:T(8,128)(2,1)S(1)}, u32[]{:S(2)}, u32[]{:S(2)}) collective-permute-start(bf16[4,1,128,128]{3,2,1,0:T(8,128)(2,1)S(1)} %get-tuple-element.16), channel_id=1, source_target_pairs={{0,1},{1,2},{2,3},{3,4},{4,5},{5,6},{6,7},{8,9},{9,10},{10,11},{11... | collective-permute-start | bytes 393224 | tf_op jit(solution)/shard_map/ppermute | solution.py:17
  114.8 8.1 %collective-permute-start.17 = (bf16[4,1,128,128]{3,2,1,0:T(8,128)(2,1)S(1)}, bf16[4,1,128,128]{3,2,1,0:T(8,128)(2,1)S(1)}, u32[]{:S(2)}, u32[]{:S(2)}) collective-permute-start(bf16[4,1,128,128]{3,2,1,0:T(8,128)(2,1)S(1)} %get-tuple-element.17), channel_id=1, source_target_pairs={{1,0},{2,1},{3,2},{4,3},{5,4},{6,5},{7,6},{9,8},{10,9},{11,10},{12... | collective-permute-start | bytes 393224 | tf_op jit(solution)/shard_map/ppermute | solution.py:19
  146.2 12.1 %collective-permute-start.8 = (bf16[1,4,128,128]{2,3,1,0:T(8,128)(2,1)S(1)}, bf16[1,4,128,128]{2,3,1,0:T(8,128)(2,1)S(1)}, u32[]{:S(2)}, u32[]{:S(2)}) collective-permute-start(bf16[1,4,128,128]{2,3,1,0:T(8,128)(2,1)S(1)} %get-tuple-element.26), channel_id=1, source_target_pairs={{0,8},{8,16},{16,24},{24,32},{32,40},{40,48},{48,56},{56,64},{64,7... | collective-permute-start | bytes 393224 | tf_op jit(solution)/shard_map/ppermute | solution.py:17
  150.5 7.8 %collective-permute-start.9 = (bf16[1,4,128,128]{2,3,1,0:T(8,128)(2,1)S(1)}, bf16[1,4,128,128]{2,3,1,0:T(8,128)(2,1)S(1)}, u32[]{:S(2)}, u32[]{:S(2)}) collective-permute-start(bf16[1,4,128,128]{2,3,1,0:T(8,128)(2,1)S(1)} %get-tuple-element.27), channel_id=1, source_target_pairs={{8,0},{16,8},{24,16},{32,24},{40,32},{48,40},{56,48},{64,56},{72,6... | collective-permute-start | bytes 393224 | tf_op jit(solution)/shard_map/ppermute | solution.py:19
  152.5 14.1 %collective-permute-start.18 = (bf16[1,4,128,128]{2,3,1,0:T(8,128)(2,1)S(1)}, bf16[1,4,128,128]{2,3,1,0:T(8,128)(2,1)S(1)}, u32[]{:S(2)}, u32[]{:S(2)}) collective-permute-start(bf16[1,4,128,128]{2,3,1,0:T(8,128)(2,1)S(1)} %get-tuple-element.22), channel_id=1, source_target_pairs={{0,8},{8,16},{16,24},{24,32},{32,40},{40,48},{48,56},{56,64},{64,7... | collective-permute-start | bytes 393224 | tf_op jit(solution)/shard_map/ppermute | solution.py:17
  156.1 10.5 %collective-permute-start.19 = (bf16[1,4,128,128]{2,3,1,0:T(8,128)(2,1)S(1)}, bf16[1,4,128,128]{2,3,1,0:T(8,128)(2,1)S(1)}, u32[]{:S(2)}, u32[]{:S(2)}) collective-permute-start(bf16[1,4,128,128]{2,3,1,0:T(8,128)(2,1)S(1)} %get-tuple-element.23), channel_id=1, source_target_pairs={{8,0},{16,8},{24,16},{32,24},{40,32},{48,40},{56,48},{64,56},{72,6... | collective-permute-start | bytes 393224 | tf_op jit(solution)/shard_map/ppermute | solution.py:19
  158.4 15.2 %collective-permute-start.10 = (bf16[4,1,128,128]{2,3,1,0:T(8,128)(2,1)S(1)}, bf16[4,1,128,128]{2,3,1,0:T(8,128)(2,1)S(1)}, u32[]{:S(2)}, u32[]{:S(2)}) collective-permute-start(bf16[4,1,128,128]{2,3,1,0:T(8,128)(2,1)S(1)} %get-tuple-element.18), channel_id=1, source_target_pairs={{0,1},{1,2},{2,3},{3,4},{4,5},{5,6},{6,7},{8,9},{9,10},{10,11},{11... | collective-permute-start | bytes 393224 | tf_op jit(solution)/shard_map/ppermute | solution.py:17
  165.0 8.6 %collective-permute-start.11 = (bf16[4,1,128,128]{2,3,1,0:T(8,128)(2,1)S(1)}, bf16[4,1,128,128]{2,3,1,0:T(8,128)(2,1)S(1)}, u32[]{:S(2)}, u32[]{:S(2)}) collective-permute-start(bf16[4,1,128,128]{2,3,1,0:T(8,128)(2,1)S(1)} %get-tuple-element.19), channel_id=1, source_target_pairs={{1,0},{2,1},{3,2},{4,3},{5,4},{6,5},{7,6},{9,8},{10,9},{11,10},{12... | collective-permute-start | bytes 393224 | tf_op jit(solution)/shard_map/ppermute | solution.py:19
  166.6 42.7 %collective-permute-start.20 = (bf16[4,1,128,128]{2,3,1,0:T(8,128)(2,1)S(1)}, bf16[4,1,128,128]{2,3,1,0:T(8,128)(2,1)S(1)}, u32[]{:S(2)}, u32[]{:S(2)}) collective-permute-start(bf16[4,1,128,128]{2,3,1,0:T(8,128)(2,1)S(1)} %get-tuple-element.12), channel_id=1, source_target_pairs={{0,1},{1,2},{2,3},{3,4},{4,5},{5,6},{6,7},{8,9},{9,10},{10,11},{11... | collective-permute-start | bytes 393224 | tf_op jit(solution)/shard_map/ppermute | solution.py:17
  172.1 37.2 %collective-permute-start.21 = (bf16[4,1,128,128]{2,3,1,0:T(8,128)(2,1)S(1)}, bf16[4,1,128,128]{2,3,1,0:T(8,128)(2,1)S(1)}, u32[]{:S(2)}, u32[]{:S(2)}) collective-permute-start(bf16[4,1,128,128]{2,3,1,0:T(8,128)(2,1)S(1)} %get-tuple-element.13), channel_id=1, source_target_pairs={{1,0},{2,1},{3,2},{4,3},{5,4},{6,5},{7,6},{9,8},{10,9},{11,10},{12... | collective-permute-start | bytes 393224 | tf_op jit(solution)/shard_map/ppermute | solution.py:19
  173.6 31.6 %copy-start.26 = (bf16[4,1,128,128]{2,3,1,0:T(8,128)(2,1)}, bf16[4,1,128,128]{2,3,1,0:T(8,128)(2,1)S(1)}, u32[]{:S(2)}) copy-start(bf16[4,1,128,128]{2,3,1,0:T(8,128)(2,1)S(1)} %collective-permute-done.11) | copy-start | bytes 393220
  247.5 3.3 collective-permute-start.12
  252.8 30.8 %all-to-all-start = ((bf16[16,8,8,128]{3,2,1,0:T(8,128)(2,1)}), bf16[16,8,8,128]{3,2,1,0:T(8,128)(2,1)S(1)}, u32[]{:S(2)}, u32[]{:S(2)}) async-start(bf16[16,8,8,128]{3,2,1,0:T(8,128)(2,1)} %copy.201), calls=%async_computation | async-start | bytes 524288 | tf_op jit(solution)/shard_map/all_to_all | solution.py:88
  283.6 28.2 %all-to-all-start.4 = ((bf16[16,432,128]{2,1,0:T(8,128)(2,1)}), bf16[16,432,128]{2,1,0:T(8,128)(2,1)}, u32[]{:S(2)}, u32[]{:S(2)}) async-start(bf16[16,432,128]{2,1,0:T(8,128)(2,1)} %bitcast.1344), calls=%async_computation.4 | async-start | bytes 3538944 | tf_op jit(solution)/shard_map/all_to_all | solution.py:102
  311.8 21.5 %all-to-all-start.2 = ((bf16[128,16,128]{2,1,0:T(8,128)(2,1)}), bf16[128,16,128]{2,1,0:T(8,128)(2,1)S(1)}, u32[]{:S(2)}, u32[]{:S(2)}) async-start(bf16[128,16,128]{2,1,0:T(8,128)(2,1)} %bitcast.132), calls=%async_computation.2 | async-start | bytes 1048576 | tf_op jit(solution)/shard_map/all_to_all | solution.py:102
  333.3 10.1 %all-to-all-start.5 = ((bf16[8,64,128]{2,1,0:T(8,128)(2,1)}), bf16[8,64,128]{2,1,0:T(8,128)(2,1)S(1)}, u32[]{:S(2)}, u32[]{:S(2)}) async-start(bf16[8,64,128]{2,1,0:T(8,128)(2,1)} %bitcast.303), calls=%async_computation.5 | async-start | bytes 262144 | tf_op jit(solution)/shard_map/all_to_all | solution.py:102
  344.2 19.3 %all-to-all-start.3 = ((bf16[128,16,128]{2,1,0:T(8,128)(2,1)}), bf16[128,16,128]{2,1,0:T(8,128)(2,1)S(1)}, u32[]{:S(2)}, u32[]{:S(2)}) async-start(bf16[128,16,128]{2,1,0:T(8,128)(2,1)} %broadcast_in_dim.53), calls=%async_computation.3 | async-start | bytes 1048576 | tf_op jit(solution)/shard_map/all_to_all | solution.py:108
  364.1 10.1 %all-to-all-start.6 = ((bf16[8,64,128]{2,1,0:T(8,128)(2,1)}), bf16[8,64,128]{2,1,0:T(8,128)(2,1)S(1)}, u32[]{:S(2)}, u32[]{:S(2)}) async-start(bf16[8,64,128]{2,1,0:T(8,128)(2,1)} %broadcast_in_dim.54), calls=%async_computation.6 | async-start | bytes 262144 | tf_op jit(solution)/shard_map/all_to_all | solution.py:108
  (34 other events, 204.4 us)
Sparse Core Ops, SparseCore 0:
  34.6 36.3 all-gather.1

commit v2 on v1

v2 whole, which is shorter than its diff:
```python
import jax
import jax.numpy as jnp
import numpy as np
from jax import lax
from jax.experimental import pallas as pl
from jax.experimental.pallas import tpu as pltpu
from jax.sharding import PartitionSpec as P

leak_slope = 0.2
both = ("sx", "sy")
vmem_bytes = 56 * 1024 * 1024


def swap_places(ways):
    pairs = [(a * 8 + b, (2 * b + a % 2) * 8 + a // 2) for a in range(16) for b in range(8)]
    return pairs if ways > 0 else [(there, here) for here, there in pairs]


def neighbours(first, last, axis):
    ends = lax.axis_size(axis) - 1
    return (
        lax.ppermute(last, axis, [(i, i + 1) for i in range(ends)]),
        lax.ppermute(first, axis, [(i + 1, i) for i in range(ends)]),
    )


def sum_parts(parts, axis):
    got = lax.all_to_all(parts.astype(jnp.bfloat16), axis, 0, 0, tiled=True)
    return got.astype(jnp.float32).sum(0)


def spread_part(part, axis, count):
    part = part.astype(jnp.bfloat16)
    got = lax.all_to_all(
        jnp.broadcast_to(part[None], (count,) + part.shape), axis, 0, 0, tiled=True
    )
    return got.reshape((-1,) + part.shape[1:])


def dot(left, right):
    return jnp.dot(left, right, preferred_element_type=jnp.float32)


def row_before(values):
    rows = lax.broadcasted_iota(jnp.int32, values.shape, 0)
    return jnp.where(rows == 0, 0.0, pltpu.roll(values, 1, 0))


def row_after(values):
    count = values.shape[0]
    rows = lax.broadcasted_iota(jnp.int32, values.shape, 0)
    return jnp.where(rows == count - 1, 0.0, pltpu.roll(values, count - 1, 0))


def call(body, outs, scratch, operands, smem=0, flops=0, name=None):
    size = sum(int(np.prod(a.shape)) * a.dtype.itemsize for a in operands)
    size += sum(int(np.prod(shape)) * jnp.dtype(kind).itemsize for shape, kind in outs)
    whole = pl.BlockSpec(memory_space=pltpu.VMEM)
    specs = [whole] * (len(operands) - smem) + [pl.BlockSpec(memory_space=pltpu.SMEM)] * smem
    return pl.pallas_call(
        body,
        out_shape=[jax.ShapeDtypeStruct(shape, kind) for shape, kind in outs],
        in_specs=specs,
        out_specs=[whole] * len(outs),
        scratch_shapes=[pltpu.VMEM(shape, kind) for shape, kind in scratch],
        compiler_params=pltpu.CompilerParams(vmem_limit_bytes=vmem_bytes),
        cost_estimate=pl.CostEstimate(flops=flops, bytes_accessed=size, transcendentals=0),
        name=name,
    )(*operands)


def pair_select():
    sel = np.zeros((256, 4, 128), np.float32)
    for k, offset in enumerate((0, 1, -1, 2)):
        for p in range(128):
            if 0 <= 2 * p + offset < 256:
                sel[2 * p + offset, k, p] = 1
    return jnp.asarray(sel.reshape(256, 512), jnp.bfloat16)


def pair_filters(kernel):
    taps = kernel.reshape(9, 3, 64, 128)
    none = jnp.zeros((9, 64, 128), kernel.dtype)
    even = jnp.concatenate([taps[:, 1], taps[:, 2], taps[:, 0], none], axis=1)
    odd = jnp.concatenate([taps[:, 0], taps[:, 1], none, taps[:, 2]], axis=1)
    return jnp.concatenate([even, odd], axis=2)


def first_body(vc, vzl, vzh, vyl, vyh, w1, sel, pooled, bits, xt, xc, acc):
    for z in range(6):
        rows = vzl[0] if z == 0 else vzh[0] if z == 5 else vc[z - 1]
        got = dot(rows.reshape(512, 256), sel[...]).astype(jnp.bfloat16)
        low = dot(vyl[z, 0], sel[...]).astype(jnp.bfloat16)
        high = dot(vyh[z, 0], sel[...]).astype(jnp.bfloat16)
        for k in range(4):
            lanes = slice(k * 128, k * 128 + 128)
            place = slice(k * 64, k * 64 + 64)
            xt[z, place, 0:128] = low[:, lanes]
            xt[z, place, 1152:1280] = high[:, lanes]
            for y in range(8):
                xt[z, place, (y + 1) * 128 : (y + 2) * 128] = got[y * 64 : y * 64 + 64, lanes]
        xc[z] = xt[z].T

    @pl.loop(0, 2)
    def _(zp):
        for zz in range(2):
            total = None
            for a in range(3):
                for b in range(3):
                    part = dot(xc[2 * zp + zz + a, b * 128 : b * 128 + 1024, :], w1[3 * a + b])
                    total = part if total is None else total + part
            acc[zz] = total
        for yp in range(4):
            mean = jnp.zeros((128, 128), jnp.float32)
            mask = jnp.zeros((128, 128), jnp.int32)
            for zz in range(2):
                for yy in range(2):
                    for par in range(2):
                        row = (2 * yp + yy) * 128
                        v = acc[zz, row : row + 128, par * 128 : par * 128 + 128]
                        up = v > 0
                        mean += jnp.where(up, v, leak_slope * v)
                        mask |= jnp.where(up, 1 << (zz * 4 + yy * 2 + par), 0)
            pooled[zp, yp] = (mean * 0.125).astype(jnp.bfloat16)
            bits[zp, yp] = mask


def first_section(vc, vzl, vzh, vyl, vyh, w1):
    return call(
        first_body,
        [
            ((2, 4, 128, 128), jnp.bfloat16),
            ((2, 4, 128, 128), jnp.int32),
            ((6, 256, 1280), jnp.bfloat16),
        ],
        [((6, 1280, 256), jnp.bfloat16), ((2, 1024, 256), jnp.float32)],
        [vc, vzl, vzh, vyl, vyh, w1, pair_select()],
        flops=5_000_000_000,
        name="first",
    )


def lay_filters(place, tap_of, turn):
    for b in range(3):
        for four in range(4):
            for c in range(3):
                for two in range(2):
                    a = four - two
                    lanes = slice(c * 256 + two * 128, c * 256 + two * 128 + 128)
                    block = (b, slice(four * 128, four * 128 + 128), lanes)
                    if 0 <= a < 3:
                        tap = tap_of(a, b, c)
                        place[block] = tap.T if turn else tap
                    else:
                        place[block] = jnp.zeros((128, 128), jnp.bfloat16)


def conv_rows(source, lanes, filters, total, count):
    rows = count * 128
    parts = None
    for b in range(3):
        part = dot(source[b : b + count, :, lanes].reshape(rows, 512), filters[b])
        parts = part if parts is None else parts + part
    total[0:rows, :] = parts


def joined(total, y):
    rows = slice(y * 128, y * 128 + 128)
    return (
        row_before(total[rows, 0:256]) + total[rows, 256:512] + row_after(total[rows, 512:768])
    )


def cot_body(cc, cl, ch, k3, hidden_grad, cot3, cells, filters, total):
    for z in range(6):
        part = (cl, cc, ch)[z // 2]
        for y in range(8):
            cells[y, :, z * 128 : z * 128 + 128] = part[z % 2, y].T
    lay_filters(filters, lambda a, b, c: k3[(2 - a) * 9 + (2 - b) * 3 + 2 - c], True)
    for j in range(2):
        conv_rows(cells, slice(j * 256, j * 256 + 512), filters, total, 6)
        for y in range(6):
            hidden_grad[y, :, j * 256 : j * 256 + 256] = joined(total, y)
    for y in range(4):
        own = cells[y + 2, :, 256:512].astype(jnp.float32)
        rows = slice(y * 128, y * 128 + 128)
        cot3[rows, 0:256] = row_after(own).astype(jnp.bfloat16)
        cot3[rows, 256:512] = own.astype(jnp.bfloat16)
        cot3[rows, 512:768] = row_before(own).astype(jnp.bfloat16)


def cot_section(cc, cl, ch, k3):
    return call(
        cot_body,
        [((6, 128, 512), jnp.float32), ((512, 768), jnp.bfloat16)],
        [
            ((8, 128, 768), jnp.bfloat16),
            ((3, 512, 768), jnp.bfloat16),
            ((768, 768), jnp.float32),
        ],
        [cc, cl, ch, k3],
        flops=3_600_000_000,
        name="cot",
    )


def grad_taps(turned, cot3, store):
    for b in range(3):
        full = dot(turned[:, b * 128 : b * 128 + 512], cot3[...])
        for a in range(3):
            for c in range(3):
                low = full[a * 128 : a * 128 + 128, c * 256 : c * 256 + 128]
                high = full[a * 128 + 128 : a * 128 + 256, c * 256 + 128 : c * 256 + 256]
                store(9 * a + 3 * b + c, (low + high).astype(jnp.bfloat16))


def mid_body(
    pc, pzl, pzh, pyl, pyh, hidden_grad, cot3, k2, k3, flags,
    output, grads, spg, cells, hidden, filters, total, spg3, turned,
):
    for z in range(6):
        lanes = slice(z * 128, z * 128 + 128)
        part = (pzl, pc, pzh)[z // 2]
        for y in range(2):
            cells[y, :, lanes] = pyl[z, y]
            cells[y + 6, :, lanes] = pyh[z, y]
        for y in range(4):
            cells[y + 2, :, lanes] = part[z % 2, y]
    lay_filters(filters, lambda a, b, c: k2[9 * a + 3 * b + c], True)
    lane = lax.broadcasted_iota(jnp.int32, (128, 256), 1)
    for j in range(2):
        conv_rows(cells, slice(j * 256, j * 256 + 512), filters, total, 6)
        edge = lane < 128 if j == 0 else lane >= 128
        inside = jnp.where(edge, flags[j], 1.0)
        for y in range(6):
            pre = joined(total, y)
            keep = inside * flags[2] if y == 0 else inside * flags[3] if y == 5 else inside
            lanes = slice(j * 256, j * 256 + 256)
            up = pre > 0
            hidden[y, :, lanes] = (jnp.where(up, pre, leak_slope * pre) * keep).astype(
                jnp.bfloat16
            )
            back = hidden_grad[y, :, lanes]
            spg[y, :, lanes] = (jnp.where(up, back, leak_slope * back) * keep).astype(
                jnp.bfloat16
            )
    turned[...] = hidden[...].reshape(768, 512).T

    def store_third(tap, value):
        grads[27 + tap] = value

    grad_taps(turned, cot3, store_third)
    for y in range(4):
        own = spg[y + 1, :, 128:384].astype(jnp.float32)
        rows = slice(y * 128, y * 128 + 128)
        spg3[rows, 0:256] = row_after(own).astype(jnp.bfloat16)
        spg3[rows, 256:512] = own.astype(jnp.bfloat16)
        spg3[rows, 512:768] = row_before(own).astype(jnp.bfloat16)
    turned[...] = cells[1:7, :, 128:640].reshape(768, 512).T

    def store_second(tap, value):
        grads[tap] = value.T

    grad_taps(turned, spg3, store_second)
    lay_filters(filters, lambda a, b, c: k3[9 * a + 3 * b + c], False)
    conv_rows(hidden, slice(0, 512), filters, total, 4)
    for y in range(4):
        done = joined(total, y).astype(jnp.bfloat16)
        for z in range(2):
            output[z, y] = done[:, z * 128 : z * 128 + 128].T


def mid_section(pc, pzl, pzh, pyl, pyh, hidden_grad, cot3, k2, k3, flags):
    return call(
        mid_body,
        [
            ((2, 4, 128, 128), jnp.bfloat16),
            ((54, 128, 128), jnp.bfloat16),
            ((6, 128, 512), jnp.bfloat16),
        ],
        [
            ((8, 128, 768), jnp.bfloat16),
            ((6, 128, 512), jnp.bfloat16),
            ((3, 512, 768), jnp.bfloat16),
            ((768, 768), jnp.float32),
            ((512, 768), jnp.bfloat16),
            ((512, 768), jnp.bfloat16),
        ],
        [pc, pzl, pzh, pyl, pyh, hidden_grad, cot3, k2, k3, flags],
        smem=1,
        flops=7_000_000_000,
        name="mid",
    )


def last_body(spg, k2, xt, bits, first, filters, total, back, full):
    lay_filters(filters, lambda a, b, c: k2[(2 - a) * 9 + (2 - b) * 3 + 2 - c], False)
    conv_rows(spg, slice(0, 512), filters, total, 4)
    for y in range(4):
        grad = joined(total, y).astype(jnp.bfloat16).astype(jnp.float32)
        for z in range(2):
            share = grad[:, z * 128 : z * 128 + 128] * 0.125
            up, down = share.astype(jnp.bfloat16), (share * leak_slope).astype(jnp.bfloat16)
            up, down = up.astype(jnp.float32), down.astype(jnp.float32)
            mask = bits[z, y]
            for zz in range(2):
                for yy in range(2):
                    for par in range(2):
                        bit = mask & (1 << (zz * 4 + yy * 2 + par))
                        row = (2 * y + yy) * 128
                        back[2 * z + zz, row : row + 128, par * 128 : par * 128 + 128] = (
                            jnp.where(bit != 0, up, down).astype(jnp.bfloat16)
                        )
    for b in range(3):
        parts = None
        for z in range(4):
            left = xt[z : z + 3, :, b * 128 : b * 128 + 1024].reshape(768, 1024)
            part = dot(left, back[z])
            parts = part if parts is None else parts + part
        full[...] = parts
        for a in range(3):
            for c in range(3):
                even, odd = ((2, 0), (0, 1), (1, 3))[c]
                low = full[a * 256 + even * 64 : a * 256 + even * 64 + 64, 0:128]
                high = full[a * 256 + odd * 64 : a * 256 + odd * 64 + 64, 128:256]
                tap = (9 * a + 3 * b + c) * 64
                first[tap : tap + 64, :] = (low + high).astype(jnp.bfloat16)
    first[1728:2048, :] = jnp.zeros((320, 128), jnp.bfloat16)


def last_section(spg, k2, xt, bits):
    return call(
        last_body,
        [((2048, 128), jnp.bfloat16)],
        [
            ((3, 512, 768), jnp.bfloat16),
            ((768, 768), jnp.float32),
            ((4, 1024, 256), jnp.bfloat16),
            ((768, 256), jnp.float32),
        ],
        [spg, k2, xt, bits],
        flops=6_000_000_000,
        name="last",
    )[0]


def cot_to_cells(values):
    wide = jnp.pad(values, ((0, 0), (2, 2), (0, 0), (0, 0)))
    parts = jnp.stack([wide[:, 4 * k : 4 * k + 8] for k in range(8)])
    parts = lax.all_to_all(parts.reshape(16, 2, 8, 8, 128), "sx", 0, 0, tiled=True)
    cells = parts.transpose(1, 2, 0, 3, 4).reshape(2, 8, 128, 128)
    return lax.ppermute(cells, both, swap_places(-1))


def output_to_channels(values):
    moved = lax.ppermute(values, both, swap_places(1))
    parts = jnp.swapaxes(moved.reshape(8, 16, 8, 128), 0, 1)
    parts = lax.all_to_all(parts, "sx", 0, 0, tiled=True)
    parts = parts.reshape(8, 2, 2, 4, 8, 128).transpose(1, 2, 0, 3, 4, 5)
    return parts.reshape(4, 32, 8, 128)


def on_device(volume, first_kernel, second_kernel, third_kernel, cotangent):
    sx, sy = lax.axis_index("sx"), lax.axis_index("sy")
    flags = jnp.stack([sx > 0, sx < 15, sy > 0, sy < 7]).astype(jnp.float32)
    vc = jnp.swapaxes(volume, 2, 3)
    vzl, vzh = neighbours(vc[:1], vc[-1:], "sx")
    deep = lambda y: jnp.concatenate([vzl[:, y : y + 1], vc[:, y : y + 1], vzh[:, y : y + 1]])
    vyl, vyh = neighbours(deep(0), deep(7), "sy")
    shares = jnp.concatenate(
        [jnp.swapaxes(second_kernel, 3, 4).reshape(216, 128), third_kernel.reshape(216, 128)]
    )
    filters = lax.all_gather(shares, "sx", axis=0, tiled=True).reshape(16, 54, 8, 128)
    filters = filters.swapaxes(0, 1).reshape(54, 128, 128)
    k2, k3 = filters[:27], filters[27:]
    cc = cot_to_cells(jnp.swapaxes(cotangent, 2, 3))
    cl, ch = neighbours(cc, cc, "sx")
    pooled, bits, xt = first_section(vc, vzl, vzh, vyl, vyh, pair_filters(first_kernel))
    hidden_grad, cot3 = cot_section(cc, cl, ch, k3)
    pzl, pzh = neighbours(pooled, pooled, "sx")
    tall = jnp.concatenate([pzl, pooled, pzh])
    pyl, pyh = neighbours(tall[:, :2], tall[:, 2:], "sy")
    output, grads, spg = mid_section(
        pooled, pzl, pzh, pyl, pyh, hidden_grad, cot3, k2, k3, flags
    )
    first_part = last_section(spg, k2, xt, bits)
    output = jnp.swapaxes(output_to_channels(output), 2, 3)
    share = sum_parts(grads.reshape(54, 16, 8, 128).swapaxes(0, 1).reshape(16, 432, 128), "sx")
    share = sum_parts(jnp.pad(share, ((0, 80), (0, 0))).reshape(8, 64, 128), "sy")
    share = spread_part(share, "sy", 8)[:432].astype(jnp.float32).reshape(2, 3, 3, 3, 8, 128)
    second_grad, third_grad = jnp.swapaxes(share[0], 3, 4), share[1]
    first_sum = spread_part(sum_parts(first_part.reshape(128, 16, 128), both), both, 128)
    first_grad = first_sum[:1728].astype(jnp.float32).reshape(3, 3, 3, 64, 128)
    return (output, first_grad, second_grad, third_grad)


def solution(mesh):
    in_specs = (
        P("sx", "sy", None, None),
        P(),
        P(None, None, None, None, "sx"),
        P(None, None, None, "sx", None),
        P("sy", None, None, "sx"),
    )
    out_specs = (
        P("sy", None, None, "sx"),
        P(),
        P(None, None, None, None, "sx"),
        P(None, None, None, "sx", None),
    )
    return jax.shard_map(
        on_device, mesh=mesh, in_specs=in_specs, out_specs=out_specs, check_vma=False
    )
```

time: 389 us -> 280 us (0.72); the launches traced: 382 us -> 278 us
  matrix products: 84.6 us -> 0 us
  Pallas kernels: 0 us -> 44.1 us
  local copies, waits for them, and re-layouts: 70.1 us -> 26.2 us
  waiting for transfers between devices: 61.7 us -> 89.2 us
  starting transfers between devices: 123 us -> 99.2 us
  other arithmetic: 26.9 us -> 4.91 us
    dot_general x81 -> x0, matrix products: 64.4 us -> none  [kernel_grad(): lax.dot_general(window, flat_cot, (((0,), (0,)), ((), ())), preferred_ele...]
    pallas_call x0 -> x4, Pallas kernels: none -> 44.1 us  [call(): pl.pallas_call(body, out_shape=[jax.ShapeDtypeStruct(shape, kind) for sha...]
    ppermute x22 -> x12, waiting for transfers between devices: 4.42 us -> 33.6 us  [the longest x5 17.3 us: neighbours(): lax.ppermute(first, axis, [(i + 1, i) for i in range(ends)])]
    conv_general_dilated x17 -> x0, local copies, waits for them, and re-layouts: 24.2 us -> none  [conv_valid(): lax.conv_general_dilated(padded[None], kernel, (1, 1, 1), 'VALID', dimens...]
    ppermute x22 -> x12, starting transfers between devices: 69.9 us -> 47.7 us  [the longest x5 37 us: neighbours(): lax.ppermute(last, axis, [(i, i + 1) for i in range(ends)])]
    conv_general_dilated x5 -> x0, matrix products: 20.2 us -> none  [conv_valid(): lax.conv_general_dilated(padded[None], kernel, (1, 1, 1), 'VALID', dimens...]
    broadcast_in_dim x5 -> x0, other arithmetic: 9.17 us -> none  [conv_valid(): padded[None]]
    unnamed x81 -> x34, local copies, waits for them, and re-layouts: 21.3 us -> 13.7 us
  transfers between devices with their start and end apart: 30 -> 20, of which waited for: 8 -> 13; matrix products, arithmetic and copies ran while one was open for 30% -> 9% of each run, Pallas kernels for 0% -> 11%
where the time goes in v2:
time: 280 us; the launch traced here: 278 us
  starting transfers between devices  99.2 us (35%)
  waiting for transfers between devices  89.2 us (32%)
  Pallas kernels  44.1 us (16%)
  local copies, waits for them, and re-layouts  26.2 us (9%)
  between operations  14.4 us (5%)
  other arithmetic  4.91 us (2%)
    pallas_call x4, Pallas kernels, call(): pl.pallas_call(body, out_shape=[jax.ShapeDtypeStruct(shape, kind) for sha...  44.1 us
    ppermute x5, starting transfers between devices, neighbours(): lax.ppermute(last, axis, [(i, i + 1) for i in range(ends)])  37 us
    all_to_all x3, waiting for transfers between devices, sum_parts(): got = lax.all_to_all(parts.astype(jnp.bfloat16), axis, 0, 0, tiled=True)  32.1 us
    all_to_all x1, starting transfers between devices, output_to_channels(): parts = lax.all_to_all(parts, 'sx', 0, 0, tiled=True)  22 us
    all_to_all x2, waiting for transfers between devices, spread_part(): lax.all_to_all(jnp.broadcast_to(part[None], (count,) + part.shape), axis,...  19.1 us
    ppermute x5, waiting for transfers between devices, neighbours(): lax.ppermute(first, axis, [(i + 1, i) for i in range(ends)])  17.3 us
    ppermute x5, waiting for transfers between devices, neighbours(): lax.ppermute(last, axis, [(i, i + 1) for i in range(ends)])  16.3 us
    all_to_all x3, starting transfers between devices, sum_parts(): got = lax.all_to_all(parts.astype(jnp.bfloat16), axis, 0, 0, tiled=True)  13.8 us
  transfers between devices with their start and end apart: 20, of which 13 were waited for; matrix products, arithmetic and copies ran while one was open for 9% of the time, Pallas kernels for 11%

profile of v2, /device:TPU:1, one launch (start us, length us, event | category | flops | bytes accessed | tf_op | source)
XLA Modules:
  0.0 278.0 jit_solution(12599764421296589508)
XLA Ops:
  20.6 7.2 %all-to-all-start = ((bf16[16,2,8,8,128]{4,3,2,1,0:T(8,128)(2,1)}), bf16[16,2,8,8,128]{4,3,2,1,0:T(8,128)(2,1)S(1)}, u32[]{:S(2)}, u32[]{:S(2)}) async-start(bf16[16,2,8,8,128]{4,3,2,1,0:T(8,128)(2,1)} %bitcast.14), calls=%async_computation | async-start | bytes 1048576 | tf_op jit(solution)/shard_map/all_to_all | solution.py:350
  27.8 2.0 collective-permute-start.1
  29.8 3.5 %collective-permute-start = (bf16[1,8,64,256]{3,2,1,0:T(8,128)(2,1)S(1)}, bf16[1,8,64,256]{3,2,1,0:T(8,128)(2,1)S(1)}, u32[]{:S(2)}, u32[]{:S(2)}) collective-permute-start(bf16[1,8,64,256]{3,2,1,0:T(8,128)(2,1)S(1)} %get-tuple-element.25), channel_id=1, source_target_pairs={{0,8},{8,16},{16,24},{24,32},{32,40},{40,48},{48,56},{56,64},{64,7... | collective-permute-start | bytes 786440 | tf_op jit(solution)/shard_map/ppermute | solution.py:22
  33.5 9.5 %collective-permute-done.1.vzh = bf16[1,8,64,256]{3,2,1,0:T(8,128)(2,1)S(1)} collective-permute-done((bf16[1,8,64,256]{3,2,1,0:T(8,128)(2,1)S(1)}, bf16[1,8,64,256]{3,2,1,0:T(8,128)(2,1)S(1)}, u32[]{:S(2)}, u32[]{:S(2)}) %collective-permute-start.1) | collective-permute-done | bytes 262176 | tf_op jit(solution)/shard_map/ppermute | solution.py:23
  43.0 6.5 %collective-permute-done.vzl = bf16[1,8,64,256]{3,2,1,0:T(8,128)(2,1)S(1)} collective-permute-done((bf16[1,8,64,256]{3,2,1,0:T(8,128)(2,1)S(1)}, bf16[1,8,64,256]{3,2,1,0:T(8,128)(2,1)S(1)}, u32[]{:S(2)}, u32[]{:S(2)}) %collective-permute-start) | collective-permute-done | bytes 262176 | tf_op jit(solution)/shard_map/ppermute | solution.py:22
  49.5 2.7 collective-permute-start.2
  54.9 5.4 %collective-permute-done.3.vyh = bf16[6,1,64,256]{3,2,1,0:T(8,128)(2,1)S(1)} collective-permute-done((bf16[6,1,64,256]{3,2,1,0:T(8,128)(2,1)S(1)}, bf16[6,1,64,256]{3,2,1,0:T(8,128)(2,1)S(1)}, u32[]{:S(2)}, u32[]{:S(2)}) %collective-permute-start.3) | collective-permute-done | bytes 196640 | tf_op jit(solution)/shard_map/ppermute | solution.py:23
  61.0 11.3 %first.1 = (bf16[2,4,128,128]{3,2,1,0:T(8,128)(2,1)}, s32[2,4,128,128]{3,2,1,0:T(8,128)}, bf16[6,256,1280]{2,1,0:T(8,128)(2,1)}) custom-call(bf16[4,8,64,256]{3,2,1,0:T(8,128)(2,1)} %bitcast.100, bf16[1,8,64,256]{3,2,1,0:T(8,128)(2,1)} %copy-done.5, bf16[1,8,64,256]{3,2,1,0:T(8,128)(2,1)} %copy-done.4, bf16[6,1,64,256]{3,2,1,0:T(8,128)(2,1)} %copy-done.10, ...), custom_call_target="tpu_custom_call" | custom-call | flops 5000000000 | bytes 8126464 | tf_op jit(solution)/shard_map/first/pallas_call | solution.py:60
  72.3 5.5 %collective-permute-start.4 = (bf16[2,4,128,128]{3,2,1,0:T(8,128)(2,1)}, bf16[2,4,128,128]{3,2,1,0:T(8,128)(2,1)S(1)}, u32[]{:S(2)}, u32[]{:S(2)}) collective-permute-start(bf16[2,4,128,128]{3,2,1,0:T(8,128)(2,1)} %get-tuple-element.12.pc), channel_id=1, source_target_pairs={{0,8},{8,16},{16,24},{24,32},{32,40},{40,48},{48,56},{56,64},{64,7... | collective-permute-start | bytes 786440 | tf_op jit(solution)/shard_map/ppermute | solution.py:22
  78.5 1.9 collective-permute-start.5
  81.2 3.0 %collective-permute-done.4.pzl = bf16[2,4,128,128]{3,2,1,0:T(8,128)(2,1)S(1)} collective-permute-done((bf16[2,4,128,128]{3,2,1,0:T(8,128)(2,1)}, bf16[2,4,128,128]{3,2,1,0:T(8,128)(2,1)S(1)}, u32[]{:S(2)}, u32[]{:S(2)}) %collective-permute-start.4) | collective-permute-done | bytes 262176 | tf_op jit(solution)/shard_map/ppermute | solution.py:22
  87.8 8.3 %collective-permute-start.6 = (bf16[6,2,128,128]{3,2,1,0:T(8,128)(2,1)S(1)}, bf16[6,2,128,128]{3,2,1,0:T(8,128)(2,1)}, u32[]{:S(2)}, u32[]{:S(2)}) collective-permute-start(bf16[6,2,128,128]{3,2,1,0:T(8,128)(2,1)S(1)} %get-tuple-element.27), channel_id=1, source_target_pairs={{0,1},{1,2},{2,3},{3,4},{4,5},{5,6},{6,7},{8,9},{9,10},{10,11},{11... | collective-permute-start | bytes 1179656 | tf_op jit(solution)/shard_map/ppermute | solution.py:22
  96.1 1.9 collective-permute-start.10
  98.0 16.9 %collective-permute-start.9 = (bf16[2,8,128,128]{3,2,1,0:T(8,128)(2,1)S(1)}, bf16[2,8,128,128]{3,2,1,0:T(8,128)(2,1)S(1)}, u32[]{:S(2)}, u32[]{:S(2)}) collective-permute-start(bf16[2,8,128,128]{3,2,1,0:T(8,128)(2,1)S(1)} %collective-permute-done.8.cc), channel_id=1, source_target_pairs={{0,8},{8,16},{16,24},{24,32},{32,40},{40,48},{48,56},{56,64},{64,7... | collective-permute-start | bytes 1572872 | tf_op jit(solution)/shard_map/ppermute | solution.py:22
  116.5 1.8 copy_bitcast_fusion.1
  119.6 6.8 %collective-permute-done.9.cl = bf16[2,8,128,128]{3,2,1,0:T(8,128)(2,1)S(1)} collective-permute-done((bf16[2,8,128,128]{3,2,1,0:T(8,128)(2,1)S(1)}, bf16[2,8,128,128]{3,2,1,0:T(8,128)(2,1)S(1)}, u32[]{:S(2)}, u32[]{:S(2)}) %collective-permute-start.9) | collective-permute-done | bytes 524320 | tf_op jit(solution)/shard_map/ppermute | solution.py:22
  127.3 7.2 %cot.1 = (f32[6,128,512]{2,1,0:T(8,128)}, bf16[512,768]{1,0:T(8,128)(2,1)}) custom-call(bf16[2,8,128,128]{3,2,1,0:T(8,128)(2,1)} %copy-done.6, bf16[2,8,128,128]{3,2,1,0:T(8,128)(2,1)} %copy-done.8, bf16[2,8,128,128]{3,2,1,0:T(8,128)(2,1)} %copy-done.7, bf16[27,128,128]{2,1,0:T(8,128)(2,1)} %get-tuple-element.38.k3), custom_call_target="tpu_custom_call" | custom-call | flops 3600000000 | bytes 4816896 | tf_op jit(solution)/shard_map/cot/pallas_call | solution.py:60
  135.2 14.4 %mid.1 = (bf16[2,4,128,128]{3,2,1,0:T(8,128)(2,1)}, bf16[54,128,128]{2,1,0:T(8,128)(2,1)}, bf16[6,128,512]{2,1,0:T(8,128)(2,1)}) custom-call(bf16[2,4,128,128]{3,2,1,0:T(8,128)(2,1)} %get-tuple-element.12.pc, bf16[2,4,128,128]{3,2,1,0:T(8,128)(2,1)} %copy-done.2, bf16[2,4,128,128]{3,2,1,0:T(8,128)(2,1)} %copy-done.3, ...), custom_call_target="tpu_custom_call" | custom-call | flops 7000000000 | bytes 8519696 | tf_op jit(solution)/shard_map/mid/pallas_call | solution.py:60
  152.0 22.0 %all-to-all-start.1 = ((bf16[16,8,8,128]{3,2,1,0:T(8,128)(2,1)}), bf16[16,8,8,128]{3,2,1,0:T(8,128)(2,1)S(1)}, u32[]{:S(2)}, u32[]{:S(2)}) async-start(bf16[16,8,8,128]{3,2,1,0:T(8,128)(2,1)} %bitcast.87), calls=%async_computation.1 | async-start | bytes 524288 | tf_op jit(solution)/shard_map/all_to_all | solution.py:358
  174.1 3.0 %copy_bitcast_fusion = bf16[16,432,128]{2,1,0:T(8,128)(2,1)} fusion(bf16[54,128,128]{2,1,0:T(8,128)(2,1)} %get-tuple-element.19), kind=kLoop, calls=%fused_computation | loop fusion | bytes 3538944 | tf_op jit(solution)/shard_map/reshape | solution.py:388
  177.1 4.4 %all-to-all-done.1 = bf16[16,8,8,128]{3,2,1,0:T(8,128)(2,1)S(1)} async-done(((bf16[16,8,8,128]{3,2,1,0:T(8,128)(2,1)}), bf16[16,8,8,128]{3,2,1,0:T(8,128)(2,1)S(1)}, u32[]{:S(2)}, u32[]{:S(2)}) %all-to-all-start.1) | async-done | bytes 262176 | tf_op jit(solution)/shard_map/all_to_all | solution.py:358
  181.5 3.9 %all-to-all-start.4 = ((bf16[16,432,128]{2,1,0:T(8,128)(2,1)}), bf16[16,432,128]{2,1,0:T(8,128)(2,1)S(1)}, u32[]{:S(2)}, u32[]{:S(2)}) async-start(bf16[16,432,128]{2,1,0:T(8,128)(2,1)} %copy_bitcast_fusion), calls=%async_computation.4 | async-start | bytes 3538944 | tf_op jit(solution)/shard_map/all_to_all | solution.py:28
  185.4 11.1 %last.1 = bf16[2048,128]{1,0:T(8,128)(2,1)} custom-call(bf16[6,128,512]{2,1,0:T(8,128)(2,1)} %get-tuple-element.16.spg, bf16[27,128,128]{2,1,0:T(8,128)(2,1)} %get-tuple-element.37.k2, bf16[6,256,1280]{2,1,0:T(8,128)(2,1)} %get-tuple-element.17.xt, s32[2,4,128,128]{3,2,1,0:T(8,128)} %get-tuple-element.18.bits), custom_call_target="tpu_custom_call" | custom-call | flops 6000000000 | bytes 6651904 | tf_op jit(solution)/shard_map/last/pallas_call | solution.py:60
  196.5 12.4 %all-to-all-done.4 = bf16[16,432,128]{2,1,0:T(8,128)(2,1)S(1)} async-done(((bf16[16,432,128]{2,1,0:T(8,128)(2,1)}), bf16[16,432,128]{2,1,0:T(8,128)(2,1)S(1)}, u32[]{:S(2)}, u32[]{:S(2)}) %all-to-all-start.4) | async-done | bytes 1769504 | tf_op jit(solution)/shard_map/all_to_all | solution.py:28
  208.9 6.5 %all-to-all-start.2 = ((bf16[128,16,128]{2,1,0:T(8,128)(2,1)}), bf16[128,16,128]{2,1,0:T(8,128)(2,1)S(1)}, u32[]{:S(2)}, u32[]{:S(2)}) async-start(bf16[128,16,128]{2,1,0:T(8,128)(2,1)} %bitcast.103), calls=%async_computation.2 | async-start | bytes 1048576 | tf_op jit(solution)/shard_map/all_to_all | solution.py:28
  216.3 13.1 %all-to-all-done.2 = bf16[128,16,128]{2,1,0:T(8,128)(2,1)S(1)} async-done(((bf16[128,16,128]{2,1,0:T(8,128)(2,1)}), bf16[128,16,128]{2,1,0:T(8,128)(2,1)S(1)}, u32[]{:S(2)}, u32[]{:S(2)}) %all-to-all-start.2) | async-done | bytes 524320 | tf_op jit(solution)/shard_map/all_to_all | solution.py:28
  229.5 3.4 %all-to-all-start.5 = ((bf16[8,64,128]{2,1,0:T(8,128)(2,1)}), bf16[8,64,128]{2,1,0:T(8,128)(2,1)S(1)}, u32[]{:S(2)}, u32[]{:S(2)}) async-start(bf16[8,64,128]{2,1,0:T(8,128)(2,1)} %bitcast.40), calls=%async_computation.5 | async-start | bytes 262144 | tf_op jit(solution)/shard_map/all_to_all | solution.py:28
  233.0 6.6 %all-to-all-done.5 = bf16[8,64,128]{2,1,0:T(8,128)(2,1)S(1)} async-done(((bf16[8,64,128]{2,1,0:T(8,128)(2,1)}), bf16[8,64,128]{2,1,0:T(8,128)(2,1)S(1)}, u32[]{:S(2)}, u32[]{:S(2)}) %all-to-all-start.5) | async-done | bytes 131104 | tf_op jit(solution)/shard_map/all_to_all | solution.py:28
  240.4 5.1 %all-to-all-start.3 = ((bf16[128,16,128]{2,1,0:T(8,128)(2,1)}), bf16[128,16,128]{2,1,0:T(8,128)(2,1)S(1)}, u32[]{:S(2)}, u32[]{:S(2)}) async-start(bf16[128,16,128]{2,1,0:T(8,128)(2,1)} %broadcast_in_dim.7), calls=%async_computation.3 | async-start | bytes 1048576 | tf_op jit(solution)/shard_map/all_to_all | solution.py:34
  245.5 14.1 %all-to-all-done.3 = bf16[128,16,128]{2,1,0:T(8,128)(2,1)S(1)} async-done(((bf16[128,16,128]{2,1,0:T(8,128)(2,1)}), bf16[128,16,128]{2,1,0:T(8,128)(2,1)S(1)}, u32[]{:S(2)}, u32[]{:S(2)}) %all-to-all-start.3) | async-done | bytes 524320 | tf_op jit(solution)/shard_map/all_to_all | solution.py:34
  260.3 3.4 %all-to-all-start.6 = ((bf16[8,64,128]{2,1,0:T(8,128)(2,1)}), bf16[8,64,128]{2,1,0:T(8,128)(2,1)S(1)}, u32[]{:S(2)}, u32[]{:S(2)}) async-start(bf16[8,64,128]{2,1,0:T(8,128)(2,1)} %broadcast_in_dim.8), calls=%async_computation.6 | async-start | bytes 262144 | tf_op jit(solution)/shard_map/all_to_all | solution.py:34
  265.5 4.9 %all-to-all-done.6 = bf16[8,64,128]{2,1,0:T(8,128)(2,1)S(1)} async-done(((bf16[8,64,128]{2,1,0:T(8,128)(2,1)}), bf16[8,64,128]{2,1,0:T(8,128)(2,1)S(1)}, u32[]{:S(2)}, u32[]{:S(2)}) %all-to-all-start.6) | async-done | bytes 131104 | tf_op jit(solution)/shard_map/all_to_all | solution.py:34
  (77 shorter events, 33.7 us)
Async XLA Ops:
  7.2 20.6 %copy-start = (bf16[4,8,256,64]{2,3,1,0:T(8,128)(2,1)S(1)}, bf16[4,8,256,64]{2,3,1,0:T(8,128)(2,1)}, u32[]{:S(2)}) copy-start(bf16[4,8,256,64]{2,3,1,0:T(8,128)(2,1)} %param.6) | copy-start | bytes 3145732
  7.2 107.7 %all-gather.2.cloned.1.call-start = ((), (), s32[]{:S(2)}) async-start(), calls=%async_computation.7 | async-start | bytes 1880064 | tf_op jit(solution)/shard_map/all_gather | solution.py:373
  8.8 24.6 %copy-start.1 = (bf16[3,3,3,64,128]{4,3,2,1,0:T(8,128)(2,1)S(1)}, bf16[3,3,3,64,128]{4,3,2,1,0:T(8,128)(2,1)}, u32[]{:S(2)}) copy-start(bf16[3,3,3,64,128]{4,3,2,1,0:T(8,128)(2,1)} %param.7) | copy-start | bytes 1327108
  20.6 59.8 %all-to-all-start = ((bf16[16,2,8,8,128]{4,3,2,1,0:T(8,128)(2,1)}), bf16[16,2,8,8,128]{4,3,2,1,0:T(8,128)(2,1)S(1)}, u32[]{:S(2)}, u32[]{:S(2)}) async-start(bf16[16,2,8,8,128]{4,3,2,1,0:T(8,128)(2,1)} %bitcast.14), calls=%async_computation | async-start | bytes 1048576 | tf_op jit(solution)/shard_map/all_to_all | solution.py:350
  27.8 15.2 %collective-permute-start.1 = (bf16[1,8,64,256]{3,2,1,0:T(8,128)(2,1)S(1)}, bf16[1,8,64,256]{3,2,1,0:T(8,128)(2,1)S(1)}, u32[]{:S(2)}, u32[]{:S(2)}) collective-permute-start(bf16[1,8,64,256]{3,2,1,0:T(8,128)(2,1)S(1)} %get-tuple-element.24), channel_id=1, source_target_pairs={{8,0},{16,8},{24,16},{32,24},{40,32},{48,40},{56,48},{64,56},{72,6... | collective-permute-start | bytes 786440 | tf_op jit(solution)/shard_map/ppermute | solution.py:23
  29.8 19.7 %collective-permute-start = (bf16[1,8,64,256]{3,2,1,0:T(8,128)(2,1)S(1)}, bf16[1,8,64,256]{3,2,1,0:T(8,128)(2,1)S(1)}, u32[]{:S(2)}, u32[]{:S(2)}) collective-permute-start(bf16[1,8,64,256]{3,2,1,0:T(8,128)(2,1)S(1)} %get-tuple-element.25), channel_id=1, source_target_pairs={{0,8},{8,16},{16,24},{24,32},{32,40},{40,48},{48,56},{56,64},{64,7... | collective-permute-start | bytes 786440 | tf_op jit(solution)/shard_map/ppermute | solution.py:22
  43.0 17.3 %copy-start.4 = (bf16[1,8,64,256]{3,2,1,0:T(8,128)(2,1)}, bf16[1,8,64,256]{3,2,1,0:T(8,128)(2,1)S(1)}, u32[]{:S(2)}) copy-start(bf16[1,8,64,256]{3,2,1,0:T(8,128)(2,1)S(1)} %collective-permute-done.1.vzh) | copy-start | bytes 786436
  49.5 10.8 %copy-start.5 = (bf16[1,8,64,256]{3,2,1,0:T(8,128)(2,1)}, bf16[1,8,64,256]{3,2,1,0:T(8,128)(2,1)S(1)}, u32[]{:S(2)}) copy-start(bf16[1,8,64,256]{3,2,1,0:T(8,128)(2,1)S(1)} %collective-permute-done.vzl) | copy-start | bytes 786436
  49.5 5.3 %collective-permute-start.2 = (bf16[6,1,64,256]{3,2,1,0:T(8,128)(2,1)S(1)}, bf16[6,1,64,256]{3,2,1,0:T(8,128)(2,1)S(1)}, u32[]{:S(2)}, u32[]{:S(2)}) collective-permute-start(bf16[6,1,64,256]{3,2,1,0:T(8,128)(2,1)S(1)} %pad_maximum_fusion), channel_id=1, source_target_pairs={{0,1},{1,2},{2,3},{3,4},{4,5},{5,6},{6,7},{8,9},{9,10},{10,11},{11... | collective-permute-start | bytes 589832 | tf_op jit(solution)/shard_map/ppermute | solution.py:22
  52.3 8.0 %collective-permute-start.3 = (bf16[6,1,64,256]{3,2,1,0:T(8,128)(2,1)S(1)}, bf16[6,1,64,256]{3,2,1,0:T(8,128)(2,1)S(1)}, u32[]{:S(2)}, u32[]{:S(2)}) collective-permute-start(bf16[6,1,64,256]{3,2,1,0:T(8,128)(2,1)S(1)} %pad_maximum_fusion.1), channel_id=1, source_target_pairs={{1,0},{2,1},{3,2},{4,3},{5,4},{6,5},{7,6},{9,8},{10,9},{11,10},{12... | collective-permute-start | bytes 589832 | tf_op jit(solution)/shard_map/ppermute | solution.py:23
  54.9 5.4 %copy-start.10 = (bf16[6,1,64,256]{3,2,1,0:T(8,128)(2,1)}, bf16[6,1,64,256]{3,2,1,0:T(8,128)(2,1)S(1)}, u32[]{:S(2)}) copy-start(bf16[6,1,64,256]{3,2,1,0:T(8,128)(2,1)S(1)} %collective-permute-done.2.vyl) | copy-start | bytes 589828
  60.3 0.7 copy-start.11
  72.3 11.9 %collective-permute-start.4 = (bf16[2,4,128,128]{3,2,1,0:T(8,128)(2,1)}, bf16[2,4,128,128]{3,2,1,0:T(8,128)(2,1)S(1)}, u32[]{:S(2)}, u32[]{:S(2)}) collective-permute-start(bf16[2,4,128,128]{3,2,1,0:T(8,128)(2,1)} %get-tuple-element.12.pc), channel_id=1, source_target_pairs={{0,8},{8,16},{16,24},{24,32},{32,40},{40,48},{48,56},{56,64},{64,7... | collective-permute-start | bytes 786440 | tf_op jit(solution)/shard_map/ppermute | solution.py:22
  78.5 7.9 %collective-permute-start.5 = (bf16[2,4,128,128]{3,2,1,0:T(8,128)(2,1)}, bf16[2,4,128,128]{3,2,1,0:T(8,128)(2,1)S(1)}, u32[]{:S(2)}, u32[]{:S(2)}) collective-permute-start(bf16[2,4,128,128]{3,2,1,0:T(8,128)(2,1)} %get-tuple-element.12.pc), channel_id=1, source_target_pairs={{8,0},{16,8},{24,16},{32,24},{40,32},{48,40},{56,48},{64,56},{72,6... | collective-permute-start | bytes 786440 | tf_op jit(solution)/shard_map/ppermute | solution.py:23
  80.5 15.6 %collective-permute-start.8 = (bf16[2,8,128,128]{3,2,1,0:T(8,128)(2,1)S(1)}, bf16[2,8,128,128]{3,2,1,0:T(8,128)(2,1)S(1)}, u32[]{:S(2)}, u32[]{:S(2)}) collective-permute-start(bf16[2,8,128,128]{3,2,1,0:T(8,128)(2,1)S(1)} %copy_bitcast_fusion.3), channel_id=1, source_target_pairs={{0,0},{16,1},{32,2},{48,3},{64,4},{80,5},{96,6},{112,7},{8,8},{24,... | collective-permute-start | bytes 1572872 | tf_op jit(solution)/shard_map/ppermute | solution.py:352
  84.2 32.3 %copy-start.2 = (bf16[2,4,128,128]{3,2,1,0:T(8,128)(2,1)}, bf16[2,4,128,128]{3,2,1,0:T(8,128)(2,1)S(1)}, u32[]{:S(2)}) copy-start(bf16[2,4,128,128]{3,2,1,0:T(8,128)(2,1)S(1)} %collective-permute-done.4.pzl) | copy-start | bytes 786436
  86.4 30.1 %copy-start.3 = (bf16[2,4,128,128]{3,2,1,0:T(8,128)(2,1)}, bf16[2,4,128,128]{3,2,1,0:T(8,128)(2,1)S(1)}, u32[]{:S(2)}) copy-start(bf16[2,4,128,128]{3,2,1,0:T(8,128)(2,1)S(1)} %collective-permute-done.5.pzh) | copy-start | bytes 786436
  86.5 48.0 %collective-permute-start.7 = (bf16[6,2,128,128]{3,2,1,0:T(8,128)(2,1)S(1)}, bf16[6,2,128,128]{3,2,1,0:T(8,128)(2,1)S(1)}, u32[]{:S(2)}, u32[]{:S(2)}) collective-permute-start(bf16[6,2,128,128]{3,2,1,0:T(8,128)(2,1)S(1)} %get-tuple-element.26), channel_id=1, source_target_pairs={{1,0},{2,1},{3,2},{4,3},{5,4},{6,5},{7,6},{9,8},{10,9},{11,10},{12... | collective-permute-start | bytes 1179656 | tf_op jit(solution)/shard_map/ppermute | solution.py:23
  87.8 46.7 %collective-permute-start.6 = (bf16[6,2,128,128]{3,2,1,0:T(8,128)(2,1)S(1)}, bf16[6,2,128,128]{3,2,1,0:T(8,128)(2,1)}, u32[]{:S(2)}, u32[]{:S(2)}) collective-permute-start(bf16[6,2,128,128]{3,2,1,0:T(8,128)(2,1)S(1)} %get-tuple-element.27), channel_id=1, source_target_pairs={{0,1},{1,2},{2,3},{3,4},{4,5},{5,6},{6,7},{8,9},{9,10},{10,11},{11... | collective-permute-start | bytes 1179656 | tf_op jit(solution)/shard_map/ppermute | solution.py:22
  96.1 20.4 %copy-start.6 = (bf16[2,8,128,128]{3,2,1,0:T(8,128)(2,1)}, bf16[2,8,128,128]{3,2,1,0:T(8,128)(2,1)S(1)}, u32[]{:S(2)}) copy-start(bf16[2,8,128,128]{3,2,1,0:T(8,128)(2,1)S(1)} %collective-permute-done.8.cc) | copy-start | bytes 1572868
  96.1 23.5 %collective-permute-start.10 = (bf16[2,8,128,128]{3,2,1,0:T(8,128)(2,1)S(1)}, bf16[2,8,128,128]{3,2,1,0:T(8,128)(2,1)S(1)}, u32[]{:S(2)}, u32[]{:S(2)}) collective-permute-start(bf16[2,8,128,128]{3,2,1,0:T(8,128)(2,1)S(1)} %collective-permute-done.8.cc), channel_id=1, source_target_pairs={{8,0},{16,8},{24,16},{32,24},{40,32},{48,40},{56,48},{64,56},{72,6... | collective-permute-start | bytes 1572872 | tf_op jit(solution)/shard_map/ppermute | solution.py:23
  98.0 28.4 %collective-permute-start.9 = (bf16[2,8,128,128]{3,2,1,0:T(8,128)(2,1)S(1)}, bf16[2,8,128,128]{3,2,1,0:T(8,128)(2,1)S(1)}, u32[]{:S(2)}, u32[]{:S(2)}) collective-permute-start(bf16[2,8,128,128]{3,2,1,0:T(8,128)(2,1)S(1)} %collective-permute-done.8.cc), channel_id=1, source_target_pairs={{0,8},{8,16},{16,24},{24,32},{32,40},{40,48},{48,56},{56,64},{64,7... | collective-permute-start | bytes 1572872 | tf_op jit(solution)/shard_map/ppermute | solution.py:22
  119.6 6.8 %copy-start.7 = (bf16[2,8,128,128]{3,2,1,0:T(8,128)(2,1)}, bf16[2,8,128,128]{3,2,1,0:T(8,128)(2,1)S(1)}, u32[]{:S(2)}) copy-start(bf16[2,8,128,128]{3,2,1,0:T(8,128)(2,1)S(1)} %collective-permute-done.10.ch) | copy-start | bytes 1572868
  126.4 0.8 copy-start.8
  134.5 0.7 copy-start.9
  149.7 1.6 collective-permute-start.11
  152.0 29.4 %all-to-all-start.1 = ((bf16[16,8,8,128]{3,2,1,0:T(8,128)(2,1)}), bf16[16,8,8,128]{3,2,1,0:T(8,128)(2,1)S(1)}, u32[]{:S(2)}, u32[]{:S(2)}) async-start(bf16[16,8,8,128]{3,2,1,0:T(8,128)(2,1)} %bitcast.87), calls=%async_computation.1 | async-start | bytes 524288 | tf_op jit(solution)/shard_map/all_to_all | solution.py:358
  181.5 27.4 %all-to-all-start.4 = ((bf16[16,432,128]{2,1,0:T(8,128)(2,1)}), bf16[16,432,128]{2,1,0:T(8,128)(2,1)S(1)}, u32[]{:S(2)}, u32[]{:S(2)}) async-start(bf16[16,432,128]{2,1,0:T(8,128)(2,1)} %copy_bitcast_fusion), calls=%async_computation.4 | async-start | bytes 3538944 | tf_op jit(solution)/shard_map/all_to_all | solution.py:28
  208.9 20.6 %all-to-all-start.2 = ((bf16[128,16,128]{2,1,0:T(8,128)(2,1)}), bf16[128,16,128]{2,1,0:T(8,128)(2,1)S(1)}, u32[]{:S(2)}, u32[]{:S(2)}) async-start(bf16[128,16,128]{2,1,0:T(8,128)(2,1)} %bitcast.103), calls=%async_computation.2 | async-start | bytes 1048576 | tf_op jit(solution)/shard_map/all_to_all | solution.py:28
  229.5 10.1 %all-to-all-start.5 = ((bf16[8,64,128]{2,1,0:T(8,128)(2,1)}), bf16[8,64,128]{2,1,0:T(8,128)(2,1)S(1)}, u32[]{:S(2)}, u32[]{:S(2)}) async-start(bf16[8,64,128]{2,1,0:T(8,128)(2,1)} %bitcast.40), calls=%async_computation.5 | async-start | bytes 262144 | tf_op jit(solution)/shard_map/all_to_all | solution.py:28
  240.4 19.3 %all-to-all-start.3 = ((bf16[128,16,128]{2,1,0:T(8,128)(2,1)}), bf16[128,16,128]{2,1,0:T(8,128)(2,1)S(1)}, u32[]{:S(2)}, u32[]{:S(2)}) async-start(bf16[128,16,128]{2,1,0:T(8,128)(2,1)} %broadcast_in_dim.7), calls=%async_computation.3 | async-start | bytes 1048576 | tf_op jit(solution)/shard_map/all_to_all | solution.py:34
  260.3 10.1 %all-to-all-start.6 = ((bf16[8,64,128]{2,1,0:T(8,128)(2,1)}), bf16[8,64,128]{2,1,0:T(8,128)(2,1)S(1)}, u32[]{:S(2)}, u32[]{:S(2)}) async-start(bf16[8,64,128]{2,1,0:T(8,128)(2,1)} %broadcast_in_dim.8), calls=%async_computation.6 | async-start | bytes 262144 | tf_op jit(solution)/shard_map/all_to_all | solution.py:34
Sparse Core Ops, SparseCore 0:
  10.3 43.6 all-gather.1

commit v3 on v2

--- a/solution.py
+++ b/solution.py
@@ -7,13 +7,16 @@
 from jax.sharding import PartitionSpec as P
 
 leak_slope = 0.2
-both = ("sx", "sy")
 vmem_bytes = 56 * 1024 * 1024
 
 
-def swap_places(ways):
-    pairs = [(a * 8 + b, (2 * b + a % 2) * 8 + a // 2) for a in range(16) for b in range(8)]
-    return pairs if ways > 0 else [(there, here) for here, there in pairs]
+def partner_neighbours(first, last):
+    low = lax.axis_index("sx") % 2 == 0
+    near = lax.ppermute(jnp.where(low, last, first), "sx", [(i, i ^ 1) for i in range(16)])
+    far = lax.ppermute(
+        jnp.where(low, first, last), "sx", [(i, i - 1 + 2 * (i % 2)) for i in range(1, 15)]
+    )
+    return jnp.where(low, far, near), jnp.where(low, near, far)
 
 
 def neighbours(first, last, axis):
@@ -24,17 +27,25 @@
     )
 
 
-def sum_parts(parts, axis):
-    got = lax.all_to_all(parts.astype(jnp.bfloat16), axis, 0, 0, tiled=True)
-    return got.astype(jnp.float32).sum(0)
-
-
-def spread_part(part, axis, count):
-    part = part.astype(jnp.bfloat16)
-    got = lax.all_to_all(
-        jnp.broadcast_to(part[None], (count,) + part.shape), axis, 0, 0, tiled=True
-    )
-    return got.reshape((-1,) + part.shape[1:])
+def other_core(values):
+    return lax.ppermute(values, "sx", [(i, i ^ 1) for i in range(16)])
+
+
+def to_chips(parts):
+    groups = [list(range(0, 16, 2)), list(range(1, 16, 2))]
+    return lax.all_to_all(parts, "sx", 0, 0, axis_index_groups=groups, tiled=True)
+
+
+def to_sy(parts):
+    return lax.all_to_all(parts, "sy", 0, 0, tiled=True)
+
+
+def repeated(part):
+    return jnp.broadcast_to(part[None], (8,) + part.shape)
+
+
+def sum_first(parts):
+    return parts.astype(jnp.float32).sum(0)
 
 
 def dot(left, right):
@@ -211,12 +222,12 @@
             for c in range(3):
                 low = full[a * 128 : a * 128 + 128, c * 256 : c * 256 + 128]
                 high = full[a * 128 + 128 : a * 128 + 256, c * 256 + 128 : c * 256 + 256]
-                store(9 * a + 3 * b + c, (low + high).astype(jnp.bfloat16))
+                store(9 * a + 3 * b + c, low + high)
 
 
 def mid_body(
     pc, pzl, pzh, pyl, pyh, hidden_grad, cot3, k2, k3, flags,
-    output, grads, spg, cells, hidden, filters, total, spg3, turned,
+    maps, spg, cells, hidden, filters, total, spg3, turned,
 ):
     for z in range(6):
         lanes = slice(z * 128, z * 128 + 128)
@@ -246,8 +257,12 @@
             )
     turned[...] = hidden[...].reshape(768, 512).T
 
+    def store(place, value):
+        for i in range(16):
+            maps[i % 2, i // 2, place] = value[i * 8 : i * 8 + 8]
+
     def store_third(tap, value):
-        grads[27 + tap] = value
+        store(27 + tap, value)
 
     grad_taps(turned, cot3, store_third)
     for y in range(4):
@@ -259,23 +274,22 @@
     turned[...] = cells[1:7, :, 128:640].reshape(768, 512).T
 
     def store_second(tap, value):
-        grads[tap] = value.T
+        store(tap, value.T)
 
     grad_taps(turned, spg3, store_second)
     lay_filters(filters, lambda a, b, c: k3[9 * a + 3 * b + c], False)
     conv_rows(hidden, slice(0, 512), filters, total, 4)
     for y in range(4):
-        done = joined(total, y).astype(jnp.bfloat16)
+        done = joined(total, y)
         for z in range(2):
-            output[z, y] = done[:, z * 128 : z * 128 + 128].T
+            store(54 + z * 4 + y, done[:, z * 128 : z * 128 + 128].T)
 
 
 def mid_section(pc, pzl, pzh, pyl, pyh, hidden_grad, cot3, k2, k3, flags):
     return call(
         mid_body,
         [
-            ((2, 4, 128, 128), jnp.bfloat16),
-            ((54, 128, 128), jnp.bfloat16),
+            ((2, 8, 62, 8, 128), jnp.float32),
             ((6, 128, 512), jnp.bfloat16),
         ],
         [
@@ -323,15 +337,15 @@
                 even, odd = ((2, 0), (0, 1), (1, 3))[c]
                 low = full[a * 256 + even * 64 : a * 256 + even * 64 + 64, 0:128]
                 high = full[a * 256 + odd * 64 : a * 256 + odd * 64 + 64, 128:256]
-                tap = (9 * a + 3 * b + c) * 64
-                first[tap : tap + 64, :] = (low + high).astype(jnp.bfloat16)
-    first[1728:2048, :] = jnp.zeros((320, 128), jnp.bfloat16)
+                tap = 9 * a + 3 * b + c
+                first[tap // 16, tap % 16 * 64 : tap % 16 * 64 + 64, :] = low + high
+    first[1, 704:1024, :] = jnp.zeros((320, 128), jnp.float32)
 
 
 def last_section(spg, k2, xt, bits):
     return call(
         last_body,
-        [((2048, 128), jnp.bfloat16)],
+        [((2, 1024, 128), jnp.float32)],
         [
             ((3, 512, 768), jnp.bfloat16),
             ((768, 768), jnp.float32),
@@ -344,27 +358,23 @@
     )[0]
 
 
-def cot_to_cells(values):
-    wide = jnp.pad(values, ((0, 0), (2, 2), (0, 0), (0, 0)))
-    parts = jnp.stack([wide[:, 4 * k : 4 * k + 8] for k in range(8)])
-    parts = lax.all_to_all(parts.reshape(16, 2, 8, 8, 128), "sx", 0, 0, tiled=True)
-    cells = parts.transpose(1, 2, 0, 3, 4).reshape(2, 8, 128, 128)
-    return lax.ppermute(cells, both, swap_places(-1))
-
-
-def output_to_channels(values):
-    moved = lax.ppermute(values, both, swap_places(1))
-    parts = jnp.swapaxes(moved.reshape(8, 16, 8, 128), 0, 1)
-    parts = lax.all_to_all(parts, "sx", 0, 0, tiled=True)
-    parts = parts.reshape(8, 2, 2, 4, 8, 128).transpose(1, 2, 0, 3, 4, 5)
-    return parts.reshape(4, 32, 8, 128)
+def cot_rows(values):
+    own = values.reshape(4, 8, 4, 8, 128)
+    below = jnp.pad(own[:, :7, 2:], ((0, 0), (1, 0), (0, 0), (0, 0), (0, 0)))
+    above = jnp.pad(own[:, 1:, :2], ((0, 0), (0, 1), (0, 0), (0, 0), (0, 0)))
+    return jnp.swapaxes(jnp.concatenate([below, own, above], axis=2), 0, 1)
+
+
+def after(values, *done):
+    return lax.optimization_barrier((values,) + done)[0]
 
 
 def on_device(volume, first_kernel, second_kernel, third_kernel, cotangent):
     sx, sy = lax.axis_index("sx"), lax.axis_index("sy")
+    core = sx % 2
     flags = jnp.stack([sx > 0, sx < 15, sy > 0, sy < 7]).astype(jnp.float32)
     vc = jnp.swapaxes(volume, 2, 3)
-    vzl, vzh = neighbours(vc[:1], vc[-1:], "sx")
+    vzl, vzh = partner_neighbours(vc[:1], vc[-1:])
     deep = lambda y: jnp.concatenate([vzl[:, y : y + 1], vc[:, y : y + 1], vzh[:, y : y + 1]])
     vyl, vyh = neighbours(deep(0), deep(7), "sy")
     shares = jnp.concatenate(
@@ -373,25 +383,56 @@
     filters = lax.all_gather(shares, "sx", axis=0, tiled=True).reshape(16, 54, 8, 128)
     filters = filters.swapaxes(0, 1).reshape(54, 128, 128)
     k2, k3 = filters[:27], filters[27:]
-    cc = cot_to_cells(jnp.swapaxes(cotangent, 2, 3))
-    cl, ch = neighbours(cc, cc, "sx")
-    pooled, bits, xt = first_section(vc, vzl, vzh, vyl, vyh, pair_filters(first_kernel))
+    cot_tall = to_sy(after(cot_rows(jnp.swapaxes(cotangent, 2, 3)), vzl, vzh))
+    cot_parts = lax.all_to_all(cot_tall.reshape(16, 2, 8, 8, 128), "sx", 0, 0, tiled=True)
+    cc = cot_parts.transpose(1, 2, 0, 3, 4).reshape(2, 8, 128, 128)
+    cl, ch = partner_neighbours(cc, cc)
+    w1 = after(pair_filters(first_kernel), cot_tall)
+    pooled, bits, xt = first_section(vc, vzl, vzh, vyl, vyh, w1)
     hidden_grad, cot3 = cot_section(cc, cl, ch, k3)
-    pzl, pzh = neighbours(pooled, pooled, "sx")
+    pzl, pzh = partner_neighbours(pooled, pooled)
     tall = jnp.concatenate([pzl, pooled, pzh])
     pyl, pyh = neighbours(tall[:, :2], tall[:, 2:], "sy")
-    output, grads, spg = mid_section(
-        pooled, pzl, pzh, pyl, pyh, hidden_grad, cot3, k2, k3, flags
-    )
+    maps, spg = mid_section(pooled, pzl, pzh, pyl, pyh, hidden_grad, cot3, k2, k3, flags)
+    from_other = other_core(maps[1 - core].astype(jnp.bfloat16))
+    own = maps[core]
     first_part = last_section(spg, k2, xt, bits)
-    output = jnp.swapaxes(output_to_channels(output), 2, 3)
-    share = sum_parts(grads.reshape(54, 16, 8, 128).swapaxes(0, 1).reshape(16, 432, 128), "sx")
-    share = sum_parts(jnp.pad(share, ((0, 80), (0, 0))).reshape(8, 64, 128), "sy")
-    share = spread_part(share, "sy", 8)[:432].astype(jnp.float32).reshape(2, 3, 3, 3, 8, 128)
-    second_grad, third_grad = jnp.swapaxes(share[0], 3, 4), share[1]
-    first_sum = spread_part(sum_parts(first_part.reshape(128, 16, 128), both), both, 128)
-    first_grad = first_sum[:1728].astype(jnp.float32).reshape(3, 3, 3, 64, 128)
-    return (output, first_grad, second_grad, third_grad)
+    first_from = other_core(first_part[1 - core].astype(jnp.bfloat16))
+    first_half = first_part[core] + first_from.astype(jnp.float32)
+    grads = own[:, :54] + from_other[:, :54].astype(jnp.float32)
+    mine, theirs = own[:, 54:].astype(jnp.bfloat16), from_other[:, 54:]
+    parts = jnp.concatenate(
+        [
+            grads.astype(jnp.bfloat16),
+            jnp.where(core == 0, mine, theirs),
+            jnp.where(core == 0, theirs, mine),
+            first_half.astype(jnp.bfloat16).reshape(8, 16, 8, 128),
+        ],
+        axis=1,
+    )
+    parts = to_chips(parts)
+    grads = jnp.pad(sum_first(parts[:, :54]), ((0, 2), (0, 0), (0, 0)))
+    first_half = sum_first(parts[:, 70:])
+    parts = jnp.concatenate(
+        [
+            grads.astype(jnp.bfloat16).reshape(8, 7, 8, 128),
+            first_half.astype(jnp.bfloat16).reshape(8, 2, 8, 128),
+            parts[:, 54:70],
+        ],
+        axis=1,
+    )
+    parts = to_sy(parts)
+    output = parts[:, 9:].reshape(8, 4, 4, 8, 128).swapaxes(0, 1).reshape(4, 32, 8, 128)
+    share = to_sy(repeated(sum_first(parts[:, :9]).astype(jnp.bfloat16)))
+    grads = share[:, :7].reshape(56, 8, 128)[:54].astype(jnp.float32)
+    grads = grads.reshape(2, 3, 3, 3, 8, 128)
+    half = to_chips(repeated(share[:, 7:].reshape(128, 128))).reshape(1024, 128)
+    other = other_core(half)
+    first_grad = jnp.concatenate(
+        [jnp.where(core == 0, half, other), jnp.where(core == 0, other, half)[:704]]
+    )
+    first_grad = first_grad.astype(jnp.float32).reshape(3, 3, 3, 64, 128)
+    return (jnp.swapaxes(output, 2, 3), first_grad, jnp.swapaxes(grads[0], 3, 4), grads[1])
 
 
 def solution(mesh):

time: 280 us -> 216 us (0.77)
  waiting for transfers between devices: 89.2 us -> 27 us
  blocking collectives: 0 us -> 57.7 us
  starting transfers between devices: 99.2 us -> 48.1 us
  local copies, waits for them, and re-layouts: 26.2 us -> 15.5 us
    all_to_all x0 -> x3, blocking collectives: none -> 57.7 us  [the longest x1 30.6 us: to_chips(): lax.all_to_all(parts, 'sx', 0, 0, axis_index_groups=groups, tiled=True)]
    all_to_all x7 -> x3, waiting for transfers between devices: 55.5 us -> 7.03 us  [the longest x1 4.96 us: to_chips(): lax.all_to_all(parts, 'sx', 0, 0, axis_index_groups=groups, tiled=True)]
    all_to_all x7 -> x3, starting transfers between devices: 51.5 us -> 17 us  [the longest x1 7.21 us: to_sy(): return lax.all_to_all(parts, 'sy', 0, 0, tiled=True)]
    ppermute x5 -> x2, starting transfers between devices: 37 us -> 10.7 us  [neighbours(): lax.ppermute(last, axis, [(i, i + 1) for i in range(ends)])]
    ppermute x2 -> x9, waiting for transfers between devices: 0.01 us -> 18.7 us  [the longest x3 18.2 us: partner_neighbours(): lax.ppermute(jnp.where(low, first, last), 'sx', [(i, i - 1 + 2 * (i % 2))...]
    ppermute x5 -> x2, waiting for transfers between devices: 17.3 us -> 0.01 us  [neighbours(): lax.ppermute(first, axis, [(i + 1, i) for i in range(ends)])]
    ppermute x2 -> x9, starting transfers between devices: 2.29 us -> 17.6 us  [the longest x3 11.5 us: partner_neighbours(): lax.ppermute(jnp.where(low, first, last), 'sx', [(i, i - 1 + 2 * (i % 2))...]
    ppermute x5 -> x2, waiting for transfers between devices: 16.3 us -> 1.29 us  [neighbours(): lax.ppermute(last, axis, [(i, i + 1) for i in range(ends)])]
  transfers between devices with their start and end apart: 20 -> 17, of which waited for: 13 -> 7; matrix products, arithmetic and copies ran while one was open for 9% -> 7% of each run, Pallas kernels for 11% -> 14%
where the time goes in v3:
time: 216 us; the launch traced here: 215 us
  blocking collectives  57.7 us (27%)
  starting transfers between devices  48.1 us (22%)
  Pallas kernels  44.9 us (21%)
  waiting for transfers between devices  27 us (12%)
  local copies, waits for them, and re-layouts  15.5 us (7%)
  between operations  14.5 us (7%)
  other arithmetic  7.64 us (4%)
    pallas_call x4, Pallas kernels, call(): pl.pallas_call(body, out_shape=[jax.ShapeDtypeStruct(shape, kind) for sha...  44.9 us
    all_to_all x1, blocking collectives, to_chips(): lax.all_to_all(parts, 'sx', 0, 0, axis_index_groups=groups, tiled=True)  30.6 us
    all_to_all x2, blocking collectives, to_sy(): return lax.all_to_all(parts, 'sy', 0, 0, tiled=True)  27.1 us
    ppermute x3, waiting for transfers between devices, partner_neighbours(): lax.ppermute(jnp.where(low, first, last), 'sx', [(i, i - 1 + 2 * (i % 2))...  18.2 us
    ppermute x3, starting transfers between devices, partner_neighbours(): lax.ppermute(jnp.where(low, first, last), 'sx', [(i, i - 1 + 2 * (i % 2))...  11.5 us
    ppermute x2, starting transfers between devices, neighbours(): lax.ppermute(last, axis, [(i, i + 1) for i in range(ends)])  10.7 us
    all_to_all x1, starting transfers between devices, to_sy(): return lax.all_to_all(parts, 'sy', 0, 0, tiled=True)  7.21 us
    all_to_all x1, starting transfers between devices, on_device(): lax.all_to_all(cot_tall.reshape(16, 2, 8, 8, 128), 'sx', 0, 0, tiled=True)  6.36 us
  transfers between devices with their start and end apart: 17, of which 7 were waited for; matrix products, arithmetic and copies ran while one was open for 7% of the time, Pallas kernels for 14%

profile of v3, /device:TPU:1, one launch (start us, length us, event | category | flops | bytes accessed | tf_op | source)
XLA Modules:
  0.0 215.4 jit_solution(12141270849369959677)
XLA Ops:
  7.2 1.1 broadcast_select_fusion.7
  8.4 4.9 %collective-permute-start = (bf16[1,8,64,256]{3,2,1,0:T(8,128)(2,1)S(1)}, bf16[1,8,64,256]{3,2,1,0:T(8,128)(2,1)S(1)}, u32[]{:S(2)}, u32[]{:S(2)}) collective-permute-start(bf16[1,8,64,256]{3,2,1,0:T(8,128)(2,1)S(1)} %get-tuple-element.33), channel_id=1, source_target_pairs={{8,16},{16,8},{24,32},{32,24},{40,48},{48,40},{56,64},{64,56},{72,... | collective-permute-start | bytes 786440 | tf_op jit(solution)/shard_map/ppermute | solution.py:16
  13.4 1.5 pad_maximum_fusion.6
  17.1 2.3 %collective-permute-done = bf16[1,8,64,256]{3,2,1,0:T(8,128)(2,1)S(1)} collective-permute-done((bf16[1,8,64,256]{3,2,1,0:T(8,128)(2,1)S(1)}, bf16[1,8,64,256]{3,2,1,0:T(8,128)(2,1)S(1)}, u32[]{:S(2)}, u32[]{:S(2)}) %collective-permute-start) | collective-permute-done | bytes 262176 | tf_op jit(solution)/shard_map/ppermute | solution.py:16
  20.4 7.2 %all-to-all-start = ((bf16[8,4,8,8,128]{4,3,2,1,0:T(8,128)(2,1)}), bf16[8,4,8,8,128]{4,3,2,1,0:T(8,128)(2,1)}, u32[]{:S(2)}, u32[]{:S(2)}) async-start(bf16[8,4,8,8,128]{4,3,2,1,0:T(8,128)(2,1)} %copy.24), calls=%async_computation | async-start | bytes 1048576 | tf_op jit(solution)/shard_map/all_to_all | solution.py:40
  27.7 1.3 collective-permute-start.3
  29.0 5.5 %collective-permute-start.2 = (bf16[6,1,64,256]{3,2,1,0:T(8,128)(2,1)S(1)}, bf16[6,1,64,256]{3,2,1,0:T(8,128)(2,1)S(1)}, u32[]{:S(2)}, u32[]{:S(2)}) collective-permute-start(bf16[6,1,64,256]{3,2,1,0:T(8,128)(2,1)S(1)} %pad_maximum_fusion.4), channel_id=1, source_target_pairs={{0,1},{1,2},{2,3},{3,4},{4,5},{5,6},{6,7},{8,9},{9,10},{10,11},{11... | collective-permute-start | bytes 589832 | tf_op jit(solution)/shard_map/ppermute | solution.py:25
  34.6 1.2 maximum_maximum_fusion.w1
  35.7 2.1 all-to-all-done
  37.8 6.4 %all-to-all-start.1 = ((bf16[16,2,8,8,128]{4,3,2,1,0:T(8,128)(2,1)}), bf16[16,2,8,8,128]{4,3,2,1,0:T(8,128)(2,1)S(1)}, u32[]{:S(2)}, u32[]{:S(2)}) async-start(bf16[16,2,8,8,128]{4,3,2,1,0:T(8,128)(2,1)} %bitcast.9), calls=%async_computation.1 | async-start | bytes 1048576 | tf_op jit(solution)/shard_map/all_to_all | solution.py:387
  44.2 1.3 collective-permute-done.2.vyl
  46.2 11.4 %first.1 = (bf16[2,4,128,128]{3,2,1,0:T(8,128)(2,1)}, s32[2,4,128,128]{3,2,1,0:T(8,128)}, bf16[6,256,1280]{2,1,0:T(8,128)(2,1)}) custom-call(bf16[4,8,64,256]{3,2,1,0:T(8,128)(2,1)} %bitcast.80, bf16[1,8,64,256]{3,2,1,0:T(8,128)(2,1)} %copy-done.7, bf16[1,8,64,256]{3,2,1,0:T(8,128)(2,1)} %copy-done.6, bf16[6,1,64,256]{3,2,1,0:T(8,128)(2,1)} %copy-done.12, ...), custom_call_target="tpu_custom_call" | custom-call | flops 5000000000 | bytes 8126464 | tf_op jit(solution)/shard_map/first/pallas_call | solution.py:71
  57.6 4.4 %collective-permute-start.4 = (bf16[2,4,128,128]{3,2,1,0:T(8,128)(2,1)}, bf16[2,4,128,128]{3,2,1,0:T(8,128)(2,1)S(1)}, u32[]{:S(2)}, u32[]{:S(2)}) collective-permute-start(bf16[2,4,128,128]{3,2,1,0:T(8,128)(2,1)} %get-tuple-element.15.pc), channel_id=1, source_target_pairs={{8,16},{16,8},{24,32},{32,24},{40,48},{48,40},{56,64},{64,56},{72,... | collective-permute-start | bytes 786440 | tf_op jit(solution)/shard_map/ppermute | solution.py:16
  62.9 2.1 collective-permute-start.8
  65.1 9.9 %collective-permute-done.4 = bf16[2,4,128,128]{3,2,1,0:T(8,128)(2,1)S(1)} collective-permute-done((bf16[2,4,128,128]{3,2,1,0:T(8,128)(2,1)}, bf16[2,4,128,128]{3,2,1,0:T(8,128)(2,1)S(1)}, u32[]{:S(2)}, u32[]{:S(2)}) %collective-permute-start.4) | collective-permute-done | bytes 262176 | tf_op jit(solution)/shard_map/ppermute | solution.py:16
  75.3 5.2 %collective-permute-start.6 = (bf16[6,2,128,128]{3,2,1,0:T(8,128)(2,1)S(1)}, bf16[6,2,128,128]{3,2,1,0:T(8,128)(2,1)S(1)}, u32[]{:S(2)}, u32[]{:S(2)}) collective-permute-start(bf16[6,2,128,128]{3,2,1,0:T(8,128)(2,1)S(1)} %get-tuple-element.35), channel_id=1, source_target_pairs={{0,1},{1,2},{2,3},{3,4},{4,5},{5,6},{6,7},{8,9},{9,10},{10,11},{11... | collective-permute-start | bytes 1179656 | tf_op jit(solution)/shard_map/ppermute | solution.py:25
  80.6 1.5 collective-permute-start.7
  82.0 6.0 %collective-permute-done.8 = bf16[2,8,128,128]{3,2,1,0:T(8,128)(2,1)S(1)} collective-permute-done((bf16[2,8,128,128]{3,2,1,0:T(8,128)(2,1)S(1)}, bf16[2,8,128,128]{3,2,1,0:T(8,128)(2,1)S(1)}, u32[]{:S(2)}, u32[]{:S(2)}) %collective-permute-start.8) | collective-permute-done | bytes 524320 | tf_op jit(solution)/shard_map/ppermute | solution.py:16
  89.1 1.6 fusion.9
  90.6 1.2 copy.33
  91.8 1.2 copy.32
  93.0 7.3 %cot.1 = (f32[6,128,512]{2,1,0:T(8,128)}, bf16[512,768]{1,0:T(8,128)(2,1)}) custom-call(bf16[2,8,128,128]{3,2,1,0:T(8,128)(2,1)} %copy-done.4, bf16[2,8,128,128]{3,2,1,0:T(8,128)(2,1)} %get-tuple-element.29.cl, bf16[2,8,128,128]{3,2,1,0:T(8,128)(2,1)} %get-tuple-element.28.ch, bf16[27,128,128]{2,1,0:T(8,128)(2,1)} %bitcast.76), custom_call_target="tpu_custom_call" | custom-call | flops 3600000000 | bytes 4816896 | tf_op jit(solution)/shard_map/cot/pallas_call | solution.py:71
  101.1 14.9 %mid.1 = (f32[2,8,62,8,128]{4,3,2,1,0:T(8,128)}, bf16[6,128,512]{2,1,0:T(8,128)(2,1)}) custom-call(bf16[2,4,128,128]{3,2,1,0:T(8,128)(2,1)} %get-tuple-element.15.pc, bf16[2,4,128,128]{3,2,1,0:T(8,128)(2,1)} %copy-done.1, bf16[2,4,128,128]{3,2,1,0:T(8,128)(2,1)} %copy-done, bf16[6,2,128,128]{3,2,1,0:T(8,128)(2,1)} %copy-done.9, ...), custom_call_target="tpu_custom_call" | custom-call | flops 7000000000 | bytes 10551312 | tf_op jit(solution)/shard_map/mid/pallas_call | solution.py:71
  116.0 1.7 fusion.3
  117.8 11.3 %last.1 = f32[2,1024,128]{2,1,0:T(8,128)} custom-call(bf16[6,128,512]{2,1,0:T(8,128)(2,1)} %get-tuple-element.19.spg, bf16[27,128,128]{2,1,0:T(8,128)(2,1)} %bitcast.75, bf16[6,256,1280]{2,1,0:T(8,128)(2,1)} %get-tuple-element.20.xt, s32[2,4,128,128]{3,2,1,0:T(8,128)} %get-tuple-element.21.bits), custom_call_target="tpu_custom_call" | custom-call | flops 6000000000 | bytes 7176192 | tf_op jit(solution)/shard_map/last/pallas_call | solution.py:71
  130.8 1.8 dynamic-slice_bitcast_fusion
  133.2 30.6 %all_to_all.30 = bf16[8,86,8,128]{3,2,1,0:T(8,128)(2,1)S(1)} all-to-all(bf16[8,86,8,128]{3,2,1,0:T(8,128)(2,1)S(1)} %pad_maximum_fusion), channel_id=1, replica_groups={{0,16,32,48,64,80,96,112},{8,24,40,56,72,88,104,120},{1,17,33,49,65,81,..., dimensions={0} | all-to-all | bytes 2818048 | tf_op jit(solution)/shard_map/all_to_all | solution.py:36
  164.0 17.9 %all_to_all.31 = bf16[8,25,8,128]{3,2,1,0:T(8,128)(2,1)S(1)} all-to-all(bf16[8,25,8,128]{3,2,1,0:T(8,128)(2,1)S(1)} %pad_maximum_fusion.3), channel_id=1, replica_groups=mesh['sx'=16,'sy'=8] {'sy'}, dimensions={0} | all-to-all | bytes 819200 | tf_op jit(solution)/shard_map/all_to_all | solution.py:40
  182.0 9.2 %all_to_all.32 = bf16[8,9,8,128]{3,2,1,0:T(8,128)(2,1)S(1)} all-to-all(bf16[8,9,8,128]{3,2,1,0:T(8,128)(2,1)S(1)} %broadcast_in_dim.17), channel_id=1, replica_groups=mesh['sx'=16,'sy'=8] {'sy'}, dimensions={0} | all-to-all | bytes 294912 | tf_op jit(solution)/shard_map/all_to_all | solution.py:40
  191.9 3.4 %all-to-all-start.5 = ((bf16[8,128,128]{2,1,0:T(8,128)(2,1)}), bf16[8,128,128]{2,1,0:T(8,128)(2,1)S(1)}, u32[]{:S(2)}, u32[]{:S(2)}) async-start(bf16[8,128,128]{2,1,0:T(8,128)(2,1)} %broadcast_in_dim.19), calls=%async_computation.5 | async-start | bytes 524288 | tf_op jit(solution)/shard_map/all_to_all | solution.py:36
  196.1 5.0 %all-to-all-done.5 = bf16[8,128,128]{2,1,0:T(8,128)(2,1)S(1)} async-done(((bf16[8,128,128]{2,1,0:T(8,128)(2,1)}), bf16[8,128,128]{2,1,0:T(8,128)(2,1)S(1)}, u32[]{:S(2)}, u32[]{:S(2)}) %all-to-all-start.5) | async-done | bytes 262176 | tf_op jit(solution)/shard_map/all_to_all | solution.py:36
  201.1 5.2 %collective-permute-start.12 = (bf16[1024,128]{1,0:T(8,128)(2,1)S(1)}, bf16[1024,128]{1,0:T(8,128)(2,1)S(1)}, u32[]{:S(2)}, u32[]{:S(2)}) collective-permute-start(bf16[1024,128]{1,0:T(8,128)(2,1)S(1)} %bitcast.65), channel_id=1, source_target_pairs={{0,8},{8,0},{16,24},{24,16},{32,40},{40,32},{48,56},{56,48},{64,72... | collective-permute-start | bytes 786440 | tf_op jit(solution)/shard_map/ppermute | solution.py:31
  (83 shorter events, 13.4 us)
Async XLA Ops:
  7.2 9.7 %copy-start.2 = (bf16[4,32,128,8]{2,3,1,0:T(8,128)(2,1)S(1)}, bf16[4,32,128,8]{2,3,1,0:T(8,128)(2,1)}, u32[]{:S(2)}) copy-start(bf16[4,32,128,8]{2,3,1,0:T(8,128)(2,1)} %param.10) | copy-start | bytes 786436
  7.2 9.8 %copy-start.5 = (bf16[3,3,3,64,128]{4,3,2,1,0:T(8,128)(2,1)S(1)}, bf16[3,3,3,64,128]{4,3,2,1,0:T(8,128)(2,1)}, u32[]{:S(2)}) copy-start(bf16[3,3,3,64,128]{4,3,2,1,0:T(8,128)(2,1)} %param.7) | copy-start | bytes 1327108
  7.2 81.9 %all-gather.2.cloned.1.call-start = ((), (), s32[]{:S(2)}) async-start(), calls=%async_computation.6 | async-start | bytes 1880064 | tf_op jit(solution)/shard_map/all_gather | solution.py:383
  8.4 11.0 %collective-permute-start = (bf16[1,8,64,256]{3,2,1,0:T(8,128)(2,1)S(1)}, bf16[1,8,64,256]{3,2,1,0:T(8,128)(2,1)S(1)}, u32[]{:S(2)}, u32[]{:S(2)}) collective-permute-start(bf16[1,8,64,256]{3,2,1,0:T(8,128)(2,1)S(1)} %get-tuple-element.33), channel_id=1, source_target_pairs={{8,16},{16,8},{24,32},{32,24},{40,48},{48,40},{56,64},{64,56},{72,... | collective-permute-start | bytes 786440 | tf_op jit(solution)/shard_map/ppermute | solution.py:16
  13.3 6.1 %collective-permute-start.1 = (bf16[1,8,64,256]{3,2,1,0:T(8,128)(2,1)S(1)}, bf16[1,8,64,256]{3,2,1,0:T(8,128)(2,1)S(1)}, u32[]{:S(2)}, u32[]{:S(2)}) collective-permute-start(bf16[1,8,64,256]{3,2,1,0:T(8,128)(2,1)S(1)} %get-tuple-element.32), channel_id=1, source_target_pairs={{0,8},{8,0},{16,24},{24,16},{32,40},{40,32},{48,56},{56,48},{64,72... | collective-permute-start | bytes 786440 | tf_op jit(solution)/shard_map/ppermute | solution.py:15
  19.5 16.3 %copy-start.6 = (bf16[1,8,64,256]{3,2,1,0:T(8,128)(2,1)}, bf16[1,8,64,256]{3,2,1,0:T(8,128)(2,1)S(1)}, u32[]{:S(2)}) copy-start(bf16[1,8,64,256]{3,2,1,0:T(8,128)(2,1)S(1)} %get-tuple-element.38.vzh) | copy-start | bytes 786436
  19.5 16.3 %copy-start.7 = (bf16[1,8,64,256]{3,2,1,0:T(8,128)(2,1)}, bf16[1,8,64,256]{3,2,1,0:T(8,128)(2,1)S(1)}, u32[]{:S(2)}) copy-start(bf16[1,8,64,256]{3,2,1,0:T(8,128)(2,1)S(1)} %get-tuple-element.39.vzl) | copy-start | bytes 786436
  20.4 17.4 %all-to-all-start = ((bf16[8,4,8,8,128]{4,3,2,1,0:T(8,128)(2,1)}), bf16[8,4,8,8,128]{4,3,2,1,0:T(8,128)(2,1)}, u32[]{:S(2)}, u32[]{:S(2)}) async-start(bf16[8,4,8,8,128]{4,3,2,1,0:T(8,128)(2,1)} %copy.24), calls=%async_computation | async-start | bytes 1048576 | tf_op jit(solution)/shard_map/all_to_all | solution.py:40
  27.7 16.5 %collective-permute-start.3 = (bf16[6,1,64,256]{3,2,1,0:T(8,128)(2,1)S(1)}, bf16[6,1,64,256]{3,2,1,0:T(8,128)(2,1)S(1)}, u32[]{:S(2)}, u32[]{:S(2)}) collective-permute-start(bf16[6,1,64,256]{3,2,1,0:T(8,128)(2,1)S(1)} %pad_maximum_fusion.5), channel_id=1, source_target_pairs={{1,0},{2,1},{3,2},{4,3},{5,4},{6,5},{7,6},{9,8},{10,9},{11,10},{12... | collective-permute-start | bytes 589832 | tf_op jit(solution)/shard_map/ppermute | solution.py:26
  29.0 16.5 %collective-permute-start.2 = (bf16[6,1,64,256]{3,2,1,0:T(8,128)(2,1)S(1)}, bf16[6,1,64,256]{3,2,1,0:T(8,128)(2,1)S(1)}, u32[]{:S(2)}, u32[]{:S(2)}) collective-permute-start(bf16[6,1,64,256]{3,2,1,0:T(8,128)(2,1)S(1)} %pad_maximum_fusion.4), channel_id=1, source_target_pairs={{0,1},{1,2},{2,3},{3,4},{4,5},{5,6},{6,7},{8,9},{9,10},{10,11},{11... | collective-permute-start | bytes 589832 | tf_op jit(solution)/shard_map/ppermute | solution.py:25
  37.8 25.0 %all-to-all-start.1 = ((bf16[16,2,8,8,128]{4,3,2,1,0:T(8,128)(2,1)}), bf16[16,2,8,8,128]{4,3,2,1,0:T(8,128)(2,1)S(1)}, u32[]{:S(2)}, u32[]{:S(2)}) async-start(bf16[16,2,8,8,128]{4,3,2,1,0:T(8,128)(2,1)} %bitcast.9), calls=%async_computation.1 | async-start | bytes 1048576 | tf_op jit(solution)/shard_map/all_to_all | solution.py:387
  44.2 1.3 copy-start.11
  45.5 0.7 copy-start.12
  57.6 17.6 %copy-start.8 = (bf16[2,4,128,128]{3,2,1,0:T(8,128)(2,1)S(1)}, bf16[2,4,128,128]{3,2,1,0:T(8,128)(2,1)}, u32[]{:S(2)}) copy-start(bf16[2,4,128,128]{3,2,1,0:T(8,128)(2,1)} %get-tuple-element.15.pc) | copy-start | bytes 786436
  57.6 17.5 %collective-permute-start.4 = (bf16[2,4,128,128]{3,2,1,0:T(8,128)(2,1)}, bf16[2,4,128,128]{3,2,1,0:T(8,128)(2,1)S(1)}, u32[]{:S(2)}, u32[]{:S(2)}) collective-permute-start(bf16[2,4,128,128]{3,2,1,0:T(8,128)(2,1)} %get-tuple-element.15.pc), channel_id=1, source_target_pairs={{8,16},{16,8},{24,32},{32,24},{40,48},{48,40},{56,64},{64,56},{72,... | collective-permute-start | bytes 786440 | tf_op jit(solution)/shard_map/ppermute | solution.py:16
  62.0 13.0 %collective-permute-start.5 = (bf16[2,4,128,128]{3,2,1,0:T(8,128)(2,1)}, bf16[2,4,128,128]{3,2,1,0:T(8,128)(2,1)S(1)}, u32[]{:S(2)}, u32[]{:S(2)}) collective-permute-start(bf16[2,4,128,128]{3,2,1,0:T(8,128)(2,1)} %get-tuple-element.15.pc), channel_id=1, source_target_pairs={{0,8},{8,0},{16,24},{24,16},{32,40},{40,32},{48,56},{56,48},{64,72... | collective-permute-start | bytes 786440 | tf_op jit(solution)/shard_map/ppermute | solution.py:15
  62.9 12.4 %copy-start.4 = (bf16[2,8,128,128]{3,2,1,0:T(8,128)(2,1)}, bf16[2,8,128,128]{3,2,1,0:T(8,128)(2,1)S(1)}, u32[]{:S(2)}) copy-start(bf16[2,8,128,128]{3,2,1,0:T(8,128)(2,1)S(1)} %copy_bitcast_fusion.2.cc) | copy-start | bytes 1572868
  62.9 25.1 %collective-permute-start.8 = (bf16[2,8,128,128]{3,2,1,0:T(8,128)(2,1)S(1)}, bf16[2,8,128,128]{3,2,1,0:T(8,128)(2,1)S(1)}, u32[]{:S(2)}, u32[]{:S(2)}) collective-permute-start(bf16[2,8,128,128]{3,2,1,0:T(8,128)(2,1)S(1)} %copy_bitcast_fusion.2.cc), channel_id=1, source_target_pairs={{8,16},{16,8},{24,32},{32,24},{40,48},{48,40},{56,64},{64,56},{72,... | collective-permute-start | bytes 1572872 | tf_op jit(solution)/shard_map/ppermute | solution.py:16
  65.0 23.0 %collective-permute-start.9 = (bf16[2,8,128,128]{3,2,1,0:T(8,128)(2,1)S(1)}, bf16[2,8,128,128]{3,2,1,0:T(8,128)(2,1)S(1)}, u32[]{:S(2)}, u32[]{:S(2)}) collective-permute-start(bf16[2,8,128,128]{3,2,1,0:T(8,128)(2,1)S(1)} %copy_bitcast_fusion.2.cc), channel_id=1, source_target_pairs={{0,8},{8,0},{16,24},{24,16},{32,40},{40,32},{48,56},{56,48},{64,72... | collective-permute-start | bytes 1572872 | tf_op jit(solution)/shard_map/ppermute | solution.py:15
  75.1 14.0 %copy-start = (bf16[2,4,128,128]{3,2,1,0:T(8,128)(2,1)}, bf16[2,4,128,128]{3,2,1,0:T(8,128)(2,1)S(1)}, u32[]{:S(2)}) copy-start(bf16[2,4,128,128]{3,2,1,0:T(8,128)(2,1)S(1)} %get-tuple-element.36.pzh) | copy-start | bytes 786436
  75.1 13.9 %copy-start.1 = (bf16[2,4,128,128]{3,2,1,0:T(8,128)(2,1)}, bf16[2,4,128,128]{3,2,1,0:T(8,128)(2,1)S(1)}, u32[]{:S(2)}) copy-start(bf16[2,4,128,128]{3,2,1,0:T(8,128)(2,1)S(1)} %get-tuple-element.37.pzl) | copy-start | bytes 786436
  75.3 24.9 %collective-permute-start.6 = (bf16[6,2,128,128]{3,2,1,0:T(8,128)(2,1)S(1)}, bf16[6,2,128,128]{3,2,1,0:T(8,128)(2,1)S(1)}, u32[]{:S(2)}, u32[]{:S(2)}) collective-permute-start(bf16[6,2,128,128]{3,2,1,0:T(8,128)(2,1)S(1)} %get-tuple-element.35), channel_id=1, source_target_pairs={{0,1},{1,2},{2,3},{3,4},{4,5},{5,6},{6,7},{8,9},{9,10},{10,11},{11... | collective-permute-start | bytes 1179656 | tf_op jit(solution)/shard_map/ppermute | solution.py:25
  80.6 19.7 %collective-permute-start.7 = (bf16[6,2,128,128]{3,2,1,0:T(8,128)(2,1)S(1)}, bf16[6,2,128,128]{3,2,1,0:T(8,128)(2,1)S(1)}, u32[]{:S(2)}, u32[]{:S(2)}) collective-permute-start(bf16[6,2,128,128]{3,2,1,0:T(8,128)(2,1)S(1)} %get-tuple-element.34), channel_id=1, source_target_pairs={{1,0},{2,1},{3,2},{4,3},{5,4},{6,5},{7,6},{9,8},{10,9},{11,10},{12... | collective-permute-start | bytes 1179656 | tf_op jit(solution)/shard_map/ppermute | solution.py:26
  100.2 0.8 copy-start.9
  100.3 0.9 copy-start.10
  117.7 15.0 %collective-permute-start.10 = (bf16[8,62,8,128]{3,2,1,0:T(8,128)(2,1)S(1)}, bf16[8,62,8,128]{3,2,1,0:T(8,128)(2,1)S(1)}, u32[]{:S(2)}, u32[]{:S(2)}) collective-permute-start(bf16[8,62,8,128]{3,2,1,0:T(8,128)(2,1)S(1)} %fusion.3), channel_id=1, source_target_pairs={{0,8},{8,0},{16,24},{24,16},{32,40},{40,32},{48,56},{56,48},{64,72... | collective-permute-start | bytes 3047432 | tf_op jit(solution)/shard_map/ppermute | solution.py:31
  130.2 2.4 %collective-permute-start.11 = (bf16[1024,128]{1,0:T(8,128)(2,1)S(1)}, bf16[1024,128]{1,0:T(8,128)(2,1)S(1)}, u32[]{:S(2)}, u32[]{:S(2)}) collective-permute-start(bf16[1024,128]{1,0:T(8,128)(2,1)S(1)} %fusion.8), channel_id=1, source_target_pairs={{0,8},{8,0},{16,24},{24,16},{32,40},{40,32},{48,56},{56,48},{64,72... | collective-permute-start | bytes 786440 | tf_op jit(solution)/shard_map/ppermute | solution.py:31
  130.8 1.8 copy-start.3
  191.9 9.1 %all-to-all-start.5 = ((bf16[8,128,128]{2,1,0:T(8,128)(2,1)}), bf16[8,128,128]{2,1,0:T(8,128)(2,1)S(1)}, u32[]{:S(2)}, u32[]{:S(2)}) async-start(bf16[8,128,128]{2,1,0:T(8,128)(2,1)} %broadcast_in_dim.19), calls=%async_computation.5 | async-start | bytes 524288 | tf_op jit(solution)/shard_map/all_to_all | solution.py:36
  201.1 6.4 %collective-permute-start.12 = (bf16[1024,128]{1,0:T(8,128)(2,1)S(1)}, bf16[1024,128]{1,0:T(8,128)(2,1)S(1)}, u32[]{:S(2)}, u32[]{:S(2)}) collective-permute-start(bf16[1024,128]{1,0:T(8,128)(2,1)S(1)} %bitcast.65), channel_id=1, source_target_pairs={{0,8},{8,0},{16,24},{24,16},{32,40},{40,32},{48,56},{56,48},{64,72... | collective-permute-start | bytes 786440 | tf_op jit(solution)/shard_map/ppermute | solution.py:31
Sparse Core Ops, SparseCore 0:
  15.1 44.8 all-gather.1

commit v4 on v3

--- a/solution.py
+++ b/solution.py
@@ -7,7 +7,8 @@
 from jax.sharding import PartitionSpec as P
 
 leak_slope = 0.2
-vmem_bytes = 56 * 1024 * 1024
+same_core = [list(range(0, 16, 2)), list(range(1, 16, 2))]
+mib = 1024 * 1024
 
 
 def partner_neighbours(first, last):
@@ -16,7 +17,7 @@
     far = lax.ppermute(
         jnp.where(low, first, last), "sx", [(i, i - 1 + 2 * (i % 2)) for i in range(1, 15)]
     )
-    return jnp.where(low, far, near), jnp.where(low, near, far)
+    return jnp.where(low, far, near), jnp.where(low, near, far), near
 
 
 def neighbours(first, last, axis):
@@ -32,16 +33,15 @@
 
 
 def to_chips(parts):
-    groups = [list(range(0, 16, 2)), list(range(1, 16, 2))]
-    return lax.all_to_all(parts, "sx", 0, 0, axis_index_groups=groups, tiled=True)
+    return lax.all_to_all(parts, "sx", 0, 0, axis_index_groups=same_core, tiled=True)
 
 
 def to_sy(parts):
     return lax.all_to_all(parts, "sy", 0, 0, tiled=True)
 
 
-def repeated(part):
-    return jnp.broadcast_to(part[None], (8,) + part.shape)
+def repeated(part, count):
+    return jnp.broadcast_to(part[None], (count,) + part.shape)
 
 
 def sum_first(parts):
@@ -63,7 +63,7 @@
     return jnp.where(rows == count - 1, 0.0, pltpu.roll(values, count - 1, 0))
 
 
-def call(body, outs, scratch, operands, smem=0, flops=0, name=None):
+def call(body, outs, scratch, operands, smem=0, flops=0, vmem=24, name=None):
     size = sum(int(np.prod(a.shape)) * a.dtype.itemsize for a in operands)
     size += sum(int(np.prod(shape)) * jnp.dtype(kind).itemsize for shape, kind in outs)
     whole = pl.BlockSpec(memory_space=pltpu.VMEM)
@@ -74,7 +74,7 @@
         in_specs=specs,
         out_specs=[whole] * len(outs),
         scratch_shapes=[pltpu.VMEM(shape, kind) for shape, kind in scratch],
-        compiler_params=pltpu.CompilerParams(vmem_limit_bytes=vmem_bytes),
+        compiler_params=pltpu.CompilerParams(vmem_limit_bytes=vmem * mib),
         cost_estimate=pl.CostEstimate(flops=flops, bytes_accessed=size, transcendentals=0),
         name=name,
     )(*operands)
@@ -182,11 +182,16 @@
     )
 
 
-def cot_body(cc, cl, ch, k3, hidden_grad, cot3, cells, filters, total):
-    for z in range(6):
-        part = (cl, cc, ch)[z // 2]
+def cot_body(half, near, k3, core, hidden_grad, cot3, cells, filters, total):
+    first = core[0] * 2
+    for z in range(4):
         for y in range(8):
-            cells[y, :, z * 128 : z * 128 + 128] = part[z % 2, y].T
+            lanes = pl.ds(pl.multiple_of((first + z) * 128, 128), 128)
+            cells[y, :, lanes] = half[z, y].T
+    for z in range(2):
+        for y in range(8):
+            lanes = pl.ds(pl.multiple_of((4 - 2 * first + z) * 128, 128), 128)
+            cells[y, :, lanes] = near[z, y].T
     lay_filters(filters, lambda a, b, c: k3[(2 - a) * 9 + (2 - b) * 3 + 2 - c], True)
     for j in range(2):
         conv_rows(cells, slice(j * 256, j * 256 + 512), filters, total, 6)
@@ -200,7 +205,7 @@
         cot3[rows, 512:768] = row_before(own).astype(jnp.bfloat16)
 
 
-def cot_section(cc, cl, ch, k3):
+def cot_section(half, near, core, k3):
     return call(
         cot_body,
         [((6, 128, 512), jnp.float32), ((512, 768), jnp.bfloat16)],
@@ -209,7 +214,8 @@
             ((3, 512, 768), jnp.bfloat16),
             ((768, 768), jnp.float32),
         ],
-        [cc, cl, ch, k3],
+        [half, near, k3, core.reshape(1)],
+        smem=1,
         flops=3_600_000_000,
         name="cot",
     )
@@ -265,6 +271,8 @@
         store(27 + tap, value)
 
     grad_taps(turned, cot3, store_third)
+    store(54, jnp.zeros((128, 128), jnp.float32))
+    store(55, jnp.zeros((128, 128), jnp.float32))
     for y in range(4):
         own = spg[y + 1, :, 128:384].astype(jnp.float32)
         rows = slice(y * 128, y * 128 + 128)
@@ -282,14 +290,14 @@
     for y in range(4):
         done = joined(total, y)
         for z in range(2):
-            store(54 + z * 4 + y, done[:, z * 128 : z * 128 + 128].T)
+            store(56 + z * 4 + y, done[:, z * 128 : z * 128 + 128].T)
 
 
 def mid_section(pc, pzl, pzh, pyl, pyh, hidden_grad, cot3, k2, k3, flags):
     return call(
         mid_body,
         [
-            ((2, 8, 62, 8, 128), jnp.float32),
+            ((2, 8, 64, 8, 128), jnp.float32),
             ((6, 128, 512), jnp.bfloat16),
         ],
         [
@@ -303,6 +311,7 @@
         [pc, pzl, pzh, pyl, pyh, hidden_grad, cot3, k2, k3, flags],
         smem=1,
         flops=7_000_000_000,
+        vmem=32,
         name="mid",
     )
 
@@ -338,8 +347,11 @@
                 low = full[a * 256 + even * 64 : a * 256 + even * 64 + 64, 0:128]
                 high = full[a * 256 + odd * 64 : a * 256 + odd * 64 + 64, 128:256]
                 tap = 9 * a + 3 * b + c
-                first[tap // 16, tap % 16 * 64 : tap % 16 * 64 + 64, :] = low + high
-    first[1, 704:1024, :] = jnp.zeros((320, 128), jnp.float32)
+                row = tap // 4 * 128 + tap % 2 * 64
+                first[tap // 2 % 2, row : row + 64, :] = low + high
+    first[1, 832:1024, :] = jnp.zeros((192, 128), jnp.float32)
+    first[0, 960:1024, :] = jnp.zeros((64, 128), jnp.float32)
+    first[0, 896:960, :] = jnp.zeros((64, 128), jnp.float32)
 
 
 def last_section(spg, k2, xt, bits):
@@ -365,6 +377,12 @@
     return jnp.swapaxes(jnp.concatenate([below, own, above], axis=2), 0, 1)
 
 
+def cot_deep(values):
+    wide = jnp.pad(values.reshape(32, 8, 8, 128), ((2, 2), (0, 0), (0, 0), (0, 0)))
+    wide = wide.reshape(9, 4, 8, 8, 128)
+    return jnp.stack([wide[:8], wide[1:]], axis=1).reshape(16, 4, 8, 8, 128)
+
+
 def after(values, *done):
     return lax.optimization_barrier((values,) + done)[0]
 
@@ -373,34 +391,34 @@
     sx, sy = lax.axis_index("sx"), lax.axis_index("sy")
     core = sx % 2
     flags = jnp.stack([sx > 0, sx < 15, sy > 0, sy < 7]).astype(jnp.float32)
+    shares = jnp.concatenate(
+        [jnp.swapaxes(second_kernel, 3, 4).reshape(216, 128), third_kernel.reshape(216, 128)]
+    )
+    filters = lax.all_gather(shares, "sx", axis=0, tiled=True)
     vc = jnp.swapaxes(volume, 2, 3)
-    vzl, vzh = partner_neighbours(vc[:1], vc[-1:])
+    vzl, vzh, near = partner_neighbours(after(vc[:1], shares), vc[-1:])
     deep = lambda y: jnp.concatenate([vzl[:, y : y + 1], vc[:, y : y + 1], vzh[:, y : y + 1]])
     vyl, vyh = neighbours(deep(0), deep(7), "sy")
-    shares = jnp.concatenate(
-        [jnp.swapaxes(second_kernel, 3, 4).reshape(216, 128), third_kernel.reshape(216, 128)]
-    )
-    filters = lax.all_gather(shares, "sx", axis=0, tiled=True).reshape(16, 54, 8, 128)
-    filters = filters.swapaxes(0, 1).reshape(54, 128, 128)
-    k2, k3 = filters[:27], filters[27:]
-    cot_tall = to_sy(after(cot_rows(jnp.swapaxes(cotangent, 2, 3)), vzl, vzh))
-    cot_parts = lax.all_to_all(cot_tall.reshape(16, 2, 8, 8, 128), "sx", 0, 0, tiled=True)
-    cc = cot_parts.transpose(1, 2, 0, 3, 4).reshape(2, 8, 128, 128)
-    cl, ch = partner_neighbours(cc, cc)
+    cot_tall = to_sy(after(cot_rows(jnp.swapaxes(cotangent, 2, 3)), near))
+    cot_parts = lax.all_to_all(cot_deep(cot_tall), "sx", 0, 0, tiled=True)
+    cot_half = cot_parts.transpose(1, 2, 0, 3, 4).reshape(4, 8, 128, 128)
+    cot_near = other_core(jnp.where(core == 0, cot_half[2:], cot_half[:2]))
     w1 = after(pair_filters(first_kernel), cot_tall)
     pooled, bits, xt = first_section(vc, vzl, vzh, vyl, vyh, w1)
-    hidden_grad, cot3 = cot_section(cc, cl, ch, k3)
-    pzl, pzh = partner_neighbours(pooled, pooled)
+    pzl, pzh, _ = partner_neighbours(pooled, pooled)
+    filters = filters.reshape(16, 54, 8, 128).swapaxes(0, 1).reshape(54, 128, 128)
+    k2, k3 = filters[:27], filters[27:]
+    hidden_grad, cot3 = cot_section(cot_half, cot_near, core, k3)
     tall = jnp.concatenate([pzl, pooled, pzh])
     pyl, pyh = neighbours(tall[:, :2], tall[:, 2:], "sy")
     maps, spg = mid_section(pooled, pzl, pzh, pyl, pyh, hidden_grad, cot3, k2, k3, flags)
     from_other = other_core(maps[1 - core].astype(jnp.bfloat16))
     own = maps[core]
+    mine, theirs = own[:, 56:].astype(jnp.bfloat16), from_other[:, 56:]
     first_part = last_section(spg, k2, xt, bits)
     first_from = other_core(first_part[1 - core].astype(jnp.bfloat16))
     first_half = first_part[core] + first_from.astype(jnp.float32)
-    grads = own[:, :54] + from_other[:, :54].astype(jnp.float32)
-    mine, theirs = own[:, 54:].astype(jnp.bfloat16), from_other[:, 54:]
+    grads = own[:, :56] + from_other[:, :56].astype(jnp.float32)
     parts = jnp.concatenate(
         [
             grads.astype(jnp.bfloat16),
@@ -411,26 +429,21 @@
         axis=1,
     )
     parts = to_chips(parts)
-    grads = jnp.pad(sum_first(parts[:, :54]), ((0, 2), (0, 0), (0, 0)))
-    first_half = sum_first(parts[:, 70:])
     parts = jnp.concatenate(
         [
-            grads.astype(jnp.bfloat16).reshape(8, 7, 8, 128),
-            first_half.astype(jnp.bfloat16).reshape(8, 2, 8, 128),
-            parts[:, 54:70],
+            sum_first(parts[:, :56]).astype(jnp.bfloat16).reshape(8, 7, 8, 128),
+            sum_first(parts[:, 72:]).astype(jnp.bfloat16).reshape(8, 2, 8, 128),
+            parts[:, 56:72],
         ],
         axis=1,
     )
     parts = to_sy(parts)
     output = parts[:, 9:].reshape(8, 4, 4, 8, 128).swapaxes(0, 1).reshape(4, 32, 8, 128)
-    share = to_sy(repeated(sum_first(parts[:, :9]).astype(jnp.bfloat16)))
+    share = to_sy(repeated(sum_first(parts[:, :9]).astype(jnp.bfloat16), 8))
     grads = share[:, :7].reshape(56, 8, 128)[:54].astype(jnp.float32)
     grads = grads.reshape(2, 3, 3, 3, 8, 128)
-    half = to_chips(repeated(share[:, 7:].reshape(128, 128))).reshape(1024, 128)
-    other = other_core(half)
-    first_grad = jnp.concatenate(
-        [jnp.where(core == 0, half, other), jnp.where(core == 0, other, half)[:704]]
-    )
+    first_grad = repeated(share[:, 7:].reshape(128, 128), 16)
+    first_grad = lax.all_to_all(first_grad, "sx", 0, 0, tiled=True).reshape(2048, 128)[:1728]
     first_grad = first_grad.astype(jnp.float32).reshape(3, 3, 3, 64, 128)
     return (jnp.swapaxes(output, 2, 3), first_grad, jnp.swapaxes(grads[0], 3, 4), grads[1])
 

time: 216 us -> 194 us (0.90)
  Pallas kernels: 44.9 us -> 30.4 us
  starting transfers between devices: 48.1 us -> 41.4 us
  waiting for transfers between devices: 27 us -> 20.5 us
  local copies, waits for them, and re-layouts: 15.5 us -> 18.8 us
    pallas_call x4, Pallas kernels: 44.9 us -> 30.4 us  [call(): pl.pallas_call(body, out_shape=[jax.ShapeDtypeStruct(shape, kind) for sha...]
    ppermute x3 -> x2, waiting for transfers between devices: 18.2 us -> 7.56 us  [partner_neighbours(): lax.ppermute(jnp.where(low, first, last), 'sx', [(i, i - 1 + 2 * (i % 2))...]
    ppermute x3, starting transfers between devices: 5.88 us -> 0.17 us  [other_core(): return lax.ppermute(values, 'sx', [(i, i ^ 1) for i in range(16)])]
    ppermute x3 -> x2, starting transfers between devices: 11.5 us -> 7.05 us  [partner_neighbours(): lax.ppermute(jnp.where(low, first, last), 'sx', [(i, i - 1 + 2 * (i % 2))...]
    all_to_all x2, blocking collectives: 27.1 us -> 31.4 us  [to_sy(): return lax.all_to_all(parts, 'sy', 0, 0, tiled=True)]
    unnamed x27 -> x19, local copies, waits for them, and re-layouts: 1.67 us -> 5.81 us
    all_to_all x1, blocking collectives: 30.6 us -> 26.5 us  [to_chips(): lax.all_to_all(parts, 'sx', 0, 0, axis_index_groups=same_core, tiled=True)]
    all_to_all x2, starting transfers between devices: 9.77 us -> 13.3 us  [the longest x1 7.48 us: on_device(): lax.all_to_all(first_grad, 'sx', 0, 0, tiled=True).reshape(2048, 128)[:1728]]
  transfers between devices with their start and end apart: 17 -> 15, of which waited for: 7 -> 4; matrix products, arithmetic and copies ran while one was open for 7% -> 9% of each run, Pallas kernels for 14% -> 10%
where the time goes in v4:
time: 194 us; the launch traced here: 193 us
  blocking collectives  58 us (30%)
  starting transfers between devices  41.4 us (21%)
  Pallas kernels  30.4 us (16%)
  waiting for transfers between devices  20.5 us (11%)
  local copies, waits for them, and re-layouts  18.8 us (10%)
  between operations  14.5 us (7%)
  other arithmetic  9.43 us (5%)
    all_to_all x2, blocking collectives, to_sy(): return lax.all_to_all(parts, 'sy', 0, 0, tiled=True)  31.4 us
    pallas_call x4, Pallas kernels, call(): pl.pallas_call(body, out_shape=[jax.ShapeDtypeStruct(shape, kind) for sha...  30.4 us
    all_to_all x1, blocking collectives, to_chips(): lax.all_to_all(parts, 'sx', 0, 0, axis_index_groups=same_core, tiled=True)  26.5 us
    ppermute x2, starting transfers between devices, neighbours(): lax.ppermute(last, axis, [(i, i + 1) for i in range(ends)])  9.44 us
    all_to_all x1, waiting for transfers between devices, on_device(): lax.all_to_all(first_grad, 'sx', 0, 0, tiled=True).reshape(2048, 128)[:1728]  8.21 us
    ppermute x2, waiting for transfers between devices, partner_neighbours(): lax.ppermute(jnp.where(low, first, last), 'sx', [(i, i - 1 + 2 * (i % 2))...  7.56 us
    all_to_all x1, starting transfers between devices, on_device(): lax.all_to_all(first_grad, 'sx', 0, 0, tiled=True).reshape(2048, 128)[:1728]  7.48 us
    all_to_all x1, starting transfers between devices, to_sy(): return lax.all_to_all(parts, 'sy', 0, 0, tiled=True)  7.21 us
  transfers between devices with their start and end apart: 15, of which 4 were waited for; matrix products, arithmetic and copies ran while one was open for 9% of the time, Pallas kernels for 10%

profile of v4, /device:TPU:1, one launch (start us, length us, event | category | flops | bytes accessed | tf_op | source)
XLA Modules:
  0.0 193.0 jit_solution(5012840641807478746)
XLA Ops:
  7.2 1.6 pad_maximum_fusion.6
  9.8 1.0 broadcast_select_fusion.4
  10.8 1.5 collective-permute-start.1
  12.3 3.5 %collective-permute-start = (bf16[1,8,64,256]{3,2,1,0:T(8,128)(2,1)S(1)}, bf16[1,8,64,256]{3,2,1,0:T(8,128)(2,1)S(1)}, u32[]{:S(2)}, u32[]{:S(2)}) collective-permute-start(bf16[1,8,64,256]{3,2,1,0:T(8,128)(2,1)S(1)} %get-tuple-element.31), channel_id=1, source_target_pairs={{8,16},{16,8},{24,32},{32,24},{40,48},{48,40},{56,64},{64,56},{72,... | collective-permute-start | bytes 786440 | tf_op jit(solution)/shard_map/ppermute | solution.py:17
  18.0 7.2 %all-to-all-start = ((bf16[8,4,8,8,128]{4,3,2,1,0:T(8,128)(2,1)}), bf16[8,4,8,8,128]{4,3,2,1,0:T(8,128)(2,1)}, u32[]{:S(2)}, u32[]{:S(2)}) async-start(bf16[8,4,8,8,128]{4,3,2,1,0:T(8,128)(2,1)} %copy.25), calls=%async_computation | async-start | bytes 1048576 | tf_op jit(solution)/shard_map/all_to_all | solution.py:40
  26.0 1.3 collective-permute-start.3
  28.0 5.5 %collective-permute-start.2 = (bf16[6,1,64,256]{3,2,1,0:T(8,128)(2,1)}, bf16[6,1,64,256]{3,2,1,0:T(8,128)(2,1)S(1)}, u32[]{:S(2)}, u32[]{:S(2)}) collective-permute-start(bf16[6,1,64,256]{3,2,1,0:T(8,128)(2,1)} %pad_maximum_fusion.4), channel_id=1, source_target_pairs={{0,1},{1,2},{2,3},{3,4},{4,5},{5,6},{6,7},{8,9},{9,10},{10,11},{11... | collective-permute-start | bytes 589832 | tf_op jit(solution)/shard_map/ppermute | solution.py:26
  33.5 2.7 %all-to-all-done = bf16[8,4,8,8,128]{4,3,2,1,0:T(8,128)(2,1)} async-done(((bf16[8,4,8,8,128]{4,3,2,1,0:T(8,128)(2,1)}), bf16[8,4,8,8,128]{4,3,2,1,0:T(8,128)(2,1)}, u32[]{:S(2)}, u32[]{:S(2)}) %all-to-all-start) | async-done | bytes 524320 | tf_op jit(solution)/shard_map/all_to_all | solution.py:40
  36.2 1.3 pad_slice_fusion.1
  37.6 1.1 copy.26
  38.7 5.8 %all-to-all-start.1 = ((bf16[16,4,8,8,128]{4,3,2,1,0:T(8,128)(2,1)}), bf16[16,4,8,8,128]{4,3,2,1,0:T(8,128)(2,1)}, u32[]{:S(2)}, u32[]{:S(2)}) async-start(bf16[16,4,8,8,128]{4,3,2,1,0:T(8,128)(2,1)} %bitcast.78), calls=%async_computation.1 | async-start | bytes 2097152 | tf_op jit(solution)/shard_map/all_to_all | solution.py:403
  45.4 7.3 %first.1 = (bf16[2,4,128,128]{3,2,1,0:T(8,128)(2,1)S(1)}, s32[2,4,128,128]{3,2,1,0:T(8,128)S(1)}, bf16[6,256,1280]{2,1,0:T(8,128)(2,1)S(1)}) custom-call(bf16[4,8,64,256]{3,2,1,0:T(8,128)(2,1)S(1)} %bitcast.77, bf16[1,8,64,256]{3,2,1,0:T(8,128)(2,1)S(1)} %get-tuple-element.41.vzl, bf16[1,8,64,256]{3,2,1,0:T(8,128)(2,1)S(1)} %get-tuple-element.40.vzh, ...), custom_call_target="tpu_custom_call" | custom-call | flops 5000000000 | bytes 8126464 | tf_op jit(solution)/shard_map/first/pallas_call | solution.py:71
  52.7 1.9 copy-done.3
  55.5 3.5 %collective-permute-start.4 = (bf16[2,4,128,128]{3,2,1,0:T(8,128)(2,1)S(1)}, bf16[2,4,128,128]{3,2,1,0:T(8,128)(2,1)S(1)}, u32[]{:S(2)}, u32[]{:S(2)}) collective-permute-start(bf16[2,4,128,128]{3,2,1,0:T(8,128)(2,1)S(1)} %get-tuple-element.17.pc), channel_id=1, source_target_pairs={{8,16},{16,8},{24,32},{32,24},{40,48},{48,40},{56,64},{64,56},{72,... | collective-permute-start | bytes 786440 | tf_op jit(solution)/shard_map/ppermute | solution.py:17
  59.2 7.6 %collective-permute-done.4 = bf16[2,4,128,128]{3,2,1,0:T(8,128)(2,1)S(1)} collective-permute-done((bf16[2,4,128,128]{3,2,1,0:T(8,128)(2,1)S(1)}, bf16[2,4,128,128]{3,2,1,0:T(8,128)(2,1)S(1)}, u32[]{:S(2)}, u32[]{:S(2)}) %collective-permute-start.4) | collective-permute-done | bytes 262176 | tf_op jit(solution)/shard_map/ppermute | solution.py:17
  67.8 4.0 %collective-permute-start.6 = (bf16[6,2,128,128]{3,2,1,0:T(8,128)(2,1)}, bf16[6,2,128,128]{3,2,1,0:T(8,128)(2,1)S(1)}, u32[]{:S(2)}, u32[]{:S(2)}) collective-permute-start(bf16[6,2,128,128]{3,2,1,0:T(8,128)(2,1)} %get-tuple-element.35), channel_id=1, source_target_pairs={{0,1},{1,2},{2,3},{3,4},{4,5},{5,6},{6,7},{8,9},{9,10},{10,11},{11... | collective-permute-start | bytes 1179656 | tf_op jit(solution)/shard_map/ppermute | solution.py:26
  71.7 1.3 collective-permute-start.7
  73.0 2.2 %copy_bitcast_fusion.3 = bf16[2,8,128,128]{3,2,1,0:T(8,128)(2,1)} fusion(bf16[4,8,16,8,128]{4,3,1,0,2:T(8,128)(2,1)} %bitcast.16, pred[]{:T(512)S(6)} %eq.6), kind=kLoop, calls=%fused_computation.25 | loop fusion | flops 262144 | bytes 1572865 | tf_op jit(solution)/shard_map/jit(_where)/select_n | solution.py:405
  75.2 1.5 copy_bitcast_fusion.half
  76.7 1.6 fusion.9
  78.8 4.7 %cot.1 = (f32[6,128,512]{2,1,0:T(8,128)S(1)}, bf16[512,768]{1,0:T(8,128)(2,1)S(1)}) custom-call(bf16[4,8,128,128]{3,2,1,0:T(8,128)(2,1)S(1)} %copy_bitcast_fusion.half, bf16[2,8,128,128]{3,2,1,0:T(8,128)(2,1)S(1)} %collective-permute-done.8.near, bf16[27,128,128]{2,1,0:T(8,128)(2,1)S(1)} %bitcast.72, s32[1]{0:T(128)} %bitcast.22.core), custom_call_target="tpu_custom_call" | custom-call | flops 3600000000 | bytes 4816900 | tf_op jit(solution)/shard_map/cot/pallas_call | solution.py:71
  83.5 2.0 %collective-permute-done.6.pyl = bf16[6,2,128,128]{3,2,1,0:T(8,128)(2,1)S(1)} collective-permute-done((bf16[6,2,128,128]{3,2,1,0:T(8,128)(2,1)}, bf16[6,2,128,128]{3,2,1,0:T(8,128)(2,1)S(1)}, u32[]{:S(2)}, u32[]{:S(2)}) %collective-permute-start.6) | collective-permute-done | bytes 393248 | tf_op jit(solution)/shard_map/ppermute | solution.py:26
  85.5 10.9 %mid.1 = (f32[2,8,64,8,128]{4,3,2,1,0:T(8,128)S(1)}, bf16[6,128,512]{2,1,0:T(8,128)(2,1)S(1)}) custom-call(bf16[2,4,128,128]{3,2,1,0:T(8,128)(2,1)S(1)} %get-tuple-element.17.pc, bf16[2,4,128,128]{3,2,1,0:T(8,128)(2,1)S(1)} %get-tuple-element.39.pzl, bf16[2,4,128,128]{3,2,1,0:T(8,128)(2,1)S(1)} %get-tuple-element.38.pzh, ...), custom_call_target="tpu_custom_call" | custom-call | flops 7000000000 | bytes 10682384 | tf_op jit(solution)/shard_map/mid/pallas_call | solution.py:71
  96.7 1.1 copy-done.6
  97.8 7.5 %last.1 = f32[2,1024,128]{2,1,0:T(8,128)S(1)} custom-call(bf16[6,128,512]{2,1,0:T(8,128)(2,1)S(1)} %get-tuple-element.21.spg, bf16[27,128,128]{2,1,0:T(8,128)(2,1)S(1)} %bitcast.71, bf16[6,256,1280]{2,1,0:T(8,128)(2,1)S(1)} %copy-done.4, s32[2,4,128,128]{3,2,1,0:T(8,128)S(1)} %copy-done.6), custom_call_target="tpu_custom_call" | custom-call | flops 6000000000 | bytes 7176192 | tf_op jit(solution)/shard_map/last/pallas_call | solution.py:71
  105.5 1.7 dynamic-slice_bitcast_fusion
  107.3 1.0 fusion.7
  108.8 26.5 %all_to_all.30 = bf16[8,88,8,128]{3,2,1,0:T(8,128)(2,1)S(1)} all-to-all(bf16[8,88,8,128]{3,2,1,0:T(8,128)(2,1)S(1)} %pad_maximum_fusion), channel_id=1, replica_groups={{0,16,32,48,64,80,96,112},{8,24,40,56,72,88,104,120},{1,17,33,49,65,81,..., dimensions={0} | all-to-all | bytes 2883584 | tf_op jit(solution)/shard_map/all_to_all | solution.py:36
  135.5 22.2 %all_to_all.31 = bf16[8,25,8,128]{3,2,1,0:T(8,128)(2,1)S(1)} all-to-all(bf16[8,25,8,128]{3,2,1,0:T(8,128)(2,1)S(1)} %pad_maximum_fusion.3), channel_id=1, replica_groups=mesh['sx'=16,'sy'=8] {'sy'}, dimensions={0} | all-to-all | bytes 819200 | tf_op jit(solution)/shard_map/all_to_all | solution.py:40
  157.8 9.2 %all_to_all.32 = bf16[8,9,8,128]{3,2,1,0:T(8,128)(2,1)S(1)} all-to-all(bf16[8,9,8,128]{3,2,1,0:T(8,128)(2,1)S(1)} %broadcast_in_dim.17), channel_id=1, replica_groups=mesh['sx'=16,'sy'=8] {'sy'}, dimensions={0} | all-to-all | bytes 294912 | tf_op jit(solution)/shard_map/all_to_all | solution.py:40
  167.9 7.5 %all-to-all-start.5 = ((bf16[16,128,128]{2,1,0:T(8,128)(2,1)}), bf16[16,128,128]{2,1,0:T(8,128)(2,1)S(1)}, u32[]{:S(2)}, u32[]{:S(2)}) async-start(bf16[16,128,128]{2,1,0:T(8,128)(2,1)} %broadcast_in_dim.19), calls=%async_computation.5 | async-start | bytes 1048576 | tf_op jit(solution)/shard_map/all_to_all | solution.py:446
  176.9 8.2 %all-to-all-done.5 = bf16[16,128,128]{2,1,0:T(8,128)(2,1)S(1)} async-done(((bf16[16,128,128]{2,1,0:T(8,128)(2,1)}), bf16[16,128,128]{2,1,0:T(8,128)(2,1)S(1)}, u32[]{:S(2)}, u32[]{:S(2)}) %all-to-all-start.5) | async-done | bytes 524320 | tf_op jit(solution)/shard_map/all_to_all | solution.py:446
  (72 shorter events, 12.7 us)
Async XLA Ops:
  7.2 8.7 %copy-start.7 = (bf16[4,32,128,8]{2,3,1,0:T(8,128)(2,1)S(1)}, bf16[4,32,128,8]{2,3,1,0:T(8,128)(2,1)}, u32[]{:S(2)}) copy-start(bf16[4,32,128,8]{2,3,1,0:T(8,128)(2,1)} %param.10) | copy-start | bytes 786436
  7.2 8.7 %copy-start.8 = (bf16[3,3,3,64,128]{4,3,2,1,0:T(8,128)(2,1)S(1)}, bf16[3,3,3,64,128]{4,3,2,1,0:T(8,128)(2,1)}, u32[]{:S(2)}) copy-start(bf16[3,3,3,64,128]{4,3,2,1,0:T(8,128)(2,1)} %param.7) | copy-start | bytes 1327108
  7.2 69.5 %all-gather.2.cloned.1.call-start = ((), (), s32[]{:S(2)}) async-start(), calls=%async_computation.6 | async-start | bytes 1880064 | tf_op jit(solution)/shard_map/all_gather | solution.py:397
  10.8 6.4 %collective-permute-start.1 = (bf16[1,8,64,256]{3,2,1,0:T(8,128)(2,1)S(1)}, bf16[1,8,64,256]{3,2,1,0:T(8,128)(2,1)S(1)}, u32[]{:S(2)}, u32[]{:S(2)}) collective-permute-start(bf16[1,8,64,256]{3,2,1,0:T(8,128)(2,1)S(1)} %get-tuple-element.30), channel_id=1, source_target_pairs={{0,8},{8,0},{16,24},{24,16},{32,40},{40,32},{48,56},{56,48},{64,72... | collective-permute-start | bytes 786440 | tf_op jit(solution)/shard_map/ppermute | solution.py:16
  12.3 12.9 %collective-permute-start = (bf16[1,8,64,256]{3,2,1,0:T(8,128)(2,1)S(1)}, bf16[1,8,64,256]{3,2,1,0:T(8,128)(2,1)S(1)}, u32[]{:S(2)}, u32[]{:S(2)}) collective-permute-start(bf16[1,8,64,256]{3,2,1,0:T(8,128)(2,1)S(1)} %get-tuple-element.31), channel_id=1, source_target_pairs={{8,16},{16,8},{24,32},{32,24},{40,48},{48,40},{56,64},{64,56},{72,... | collective-permute-start | bytes 786440 | tf_op jit(solution)/shard_map/ppermute | solution.py:17
  15.9 1.2 copy-start.1
  18.0 18.1 %all-to-all-start = ((bf16[8,4,8,8,128]{4,3,2,1,0:T(8,128)(2,1)}), bf16[8,4,8,8,128]{4,3,2,1,0:T(8,128)(2,1)}, u32[]{:S(2)}, u32[]{:S(2)}) async-start(bf16[8,4,8,8,128]{4,3,2,1,0:T(8,128)(2,1)} %copy.25), calls=%async_computation | async-start | bytes 1048576 | tf_op jit(solution)/shard_map/all_to_all | solution.py:40
  26.0 18.4 %collective-permute-start.3 = (bf16[6,1,64,256]{3,2,1,0:T(8,128)(2,1)}, bf16[6,1,64,256]{3,2,1,0:T(8,128)(2,1)S(1)}, u32[]{:S(2)}, u32[]{:S(2)}) collective-permute-start(bf16[6,1,64,256]{3,2,1,0:T(8,128)(2,1)} %pad_maximum_fusion.5), channel_id=1, source_target_pairs={{1,0},{2,1},{3,2},{4,3},{5,4},{6,5},{7,6},{9,8},{10,9},{11,10},{12... | collective-permute-start | bytes 589832 | tf_op jit(solution)/shard_map/ppermute | solution.py:27
  28.0 16.5 %collective-permute-start.2 = (bf16[6,1,64,256]{3,2,1,0:T(8,128)(2,1)}, bf16[6,1,64,256]{3,2,1,0:T(8,128)(2,1)S(1)}, u32[]{:S(2)}, u32[]{:S(2)}) collective-permute-start(bf16[6,1,64,256]{3,2,1,0:T(8,128)(2,1)} %pad_maximum_fusion.4), channel_id=1, source_target_pairs={{0,1},{1,2},{2,3},{3,4},{4,5},{5,6},{6,7},{8,9},{9,10},{10,11},{11... | collective-permute-start | bytes 589832 | tf_op jit(solution)/shard_map/ppermute | solution.py:26
  38.7 34.3 %all-to-all-start.1 = ((bf16[16,4,8,8,128]{4,3,2,1,0:T(8,128)(2,1)}), bf16[16,4,8,8,128]{4,3,2,1,0:T(8,128)(2,1)}, u32[]{:S(2)}, u32[]{:S(2)}) async-start(bf16[16,4,8,8,128]{4,3,2,1,0:T(8,128)(2,1)} %bitcast.78), calls=%async_computation.1 | async-start | bytes 2097152 | tf_op jit(solution)/shard_map/all_to_all | solution.py:403
  44.5 1.0 copy-start.2
  52.7 1.9 copy-start.3
  54.6 0.9 copy-start.5
  55.5 11.3 %collective-permute-start.4 = (bf16[2,4,128,128]{3,2,1,0:T(8,128)(2,1)S(1)}, bf16[2,4,128,128]{3,2,1,0:T(8,128)(2,1)S(1)}, u32[]{:S(2)}, u32[]{:S(2)}) collective-permute-start(bf16[2,4,128,128]{3,2,1,0:T(8,128)(2,1)S(1)} %get-tuple-element.17.pc), channel_id=1, source_target_pairs={{8,16},{16,8},{24,32},{32,24},{40,48},{48,40},{56,64},{64,56},{72,... | collective-permute-start | bytes 786440 | tf_op jit(solution)/shard_map/ppermute | solution.py:17
  59.0 7.7 %collective-permute-start.5 = (bf16[2,4,128,128]{3,2,1,0:T(8,128)(2,1)S(1)}, bf16[2,4,128,128]{3,2,1,0:T(8,128)(2,1)S(1)}, u32[]{:S(2)}, u32[]{:S(2)}) collective-permute-start(bf16[2,4,128,128]{3,2,1,0:T(8,128)(2,1)S(1)} %get-tuple-element.17.pc), channel_id=1, source_target_pairs={{0,8},{8,0},{16,24},{24,16},{32,40},{40,32},{48,56},{56,48},{64,72... | collective-permute-start | bytes 786440 | tf_op jit(solution)/shard_map/ppermute | solution.py:16
  67.8 17.7 %collective-permute-start.6 = (bf16[6,2,128,128]{3,2,1,0:T(8,128)(2,1)}, bf16[6,2,128,128]{3,2,1,0:T(8,128)(2,1)S(1)}, u32[]{:S(2)}, u32[]{:S(2)}) collective-permute-start(bf16[6,2,128,128]{3,2,1,0:T(8,128)(2,1)} %get-tuple-element.35), channel_id=1, source_target_pairs={{0,1},{1,2},{2,3},{3,4},{4,5},{5,6},{6,7},{8,9},{9,10},{10,11},{11... | collective-permute-start | bytes 1179656 | tf_op jit(solution)/shard_map/ppermute | solution.py:26
  71.7 13.7 %collective-permute-start.7 = (bf16[6,2,128,128]{3,2,1,0:T(8,128)(2,1)S(1)}, bf16[6,2,128,128]{3,2,1,0:T(8,128)(2,1)S(1)}, u32[]{:S(2)}, u32[]{:S(2)}) collective-permute-start(bf16[6,2,128,128]{3,2,1,0:T(8,128)(2,1)S(1)} %get-tuple-element.34), channel_id=1, source_target_pairs={{1,0},{2,1},{3,2},{4,3},{5,4},{6,5},{7,6},{9,8},{10,9},{11,10},{12... | collective-permute-start | bytes 1179656 | tf_op jit(solution)/shard_map/ppermute | solution.py:27
  75.2 3.6 %collective-permute-start.8 = (bf16[2,8,128,128]{3,2,1,0:T(8,128)(2,1)}, bf16[2,8,128,128]{3,2,1,0:T(8,128)(2,1)S(1)}, u32[]{:S(2)}, u32[]{:S(2)}) collective-permute-start(bf16[2,8,128,128]{3,2,1,0:T(8,128)(2,1)} %copy_bitcast_fusion.3), channel_id=1, source_target_pairs={{0,8},{8,0},{16,24},{24,16},{32,40},{40,32},{48,56},{56,48},{64,72... | collective-permute-start | bytes 1572872 | tf_op jit(solution)/shard_map/ppermute | solution.py:32
  85.5 11.2 %copy-start.4 = (bf16[6,256,1280]{2,1,0:T(8,128)(2,1)S(1)}, bf16[6,256,1280]{2,1,0:T(8,128)(2,1)}, u32[]{:S(2)}) copy-start(bf16[6,256,1280]{2,1,0:T(8,128)(2,1)} %copy-done.3) | copy-start | bytes 11796484
  96.4 9.0 %copy-start = (f32[2,8,64,8,128]{4,3,2,1,0:T(8,128)}, f32[2,8,64,8,128]{4,3,2,1,0:T(8,128)S(1)}, u32[]{:S(2)}) copy-start(f32[2,8,64,8,128]{4,3,2,1,0:T(8,128)S(1)} %get-tuple-element.20) | copy-start | bytes 12582916
  96.4 1.4 copy-start.6
  96.6 11.7 %collective-permute-start.9 = (bf16[8,64,8,128]{3,2,1,0:T(8,128)(2,1)S(1)}, bf16[8,64,8,128]{3,2,1,0:T(8,128)(2,1)S(1)}, u32[]{:S(2)}, u32[]{:S(2)}) collective-permute-start(bf16[8,64,8,128]{3,2,1,0:T(8,128)(2,1)S(1)} %fusion.1), channel_id=1, source_target_pairs={{0,8},{8,0},{16,24},{24,16},{32,40},{40,32},{48,56},{56,48},{64,72... | collective-permute-start | bytes 3145736 | tf_op jit(solution)/shard_map/ppermute | solution.py:32
  105.4 1.9 collective-permute-start.10
  167.9 17.2 %all-to-all-start.5 = ((bf16[16,128,128]{2,1,0:T(8,128)(2,1)}), bf16[16,128,128]{2,1,0:T(8,128)(2,1)S(1)}, u32[]{:S(2)}, u32[]{:S(2)}) async-start(bf16[16,128,128]{2,1,0:T(8,128)(2,1)} %broadcast_in_dim.19), calls=%async_computation.5 | async-start | bytes 1048576 | tf_op jit(solution)/shard_map/all_to_all | solution.py:446
Sparse Core Ops, SparseCore 0:
  10.3 47.6 all-gather.1

commit v5 on v4

--- a/solution.py
+++ b/solution.py
@@ -11,13 +11,13 @@
 mib = 1024 * 1024
 
 
-def partner_neighbours(first, last):
+def partners(first, last):
     low = lax.axis_index("sx") % 2 == 0
     near = lax.ppermute(jnp.where(low, last, first), "sx", [(i, i ^ 1) for i in range(16)])
     far = lax.ppermute(
         jnp.where(low, first, last), "sx", [(i, i - 1 + 2 * (i % 2)) for i in range(1, 15)]
     )
-    return jnp.where(low, far, near), jnp.where(low, near, far), near
+    return near, far
 
 
 def neighbours(first, last, axis):
@@ -63,7 +63,7 @@
     return jnp.where(rows == count - 1, 0.0, pltpu.roll(values, count - 1, 0))
 
 
-def call(body, outs, scratch, operands, smem=0, flops=0, vmem=24, name=None):
+def call(body, outs, scratch, operands, vmem, smem=0, flops=0, name=None):
     size = sum(int(np.prod(a.shape)) * a.dtype.itemsize for a in operands)
     size += sum(int(np.prod(shape)) * jnp.dtype(kind).itemsize for shape, kind in outs)
     whole = pl.BlockSpec(memory_space=pltpu.VMEM)
@@ -147,6 +147,7 @@
         [((6, 1280, 256), jnp.bfloat16), ((2, 1024, 256), jnp.float32)],
         [vc, vzl, vzh, vyl, vyh, w1, pair_select()],
         flops=5_000_000_000,
+        vmem=18,
         name="first",
     )
 
@@ -217,6 +218,7 @@
         [half, near, k3, core.reshape(1)],
         smem=1,
         flops=3_600_000_000,
+        vmem=16,
         name="cot",
     )
 
@@ -232,17 +234,26 @@
 
 
 def mid_body(
-    pc, pzl, pzh, pyl, pyh, hidden_grad, cot3, k2, k3, flags,
+    own, near, far, ends, near_ends, far_ends, hidden_grad, cot3, k2, k3, flags, core,
     maps, spg, cells, hidden, filters, total, spg3, turned,
 ):
-    for z in range(6):
-        lanes = slice(z * 128, z * 128 + 128)
-        part = (pzl, pc, pzh)[z // 2]
-        for y in range(2):
-            cells[y, :, lanes] = pyl[z, y]
-            cells[y + 6, :, lanes] = pyh[z, y]
-        for y in range(4):
-            cells[y + 2, :, lanes] = part[z % 2, y]
+    at_near = 512 - 512 * core[0]
+    for z in range(2):
+        for part, part_ends, at in (
+            (own, ends, None),
+            (near, near_ends, at_near + z * 128),
+            (far, far_ends, 512 - at_near + z * 128),
+        ):
+            lanes = (
+                slice(256 + z * 128, 384 + z * 128)
+                if at is None
+                else pl.ds(pl.multiple_of(at, 128), 128)
+            )
+            for y in range(2):
+                cells[y, :, lanes] = part_ends[z, y]
+                cells[y + 6, :, lanes] = part_ends[z, y + 2]
+            for y in range(4):
+                cells[y + 2, :, lanes] = part[z, y]
     lay_filters(filters, lambda a, b, c: k2[9 * a + 3 * b + c], True)
     lane = lax.broadcasted_iota(jnp.int32, (128, 256), 1)
     for j in range(2):
@@ -265,7 +276,7 @@
 
     def store(place, value):
         for i in range(16):
-            maps[i % 2, i // 2, place] = value[i * 8 : i * 8 + 8]
+            maps[(i + core[0]) % 2, i // 2, place] = value[i * 8 : i * 8 + 8]
 
     def store_third(tap, value):
         store(27 + tap, value)
@@ -293,7 +304,9 @@
             store(56 + z * 4 + y, done[:, z * 128 : z * 128 + 128].T)
 
 
-def mid_section(pc, pzl, pzh, pyl, pyh, hidden_grad, cot3, k2, k3, flags):
+def mid_section(
+    own, near, far, ends, near_ends, far_ends, hidden_grad, cot3, k2, k3, flags, core
+):
     return call(
         mid_body,
         [
@@ -308,15 +321,16 @@
             ((512, 768), jnp.bfloat16),
             ((512, 768), jnp.bfloat16),
         ],
-        [pc, pzl, pzh, pyl, pyh, hidden_grad, cot3, k2, k3, flags],
-        smem=1,
+        [own, near, far, ends, near_ends, far_ends, hidden_grad, cot3, k2, k3]
+        + [flags, core.reshape(1)],
+        smem=2,
         flops=7_000_000_000,
-        vmem=32,
+        vmem=26,
         name="mid",
     )
 
 
-def last_body(spg, k2, xt, bits, first, filters, total, back, full):
+def last_body(spg, k2, xt, bits, core, first, filters, total, back, full):
     lay_filters(filters, lambda a, b, c: k2[(2 - a) * 9 + (2 - b) * 3 + 2 - c], False)
     conv_rows(spg, slice(0, 512), filters, total, 4)
     for y in range(4):
@@ -348,13 +362,12 @@
                 high = full[a * 256 + odd * 64 : a * 256 + odd * 64 + 64, 128:256]
                 tap = 9 * a + 3 * b + c
                 row = tap // 4 * 128 + tap % 2 * 64
-                first[tap // 2 % 2, row : row + 64, :] = low + high
-    first[1, 832:1024, :] = jnp.zeros((192, 128), jnp.float32)
-    first[0, 960:1024, :] = jnp.zeros((64, 128), jnp.float32)
-    first[0, 896:960, :] = jnp.zeros((64, 128), jnp.float32)
-
-
-def last_section(spg, k2, xt, bits):
+                first[(tap // 2 + core[0]) % 2, row : row + 64, :] = low + high
+    first[core[0], 896:1024, :] = jnp.zeros((128, 128), jnp.float32)
+    first[1 - core[0], 832:1024, :] = jnp.zeros((192, 128), jnp.float32)
+
+
+def last_section(spg, k2, xt, bits, core):
     return call(
         last_body,
         [((2, 1024, 128), jnp.float32)],
@@ -364,8 +377,10 @@
             ((4, 1024, 256), jnp.bfloat16),
             ((768, 256), jnp.float32),
         ],
-        [spg, k2, xt, bits],
+        [spg, k2, xt, bits, core.reshape(1)],
+        smem=1,
         flops=6_000_000_000,
+        vmem=20,
         name="last",
     )[0]
 
@@ -396,7 +411,8 @@
     )
     filters = lax.all_gather(shares, "sx", axis=0, tiled=True)
     vc = jnp.swapaxes(volume, 2, 3)
-    vzl, vzh, near = partner_neighbours(after(vc[:1], shares), vc[-1:])
+    near, far = partners(after(vc[:1], shares), vc[-1:])
+    vzl, vzh = jnp.where(core == 0, far, near), jnp.where(core == 0, near, far)
     deep = lambda y: jnp.concatenate([vzl[:, y : y + 1], vc[:, y : y + 1], vzh[:, y : y + 1]])
     vyl, vyh = neighbours(deep(0), deep(7), "sy")
     cot_tall = to_sy(after(cot_rows(jnp.swapaxes(cotangent, 2, 3)), near))
@@ -405,19 +421,22 @@
     cot_near = other_core(jnp.where(core == 0, cot_half[2:], cot_half[:2]))
     w1 = after(pair_filters(first_kernel), cot_tall)
     pooled, bits, xt = first_section(vc, vzl, vzh, vyl, vyh, w1)
-    pzl, pzh, _ = partner_neighbours(pooled, pooled)
+    pyl, pyh = neighbours(pooled[:, :2], pooled[:, 2:], "sy")
+    near, far = partners(pooled, pooled)
+    ends = jnp.concatenate([pyl, pyh], axis=1)
+    near_ends, far_ends = partners(ends, ends)
     filters = filters.reshape(16, 54, 8, 128).swapaxes(0, 1).reshape(54, 128, 128)
     k2, k3 = filters[:27], filters[27:]
     hidden_grad, cot3 = cot_section(cot_half, cot_near, core, k3)
-    tall = jnp.concatenate([pzl, pooled, pzh])
-    pyl, pyh = neighbours(tall[:, :2], tall[:, 2:], "sy")
-    maps, spg = mid_section(pooled, pzl, pzh, pyl, pyh, hidden_grad, cot3, k2, k3, flags)
-    from_other = other_core(maps[1 - core].astype(jnp.bfloat16))
-    own = maps[core]
+    maps, spg = mid_section(
+        pooled, near, far, ends, near_ends, far_ends, hidden_grad, cot3, k2, k3, flags, core
+    )
+    from_other = other_core(maps[1].astype(jnp.bfloat16))
+    own = maps[0]
     mine, theirs = own[:, 56:].astype(jnp.bfloat16), from_other[:, 56:]
-    first_part = last_section(spg, k2, xt, bits)
-    first_from = other_core(first_part[1 - core].astype(jnp.bfloat16))
-    first_half = first_part[core] + first_from.astype(jnp.float32)
+    first_part = last_section(spg, k2, xt, bits, core)
+    first_from = other_core(first_part[1].astype(jnp.bfloat16))
+    first_half = first_part[0] + first_from.astype(jnp.float32)
     grads = own[:, :56] + from_other[:, :56].astype(jnp.float32)
     parts = jnp.concatenate(
         [

time: 194 us -> 183 us (0.943)
  blocking collectives: 58 us -> 47.7 us
  starting transfers between devices: 41.4 us -> 48.2 us
  waiting for transfers between devices: 20.5 us -> 17 us
  local copies, waits for them, and re-layouts: 18.8 us -> 16 us
    ppermute x4 -> x6, waiting for transfers between devices: 7.56 us -> 0.02 us  [the longest x3 0.01 us: partners(): lax.ppermute(jnp.where(low, last, first), 'sx', [(i, i ^ 1) for i in rang...]
    all_to_all x2, blocking collectives: 31.4 us -> 24.3 us  [to_sy(): return lax.all_to_all(parts, 'sy', 0, 0, tiled=True)]
    ppermute x4 -> x6, starting transfers between devices: 8.64 us -> 14.5 us  [the longest x3 12.8 us: partners(): lax.ppermute(jnp.where(low, first, last), 'sx', [(i, i - 1 + 2 * (i % 2))...]
    ppermute x2, waiting for transfers between devices: 0.01 us -> 4.92 us  [neighbours(): lax.ppermute(first, axis, [(i + 1, i) for i in range(ends)])]
    all_to_all x1, blocking collectives: 26.5 us -> 23.4 us  [to_chips(): lax.all_to_all(parts, 'sx', 0, 0, axis_index_groups=same_core, tiled=True)]
    ppermute x2, waiting for transfers between devices: 2 us -> 0.01 us  [neighbours(): lax.ppermute(last, axis, [(i, i + 1) for i in range(ends)])]
    unnamed x19 -> x18, local copies, waits for them, and re-layouts: 5.81 us -> 5.41 us
  transfers between devices with their start and end apart: 15 -> 17, of which waited for: 4 -> 4; matrix products, arithmetic and copies ran while one was open for 9% -> 8% of each run, Pallas kernels for 10% -> 11%
where the time goes in v5:
time: 183 us; the launch traced here: 182 us
  starting transfers between devices  48.2 us (26%)
  blocking collectives  47.7 us (26%)
  Pallas kernels  30.5 us (17%)
  waiting for transfers between devices  17 us (9%)
  local copies, waits for them, and re-layouts  16 us (9%)
  between operations  14.5 us (8%)
  other arithmetic  8.35 us (5%)
    pallas_call x4, Pallas kernels, call(): pl.pallas_call(body, out_shape=[jax.ShapeDtypeStruct(shape, kind) for sha...  30.5 us
    all_to_all x2, blocking collectives, to_sy(): return lax.all_to_all(parts, 'sy', 0, 0, tiled=True)  24.3 us
    all_to_all x1, blocking collectives, to_chips(): lax.all_to_all(parts, 'sx', 0, 0, axis_index_groups=same_core, tiled=True)  23.4 us
    ppermute x3, starting transfers between devices, partners(): lax.ppermute(jnp.where(low, first, last), 'sx', [(i, i - 1 + 2 * (i % 2))...  12.8 us
    ppermute x2, starting transfers between devices, neighbours(): lax.ppermute(last, axis, [(i, i + 1) for i in range(ends)])  9.37 us
    all_to_all x1, waiting for transfers between devices, on_device(): lax.all_to_all(first_grad, 'sx', 0, 0, tiled=True).reshape(2048, 128)[:1728]  8.21 us
    all_to_all x1, starting transfers between devices, on_device(): lax.all_to_all(first_grad, 'sx', 0, 0, tiled=True).reshape(2048, 128)[:1728]  7.7 us
    all_to_all x1, starting transfers between devices, to_sy(): return lax.all_to_all(parts, 'sy', 0, 0, tiled=True)  7.21 us
  transfers between devices with their start and end apart: 17, of which 4 were waited for; matrix products, arithmetic and copies ran while one was open for 8% of the time, Pallas kernels for 11%

profile of v5, /device:TPU:1, one launch (start us, length us, event | category | flops | bytes accessed | tf_op | source)
XLA Modules:
  0.0 182.3 jit_solution(2666602365140718208)
XLA Ops:
  7.2 1.5 pad_maximum_fusion.5
  8.8 1.0 slice.180
  9.8 1.0 broadcast_select_fusion.2
  10.8 1.5 collective-permute-start.1
  12.3 3.7 %collective-permute-start = (bf16[1,8,64,256]{3,2,1,0:T(8,128)(2,1)S(1)}, bf16[1,8,64,256]{3,2,1,0:T(8,128)(2,1)S(1)}, u32[]{:S(2)}, u32[]{:S(2)}) collective-permute-start(bf16[1,8,64,256]{3,2,1,0:T(8,128)(2,1)S(1)} %get-tuple-element.31), channel_id=1, source_target_pairs={{8,16},{16,8},{24,32},{32,24},{40,48},{48,40},{56,64},{64,56},{72,... | collective-permute-start | bytes 786440 | tf_op jit(solution)/shard_map/ppermute | solution.py:17
  18.2 7.2 %all-to-all-start = ((bf16[8,4,8,8,128]{4,3,2,1,0:T(8,128)(2,1)}), bf16[8,4,8,8,128]{4,3,2,1,0:T(8,128)(2,1)}, u32[]{:S(2)}, u32[]{:S(2)}) async-start(bf16[8,4,8,8,128]{4,3,2,1,0:T(8,128)(2,1)} %copy.25), calls=%async_computation | async-start | bytes 1048576 | tf_op jit(solution)/shard_map/all_to_all | solution.py:40
  26.1 4.9 %collective-permute-start.2 = (bf16[6,1,64,256]{3,2,1,0:T(8,128)(2,1)}, bf16[6,1,64,256]{3,2,1,0:T(8,128)(2,1)S(1)}, u32[]{:S(2)}, u32[]{:S(2)}) collective-permute-start(bf16[6,1,64,256]{3,2,1,0:T(8,128)(2,1)} %pad_maximum_fusion.3), channel_id=1, source_target_pairs={{0,1},{1,2},{2,3},{3,4},{4,5},{5,6},{6,7},{8,9},{9,10},{10,11},{11... | collective-permute-start | bytes 589832 | tf_op jit(solution)/shard_map/ppermute | solution.py:26
  31.7 1.3 collective-permute-start.3
  33.0 2.5 %all-to-all-done = bf16[8,4,8,8,128]{4,3,2,1,0:T(8,128)(2,1)} async-done(((bf16[8,4,8,8,128]{4,3,2,1,0:T(8,128)(2,1)}), bf16[8,4,8,8,128]{4,3,2,1,0:T(8,128)(2,1)}, u32[]{:S(2)}, u32[]{:S(2)}) %all-to-all-start) | async-done | bytes 524320 | tf_op jit(solution)/shard_map/all_to_all | solution.py:40
  35.5 1.3 pad_slice_fusion.1
  36.9 1.1 copy.26
  38.0 6.1 %all-to-all-start.1 = ((bf16[16,4,8,8,128]{4,3,2,1,0:T(8,128)(2,1)}), bf16[16,4,8,8,128]{4,3,2,1,0:T(8,128)(2,1)}, u32[]{:S(2)}, u32[]{:S(2)}) async-start(bf16[16,4,8,8,128]{4,3,2,1,0:T(8,128)(2,1)} %bitcast.80), calls=%async_computation.1 | async-start | bytes 2097152 | tf_op jit(solution)/shard_map/all_to_all | solution.py:419
  45.1 7.3 %first.1 = (bf16[2,4,128,128]{3,2,1,0:T(8,128)(2,1)S(1)}, s32[2,4,128,128]{3,2,1,0:T(8,128)S(1)}, bf16[6,256,1280]{2,1,0:T(8,128)(2,1)S(1)}) custom-call(bf16[4,8,64,256]{3,2,1,0:T(8,128)(2,1)S(1)} %bitcast.79, bf16[1,8,64,256]{3,2,1,0:T(8,128)(2,1)S(1)} %get-tuple-element.37.vzl, bf16[1,8,64,256]{3,2,1,0:T(8,128)(2,1)S(1)} %get-tuple-element.36.vzh, ...), custom_call_target="tpu_custom_call" | custom-call | flops 5000000000 | bytes 8126464 | tf_op jit(solution)/shard_map/first/pallas_call | solution.py:71
  52.4 1.9 %copy-done.2 = bf16[6,256,1280]{2,1,0:T(8,128)(2,1)} copy-done((bf16[6,256,1280]{2,1,0:T(8,128)(2,1)}, bf16[6,256,1280]{2,1,0:T(8,128)(2,1)S(1)}, u32[]{:S(2)}) %copy-start.2) | copy-done | bytes 3932184
  55.1 4.5 %collective-permute-start.6 = (bf16[2,2,128,128]{3,2,1,0:T(8,128)(2,1)S(1)}, bf16[2,2,128,128]{3,2,1,0:T(8,128)(2,1)S(1)}, u32[]{:S(2)}, u32[]{:S(2)}) collective-permute-start(bf16[2,2,128,128]{3,2,1,0:T(8,128)(2,1)S(1)} %get-tuple-element.42), channel_id=1, source_target_pairs={{0,1},{1,2},{2,3},{3,4},{4,5},{5,6},{6,7},{8,9},{9,10},{10,11},{11... | collective-permute-start | bytes 393224 | tf_op jit(solution)/shard_map/ppermute | solution.py:26
  59.6 1.3 collective-permute-start.7
  61.0 5.0 %collective-permute-start.5 = (bf16[2,4,128,128]{3,2,1,0:T(8,128)(2,1)S(1)}, bf16[2,4,128,128]{3,2,1,0:T(8,128)(2,1)S(1)}, u32[]{:S(2)}, u32[]{:S(2)}) collective-permute-start(bf16[2,4,128,128]{3,2,1,0:T(8,128)(2,1)S(1)} %get-tuple-element.17.own), channel_id=1, source_target_pairs={{8,16},{16,8},{24,32},{32,24},{40,48},{48,40},{56,64},{64,56},{72,... | collective-permute-start | bytes 786440 | tf_op jit(solution)/shard_map/ppermute | solution.py:17
  66.2 4.9 %collective-permute-done.7 = bf16[2,2,128,128]{3,2,1,0:T(8,128)(2,1)S(1)} collective-permute-done((bf16[2,2,128,128]{3,2,1,0:T(8,128)(2,1)S(1)}, bf16[2,2,128,128]{3,2,1,0:T(8,128)(2,1)S(1)}, u32[]{:S(2)}, u32[]{:S(2)}) %collective-permute-start.7) | collective-permute-done | bytes 131104 | tf_op jit(solution)/shard_map/ppermute | solution.py:27
  71.1 4.2 %collective-permute-start.9 = (bf16[2,4,128,128]{3,2,1,0:T(8,128)(2,1)S(1)}, bf16[2,4,128,128]{3,2,1,0:T(8,128)(2,1)S(1)}, u32[]{:S(2)}, u32[]{:S(2)}) collective-permute-start(bf16[2,4,128,128]{3,2,1,0:T(8,128)(2,1)S(1)} %constant_dynamic-update-slice_fusion.ends), channel_id=1, source_target_pairs={{8,16},{16,8},{24,32},{32,24},{40,48},{48,40},{56,64},{64,56},{72,... | collective-permute-start | bytes 786440 | tf_op jit(solution)/shard_map/ppermute | solution.py:17
  75.4 2.2 %copy_bitcast_fusion.3 = bf16[2,8,128,128]{3,2,1,0:T(8,128)(2,1)} fusion(bf16[4,8,16,8,128]{4,3,1,0,2:T(8,128)(2,1)} %bitcast.16, pred[]{:T(512)S(6)} %eq.7), kind=kLoop, calls=%fused_computation.26 | loop fusion | flops 262144 | bytes 1572865 | tf_op jit(solution)/shard_map/jit(_where)/select_n | solution.py:421
  78.0 1.5 copy_bitcast_fusion.half
  79.6 1.6 fusion.10
  81.6 4.7 %cot.1 = (f32[6,128,512]{2,1,0:T(8,128)S(1)}, bf16[512,768]{1,0:T(8,128)(2,1)S(1)}) custom-call(bf16[4,8,128,128]{3,2,1,0:T(8,128)(2,1)S(1)} %copy_bitcast_fusion.half, bf16[2,8,128,128]{3,2,1,0:T(8,128)(2,1)S(1)} %collective-permute-done.10.near, bf16[27,128,128]{2,1,0:T(8,128)(2,1)S(1)} %bitcast.74, s32[1]{0:T(128)} %bitcast.22.core), custom_call_target="tpu_custom_call" | custom-call | flops 3600000000 | bytes 4816900 | tf_op jit(solution)/shard_map/cot/pallas_call | solution.py:71
  86.3 11.0 %mid.1 = (f32[2,8,64,8,128]{4,3,2,1,0:T(8,128)S(1)}, bf16[6,128,512]{2,1,0:T(8,128)(2,1)S(1)}) custom-call(bf16[2,4,128,128]{3,2,1,0:T(8,128)(2,1)S(1)} %get-tuple-element.17.own, bf16[2,4,128,128]{3,2,1,0:T(8,128)(2,1)S(1)} %collective-permute-done.4.near, bf16[2,4,128,128]{3,2,1,0:T(8,128)(2,1)S(1)} %collective-permute-done.5.far, ...), custom_call_target="tpu_custom_call" | custom-call | flops 7000000000 | bytes 10682388 | tf_op jit(solution)/shard_map/mid/pallas_call | solution.py:71
  98.4 7.5 %last.1 = f32[2,1024,128]{2,1,0:T(8,128)S(1)} custom-call(bf16[6,128,512]{2,1,0:T(8,128)(2,1)S(1)} %get-tuple-element.21.spg, bf16[27,128,128]{2,1,0:T(8,128)(2,1)S(1)} %bitcast.73, bf16[6,256,1280]{2,1,0:T(8,128)(2,1)S(1)} %copy-done.3, s32[2,4,128,128]{3,2,1,0:T(8,128)S(1)} %copy-done.5, s32[1]{0:T(128)} %bitcast.22.core), custom_call_target="tpu_custom_call" | custom-call | flops 6000000000 | bytes 7176196 | tf_op jit(solution)/shard_map/last/pallas_call | solution.py:71
  106.3 1.4 collective-permute-done.12
  108.2 23.4 %all_to_all.30 = bf16[8,88,8,128]{3,2,1,0:T(8,128)(2,1)S(1)} all-to-all(bf16[8,88,8,128]{3,2,1,0:T(8,128)(2,1)S(1)} %pad_maximum_fusion), channel_id=1, replica_groups={{0,16,32,48,64,80,96,112},{8,24,40,56,72,88,104,120},{1,17,33,49,65,81,..., dimensions={0} | all-to-all | bytes 2883584 | tf_op jit(solution)/shard_map/all_to_all | solution.py:36
  131.8 15.0 %all_to_all.31 = bf16[8,25,8,128]{3,2,1,0:T(8,128)(2,1)S(1)} all-to-all(bf16[8,25,8,128]{3,2,1,0:T(8,128)(2,1)S(1)} %pad_maximum_fusion.2), channel_id=1, replica_groups=mesh['sx'=16,'sy'=8] {'sy'}, dimensions={0} | all-to-all | bytes 819200 | tf_op jit(solution)/shard_map/all_to_all | solution.py:40
  146.9 9.3 %all_to_all.32 = bf16[8,9,8,128]{3,2,1,0:T(8,128)(2,1)S(1)} all-to-all(bf16[8,9,8,128]{3,2,1,0:T(8,128)(2,1)S(1)} %broadcast_in_dim.17), channel_id=1, replica_groups=mesh['sx'=16,'sy'=8] {'sy'}, dimensions={0} | all-to-all | bytes 294912 | tf_op jit(solution)/shard_map/all_to_all | solution.py:40
  157.1 7.7 %all-to-all-start.5 = ((bf16[16,128,128]{2,1,0:T(8,128)(2,1)}), bf16[16,128,128]{2,1,0:T(8,128)(2,1)S(1)}, u32[]{:S(2)}, u32[]{:S(2)}) async-start(bf16[16,128,128]{2,1,0:T(8,128)(2,1)} %broadcast_in_dim.19), calls=%async_computation.5 | async-start | bytes 1048576 | tf_op jit(solution)/shard_map/all_to_all | solution.py:465
  166.2 8.2 %all-to-all-done.5 = bf16[16,128,128]{2,1,0:T(8,128)(2,1)S(1)} async-done(((bf16[16,128,128]{2,1,0:T(8,128)(2,1)}), bf16[16,128,128]{2,1,0:T(8,128)(2,1)S(1)}, u32[]{:S(2)}, u32[]{:S(2)}) %all-to-all-start.5) | async-done | bytes 524320 | tf_op jit(solution)/shard_map/all_to_all | solution.py:465
  174.5 1.0 convert.16
  (74 shorter events, 11.3 us)
Async XLA Ops:
  7.2 8.8 %copy-start.7 = (bf16[3,3,3,64,128]{4,3,2,1,0:T(8,128)(2,1)S(1)}, bf16[3,3,3,64,128]{4,3,2,1,0:T(8,128)(2,1)}, u32[]{:S(2)}) copy-start(bf16[3,3,3,64,128]{4,3,2,1,0:T(8,128)(2,1)} %param.7) | copy-start | bytes 1327108
  7.2 72.4 %all-gather.2.cloned.1.call-start = ((), (), s32[]{:S(2)}) async-start(), calls=%async_computation.6 | async-start | bytes 1880064 | tf_op jit(solution)/shard_map/all_gather | solution.py:412
  10.8 6.5 %collective-permute-start.1 = (bf16[1,8,64,256]{3,2,1,0:T(8,128)(2,1)S(1)}, bf16[1,8,64,256]{3,2,1,0:T(8,128)(2,1)S(1)}, u32[]{:S(2)}, u32[]{:S(2)}) collective-permute-start(bf16[1,8,64,256]{3,2,1,0:T(8,128)(2,1)S(1)} %get-tuple-element.30), channel_id=1, source_target_pairs={{0,8},{8,0},{16,24},{24,16},{32,40},{40,32},{48,56},{56,48},{64,72... | collective-permute-start | bytes 786440 | tf_op jit(solution)/shard_map/ppermute | solution.py:16
  12.3 4.0 %copy-start.6 = (bf16[4,32,128,8]{2,3,1,0:T(8,128)(2,1)S(1)}, bf16[4,32,128,8]{2,3,1,0:T(8,128)(2,1)}, u32[]{:S(2)}) copy-start(bf16[4,32,128,8]{2,3,1,0:T(8,128)(2,1)} %param.10) | copy-start | bytes 786436
  12.3 13.1 %collective-permute-start = (bf16[1,8,64,256]{3,2,1,0:T(8,128)(2,1)S(1)}, bf16[1,8,64,256]{3,2,1,0:T(8,128)(2,1)S(1)}, u32[]{:S(2)}, u32[]{:S(2)}) collective-permute-start(bf16[1,8,64,256]{3,2,1,0:T(8,128)(2,1)S(1)} %get-tuple-element.31), channel_id=1, source_target_pairs={{8,16},{16,8},{24,32},{32,24},{40,48},{48,40},{56,64},{64,56},{72,... | collective-permute-start | bytes 786440 | tf_op jit(solution)/shard_map/ppermute | solution.py:17
  16.1 1.2 copy-start
  18.2 17.3 %all-to-all-start = ((bf16[8,4,8,8,128]{4,3,2,1,0:T(8,128)(2,1)}), bf16[8,4,8,8,128]{4,3,2,1,0:T(8,128)(2,1)}, u32[]{:S(2)}, u32[]{:S(2)}) async-start(bf16[8,4,8,8,128]{4,3,2,1,0:T(8,128)(2,1)} %copy.25), calls=%async_computation | async-start | bytes 1048576 | tf_op jit(solution)/shard_map/all_to_all | solution.py:40
  26.1 18.0 %collective-permute-start.2 = (bf16[6,1,64,256]{3,2,1,0:T(8,128)(2,1)}, bf16[6,1,64,256]{3,2,1,0:T(8,128)(2,1)S(1)}, u32[]{:S(2)}, u32[]{:S(2)}) collective-permute-start(bf16[6,1,64,256]{3,2,1,0:T(8,128)(2,1)} %pad_maximum_fusion.3), channel_id=1, source_target_pairs={{0,1},{1,2},{2,3},{3,4},{4,5},{5,6},{6,7},{8,9},{9,10},{10,11},{11... | collective-permute-start | bytes 589832 | tf_op jit(solution)/shard_map/ppermute | solution.py:26
  31.7 12.4 %collective-permute-start.3 = (bf16[6,1,64,256]{3,2,1,0:T(8,128)(2,1)}, bf16[6,1,64,256]{3,2,1,0:T(8,128)(2,1)S(1)}, u32[]{:S(2)}, u32[]{:S(2)}) collective-permute-start(bf16[6,1,64,256]{3,2,1,0:T(8,128)(2,1)} %pad_maximum_fusion.4), channel_id=1, source_target_pairs={{1,0},{2,1},{3,2},{4,3},{5,4},{6,5},{7,6},{9,8},{10,9},{11,10},{12... | collective-permute-start | bytes 589832 | tf_op jit(solution)/shard_map/ppermute | solution.py:27
  38.0 37.4 %all-to-all-start.1 = ((bf16[16,4,8,8,128]{4,3,2,1,0:T(8,128)(2,1)}), bf16[16,4,8,8,128]{4,3,2,1,0:T(8,128)(2,1)}, u32[]{:S(2)}, u32[]{:S(2)}) async-start(bf16[16,4,8,8,128]{4,3,2,1,0:T(8,128)(2,1)} %bitcast.80), calls=%async_computation.1 | async-start | bytes 2097152 | tf_op jit(solution)/shard_map/all_to_all | solution.py:419
  44.1 1.0 copy-start.1
  52.4 1.9 %copy-start.2 = (bf16[6,256,1280]{2,1,0:T(8,128)(2,1)}, bf16[6,256,1280]{2,1,0:T(8,128)(2,1)S(1)}, u32[]{:S(2)}) copy-start(bf16[6,256,1280]{2,1,0:T(8,128)(2,1)S(1)} %get-tuple-element.22.xt) | copy-start | bytes 11796484
  54.2 0.8 copy-start.4
  55.1 11.0 %collective-permute-start.6 = (bf16[2,2,128,128]{3,2,1,0:T(8,128)(2,1)S(1)}, bf16[2,2,128,128]{3,2,1,0:T(8,128)(2,1)S(1)}, u32[]{:S(2)}, u32[]{:S(2)}) collective-permute-start(bf16[2,2,128,128]{3,2,1,0:T(8,128)(2,1)S(1)} %get-tuple-element.42), channel_id=1, source_target_pairs={{0,1},{1,2},{2,3},{3,4},{4,5},{5,6},{6,7},{8,9},{9,10},{10,11},{11... | collective-permute-start | bytes 393224 | tf_op jit(solution)/shard_map/ppermute | solution.py:26
  59.6 11.4 %collective-permute-start.7 = (bf16[2,2,128,128]{3,2,1,0:T(8,128)(2,1)S(1)}, bf16[2,2,128,128]{3,2,1,0:T(8,128)(2,1)S(1)}, u32[]{:S(2)}, u32[]{:S(2)}) collective-permute-start(bf16[2,2,128,128]{3,2,1,0:T(8,128)(2,1)S(1)} %get-tuple-element.41), channel_id=1, source_target_pairs={{1,0},{2,1},{3,2},{4,3},{5,4},{6,5},{7,6},{9,8},{10,9},{11,10},{12... | collective-permute-start | bytes 393224 | tf_op jit(solution)/shard_map/ppermute | solution.py:27
  61.0 25.3 %collective-permute-start.5 = (bf16[2,4,128,128]{3,2,1,0:T(8,128)(2,1)S(1)}, bf16[2,4,128,128]{3,2,1,0:T(8,128)(2,1)S(1)}, u32[]{:S(2)}, u32[]{:S(2)}) collective-permute-start(bf16[2,4,128,128]{3,2,1,0:T(8,128)(2,1)S(1)} %get-tuple-element.17.own), channel_id=1, source_target_pairs={{8,16},{16,8},{24,32},{32,24},{40,48},{48,40},{56,64},{64,56},{72,... | collective-permute-start | bytes 786440 | tf_op jit(solution)/shard_map/ppermute | solution.py:17
  66.0 20.2 %collective-permute-start.4 = (bf16[2,4,128,128]{3,2,1,0:T(8,128)(2,1)S(1)}, bf16[2,4,128,128]{3,2,1,0:T(8,128)(2,1)S(1)}, u32[]{:S(2)}, u32[]{:S(2)}) collective-permute-start(bf16[2,4,128,128]{3,2,1,0:T(8,128)(2,1)S(1)} %get-tuple-element.17.own), channel_id=1, source_target_pairs={{0,8},{8,0},{16,24},{24,16},{32,40},{40,32},{48,56},{56,48},{64,72... | collective-permute-start | bytes 786440 | tf_op jit(solution)/shard_map/ppermute | solution.py:16
  71.1 15.2 %collective-permute-start.9 = (bf16[2,4,128,128]{3,2,1,0:T(8,128)(2,1)S(1)}, bf16[2,4,128,128]{3,2,1,0:T(8,128)(2,1)S(1)}, u32[]{:S(2)}, u32[]{:S(2)}) collective-permute-start(bf16[2,4,128,128]{3,2,1,0:T(8,128)(2,1)S(1)} %constant_dynamic-update-slice_fusion.ends), channel_id=1, source_target_pairs={{8,16},{16,8},{24,32},{32,24},{40,48},{48,40},{56,64},{64,56},{72,... | collective-permute-start | bytes 786440 | tf_op jit(solution)/shard_map/ppermute | solution.py:17
  75.3 11.0 %collective-permute-start.8 = (bf16[2,4,128,128]{3,2,1,0:T(8,128)(2,1)S(1)}, bf16[2,4,128,128]{3,2,1,0:T(8,128)(2,1)S(1)}, u32[]{:S(2)}, u32[]{:S(2)}) collective-permute-start(bf16[2,4,128,128]{3,2,1,0:T(8,128)(2,1)S(1)} %constant_dynamic-update-slice_fusion.ends), channel_id=1, source_target_pairs={{0,8},{8,0},{16,24},{24,16},{32,40},{40,32},{48,56},{56,48},{64,72... | collective-permute-start | bytes 786440 | tf_op jit(solution)/shard_map/ppermute | solution.py:16
  77.5 4.1 %collective-permute-start.10 = (bf16[2,8,128,128]{3,2,1,0:T(8,128)(2,1)}, bf16[2,8,128,128]{3,2,1,0:T(8,128)(2,1)S(1)}, u32[]{:S(2)}, u32[]{:S(2)}) collective-permute-start(bf16[2,8,128,128]{3,2,1,0:T(8,128)(2,1)} %copy_bitcast_fusion.3), channel_id=1, source_target_pairs={{0,8},{8,0},{16,24},{24,16},{32,40},{40,32},{48,56},{56,48},{64,72... | collective-permute-start | bytes 1572872 | tf_op jit(solution)/shard_map/ppermute | solution.py:32
  86.3 11.3 %copy-start.3 = (bf16[6,256,1280]{2,1,0:T(8,128)(2,1)S(1)}, bf16[6,256,1280]{2,1,0:T(8,128)(2,1)}, u32[]{:S(2)}) copy-start(bf16[6,256,1280]{2,1,0:T(8,128)(2,1)} %copy-done.2) | copy-start | bytes 11796484
  97.4 1.0 copy-start.5
  97.6 10.1 %collective-permute-start.11 = (bf16[8,64,8,128]{3,2,1,0:T(8,128)(2,1)S(1)}, bf16[8,64,8,128]{3,2,1,0:T(8,128)(2,1)S(1)}, u32[]{:S(2)}, u32[]{:S(2)}) collective-permute-start(bf16[8,64,8,128]{3,2,1,0:T(8,128)(2,1)S(1)} %fusion.1), channel_id=1, source_target_pairs={{0,8},{8,0},{16,24},{24,16},{32,40},{40,32},{48,56},{56,48},{64,72... | collective-permute-start | bytes 3145736 | tf_op jit(solution)/shard_map/ppermute | solution.py:32
  106.0 1.6 collective-permute-start.12
  157.1 17.4 %all-to-all-start.5 = ((bf16[16,128,128]{2,1,0:T(8,128)(2,1)}), bf16[16,128,128]{2,1,0:T(8,128)(2,1)S(1)}, u32[]{:S(2)}, u32[]{:S(2)}) async-start(bf16[16,128,128]{2,1,0:T(8,128)(2,1)} %broadcast_in_dim.19), calls=%async_computation.5 | async-start | bytes 1048576 | tf_op jit(solution)/shard_map/all_to_all | solution.py:465
Sparse Core Ops, SparseCore 0:
  10.3 48.2 all-gather.1

commit v6 on v5

--- a/solution.py
+++ b/solution.py
@@ -11,12 +11,13 @@
 mib = 1024 * 1024
 
 
-def partners(first, last):
+def partners(first, last, tie=None):
     low = lax.axis_index("sx") % 2 == 0
-    near = lax.ppermute(jnp.where(low, last, first), "sx", [(i, i ^ 1) for i in range(16)])
-    far = lax.ppermute(
-        jnp.where(low, first, last), "sx", [(i, i - 1 + 2 * (i % 2)) for i in range(1, 15)]
-    )
+    to_near, to_far = jnp.where(low, last, first), jnp.where(low, first, last)
+    if tie is not None:
+        to_near, to_far = after(to_near, tie), after(to_far, tie)
+    near = lax.ppermute(to_near, "sx", [(i, i ^ 1) for i in range(16)])
+    far = lax.ppermute(to_far, "sx", [(i, i - 1 + 2 * (i % 2)) for i in range(1, 15)])
     return near, far
 
 
@@ -97,7 +98,7 @@
     return jnp.concatenate([even, odd], axis=2)
 
 
-def first_body(vc, vzl, vzh, vyl, vyh, w1, sel, pooled, bits, xt, xc, acc):
+def first_body(vc, vzl, vzh, vyl, vyh, w1, sel, pooled, xt, xc, acc):
     for z in range(6):
         rows = vzl[0] if z == 0 else vzh[0] if z == 5 else vc[z - 1]
         got = dot(rows.reshape(512, 256), sel[...]).astype(jnp.bfloat16)
@@ -133,7 +134,9 @@
                         mean += jnp.where(up, v, leak_slope * v)
                         mask |= jnp.where(up, 1 << (zz * 4 + yy * 2 + par), 0)
             pooled[zp, yp] = (mean * 0.125).astype(jnp.bfloat16)
-            bits[zp, yp] = mask
+            lanes = slice(yp * 128, yp * 128 + 128)
+            rows = pl.ds(pl.multiple_of(zp * 128, 128), 128)
+            xt[6, rows, lanes] = mask.astype(jnp.float32).astype(jnp.bfloat16)
 
 
 def first_section(vc, vzl, vzh, vyl, vyh, w1):
@@ -141,8 +144,7 @@
         first_body,
         [
             ((2, 4, 128, 128), jnp.bfloat16),
-            ((2, 4, 128, 128), jnp.int32),
-            ((6, 256, 1280), jnp.bfloat16),
+            ((7, 256, 1280), jnp.bfloat16),
         ],
         [((6, 1280, 256), jnp.bfloat16), ((2, 1024, 256), jnp.float32)],
         [vc, vzl, vzh, vyl, vyh, w1, pair_select()],
@@ -330,7 +332,7 @@
     )
 
 
-def last_body(spg, k2, xt, bits, core, first, filters, total, back, full):
+def last_body(spg, k2, xt, core, first, filters, total, back, full):
     lay_filters(filters, lambda a, b, c: k2[(2 - a) * 9 + (2 - b) * 3 + 2 - c], False)
     conv_rows(spg, slice(0, 512), filters, total, 4)
     for y in range(4):
@@ -339,7 +341,8 @@
             share = grad[:, z * 128 : z * 128 + 128] * 0.125
             up, down = share.astype(jnp.bfloat16), (share * leak_slope).astype(jnp.bfloat16)
             up, down = up.astype(jnp.float32), down.astype(jnp.float32)
-            mask = bits[z, y]
+            mask = xt[6, z * 128 : z * 128 + 128, y * 128 : y * 128 + 128]
+            mask = mask.astype(jnp.float32).astype(jnp.int32)
             for zz in range(2):
                 for yy in range(2):
                     for par in range(2):
@@ -367,7 +370,7 @@
     first[1 - core[0], 832:1024, :] = jnp.zeros((192, 128), jnp.float32)
 
 
-def last_section(spg, k2, xt, bits, core):
+def last_section(spg, k2, xt, core):
     return call(
         last_body,
         [((2, 1024, 128), jnp.float32)],
@@ -377,7 +380,7 @@
             ((4, 1024, 256), jnp.bfloat16),
             ((768, 256), jnp.float32),
         ],
-        [spg, k2, xt, bits, core.reshape(1)],
+        [spg, k2, xt, core.reshape(1)],
         smem=1,
         flops=6_000_000_000,
         vmem=20,
@@ -411,16 +414,17 @@
     )
     filters = lax.all_gather(shares, "sx", axis=0, tiled=True)
     vc = jnp.swapaxes(volume, 2, 3)
-    near, far = partners(after(vc[:1], shares), vc[-1:])
+    near, far = partners(vc[:1], vc[-1:], shares)
     vzl, vzh = jnp.where(core == 0, far, near), jnp.where(core == 0, near, far)
     deep = lambda y: jnp.concatenate([vzl[:, y : y + 1], vc[:, y : y + 1], vzh[:, y : y + 1]])
     vyl, vyh = neighbours(deep(0), deep(7), "sy")
     cot_tall = to_sy(after(cot_rows(jnp.swapaxes(cotangent, 2, 3)), near))
     cot_parts = lax.all_to_all(cot_deep(cot_tall), "sx", 0, 0, tiled=True)
     cot_half = cot_parts.transpose(1, 2, 0, 3, 4).reshape(4, 8, 128, 128)
+    cot_half = lax.optimization_barrier(cot_half)
     cot_near = other_core(jnp.where(core == 0, cot_half[2:], cot_half[:2]))
     w1 = after(pair_filters(first_kernel), cot_tall)
-    pooled, bits, xt = first_section(vc, vzl, vzh, vyl, vyh, w1)
+    pooled, xt = first_section(vc, vzl, vzh, vyl, vyh, w1)
     pyl, pyh = neighbours(pooled[:, :2], pooled[:, 2:], "sy")
     near, far = partners(pooled, pooled)
     ends = jnp.concatenate([pyl, pyh], axis=1)
@@ -434,7 +438,7 @@
     from_other = other_core(maps[1].astype(jnp.bfloat16))
     own = maps[0]
     mine, theirs = own[:, 56:].astype(jnp.bfloat16), from_other[:, 56:]
-    first_part = last_section(spg, k2, xt, bits, core)
+    first_part = last_section(spg, k2, xt, core)
     first_from = other_core(first_part[1].astype(jnp.bfloat16))
     first_half = first_part[0] + first_from.astype(jnp.float32)
     grads = own[:, :56] + from_other[:, :56].astype(jnp.float32)

time: 183 us -> 181 us (0.989)
    unnamed x18 -> x14, local copies, waits for them, and re-layouts: 5.41 us -> 5.06 us
  transfers between devices with their start and end apart: 17 -> 17, of which waited for: 4 -> 4; matrix products, arithmetic and copies ran while one was open for 8% -> 7% of each run, Pallas kernels for 11% -> 11%
where the time goes in v6:
time: 181 us; the launch traced here: 180 us
  blocking collectives  47.9 us (26%)
  starting transfers between devices  47.5 us (26%)
  Pallas kernels  30.6 us (17%)
  waiting for transfers between devices  17.9 us (10%)
  local copies, waits for them, and re-layouts  14.8 us (8%)
  between operations  14.5 us (8%)
  other arithmetic  7.04 us (4%)
    pallas_call x4, Pallas kernels, call(): pl.pallas_call(body, out_shape=[jax.ShapeDtypeStruct(shape, kind) for sha...  30.6 us
    all_to_all x2, blocking collectives, to_sy(): return lax.all_to_all(parts, 'sy', 0, 0, tiled=True)  24.7 us
    all_to_all x1, blocking collectives, to_chips(): lax.all_to_all(parts, 'sx', 0, 0, axis_index_groups=same_core, tiled=True)  23.2 us
    ppermute x3, starting transfers between devices, partners(): lax.ppermute(to_far, 'sx', [(i, i - 1 + 2 * (i % 2)) for i in range(1, 15)])  12.9 us
    ppermute x2, starting transfers between devices, neighbours(): lax.ppermute(last, axis, [(i, i + 1) for i in range(ends)])  9.78 us
    all_to_all x1, waiting for transfers between devices, on_device(): lax.all_to_all(first_grad, 'sx', 0, 0, tiled=True).reshape(2048, 128)[:1728]  8.21 us
    all_to_all x1, starting transfers between devices, on_device(): lax.all_to_all(first_grad, 'sx', 0, 0, tiled=True).reshape(2048, 128)[:1728]  7.96 us
    all_to_all x1, starting transfers between devices, to_sy(): return lax.all_to_all(parts, 'sy', 0, 0, tiled=True)  7.21 us
  transfers between devices with their start and end apart: 17, of which 4 were waited for; matrix products, arithmetic and copies ran while one was open for 7% of the time, Pallas kernels for 11%

profile of v6, /device:TPU:1, one launch (start us, length us, event | category | flops | bytes accessed | tf_op | source)
XLA Modules:
  0.0 180.2 jit_solution(9336326266285642151)
XLA Ops:
  7.2 1.5 pad_maximum_fusion.5
  8.7 1.1 broadcast_select_fusion.2
  9.8 4.9 %collective-permute-start = (bf16[1,8,64,256]{3,2,1,0:T(8,128)(2,1)S(1)}, bf16[1,8,64,256]{3,2,1,0:T(8,128)(2,1)S(1)}, u32[]{:S(2)}, u32[]{:S(2)}) collective-permute-start(bf16[1,8,64,256]{3,2,1,0:T(8,128)(2,1)S(1)} %get-tuple-element.14), channel_id=1, source_target_pairs={{8,16},{16,8},{24,32},{32,24},{40,48},{48,40},{56,64},{64,56},{72,... | collective-permute-start | bytes 786440 | tf_op jit(solution)/shard_map/ppermute | solution.py:20
  14.9 1.0 copy.23
  16.2 0.9 copy-done
  18.1 7.2 %all-to-all-start = ((bf16[8,4,8,8,128]{4,3,2,1,0:T(8,128)(2,1)}), bf16[8,4,8,8,128]{4,3,2,1,0:T(8,128)(2,1)}, u32[]{:S(2)}, u32[]{:S(2)}) async-start(bf16[8,4,8,8,128]{4,3,2,1,0:T(8,128)(2,1)} %copy.24), calls=%async_computation | async-start | bytes 1048576 | tf_op jit(solution)/shard_map/all_to_all | solution.py:41
  26.0 4.9 %collective-permute-start.2 = (bf16[6,1,64,256]{3,2,1,0:T(8,128)(2,1)}, bf16[6,1,64,256]{3,2,1,0:T(8,128)(2,1)S(1)}, u32[]{:S(2)}, u32[]{:S(2)}) collective-permute-start(bf16[6,1,64,256]{3,2,1,0:T(8,128)(2,1)} %pad_maximum_fusion.3), channel_id=1, source_target_pairs={{0,1},{1,2},{2,3},{3,4},{4,5},{5,6},{6,7},{8,9},{9,10},{10,11},{11... | collective-permute-start | bytes 589832 | tf_op jit(solution)/shard_map/ppermute | solution.py:27
  31.6 1.3 collective-permute-start.3
  32.9 3.0 %all-to-all-done = bf16[8,4,8,8,128]{4,3,2,1,0:T(8,128)(2,1)} async-done(((bf16[8,4,8,8,128]{4,3,2,1,0:T(8,128)(2,1)}), bf16[8,4,8,8,128]{4,3,2,1,0:T(8,128)(2,1)}, u32[]{:S(2)}, u32[]{:S(2)}) %all-to-all-start) | async-done | bytes 524320 | tf_op jit(solution)/shard_map/all_to_all | solution.py:41
  35.9 1.3 pad_slice_fusion.1
  37.4 1.2 copy.25
  38.5 5.6 %all-to-all-start.1 = ((bf16[16,4,8,8,128]{4,3,2,1,0:T(8,128)(2,1)}), bf16[16,4,8,8,128]{4,3,2,1,0:T(8,128)(2,1)}, u32[]{:S(2)}, u32[]{:S(2)}) async-start(bf16[16,4,8,8,128]{4,3,2,1,0:T(8,128)(2,1)} %bitcast.73), calls=%async_computation.1 | async-start | bytes 2097152 | tf_op jit(solution)/shard_map/all_to_all | solution.py:422
  44.1 0.9 copy-done.1
  45.1 7.3 %first.1 = (bf16[2,4,128,128]{3,2,1,0:T(8,128)(2,1)S(1)}, bf16[7,256,1280]{2,1,0:T(8,128)(2,1)S(1)}) custom-call(bf16[4,8,64,256]{3,2,1,0:T(8,128)(2,1)S(1)} %bitcast.70, bf16[1,8,64,256]{3,2,1,0:T(8,128)(2,1)S(1)} %get-tuple-element.37.vzl, bf16[1,8,64,256]{3,2,1,0:T(8,128)(2,1)S(1)} %get-tuple-element.36.vzh, ...), custom_call_target="tpu_custom_call" | custom-call | flops 5000000000 | bytes 8257536 | tf_op jit(solution)/shard_map/first/pallas_call | solution.py:72
  52.4 2.1 %copy-done.2 = bf16[7,256,1280]{2,1,0:T(8,128)(2,1)} copy-done((bf16[7,256,1280]{2,1,0:T(8,128)(2,1)}, bf16[7,256,1280]{2,1,0:T(8,128)(2,1)S(1)}, u32[]{:S(2)}) %copy-start.2) | copy-done | bytes 4587544
  54.5 4.9 %collective-permute-start.6 = (bf16[2,2,128,128]{3,2,1,0:T(8,128)(2,1)S(1)}, bf16[2,2,128,128]{3,2,1,0:T(8,128)(2,1)S(1)}, u32[]{:S(2)}, u32[]{:S(2)}) collective-permute-start(bf16[2,2,128,128]{3,2,1,0:T(8,128)(2,1)S(1)} %get-tuple-element.42), channel_id=1, source_target_pairs={{0,1},{1,2},{2,3},{3,4},{4,5},{5,6},{6,7},{8,9},{9,10},{10,11},{11... | collective-permute-start | bytes 393224 | tf_op jit(solution)/shard_map/ppermute | solution.py:27
  59.5 1.3 collective-permute-start.7
  60.9 3.8 %collective-permute-start.5 = (bf16[2,4,128,128]{3,2,1,0:T(8,128)(2,1)S(1)}, bf16[2,4,128,128]{3,2,1,0:T(8,128)(2,1)S(1)}, u32[]{:S(2)}, u32[]{:S(2)}) collective-permute-start(bf16[2,4,128,128]{3,2,1,0:T(8,128)(2,1)S(1)} %get-tuple-element.18.own), channel_id=1, source_target_pairs={{8,16},{16,8},{24,32},{32,24},{40,48},{48,40},{56,64},{64,56},{72,... | collective-permute-start | bytes 786440 | tf_op jit(solution)/shard_map/ppermute | solution.py:20
  64.8 5.6 %collective-permute-done.7 = bf16[2,2,128,128]{3,2,1,0:T(8,128)(2,1)S(1)} collective-permute-done((bf16[2,2,128,128]{3,2,1,0:T(8,128)(2,1)S(1)}, bf16[2,2,128,128]{3,2,1,0:T(8,128)(2,1)S(1)}, u32[]{:S(2)}, u32[]{:S(2)}) %collective-permute-start.7) | collective-permute-done | bytes 131104 | tf_op jit(solution)/shard_map/ppermute | solution.py:28
  70.4 4.2 %collective-permute-start.9 = (bf16[2,4,128,128]{3,2,1,0:T(8,128)(2,1)S(1)}, bf16[2,4,128,128]{3,2,1,0:T(8,128)(2,1)S(1)}, u32[]{:S(2)}, u32[]{:S(2)}) collective-permute-start(bf16[2,4,128,128]{3,2,1,0:T(8,128)(2,1)S(1)} %constant_dynamic-update-slice_fusion.ends), channel_id=1, source_target_pairs={{8,16},{16,8},{24,32},{32,24},{40,48},{48,40},{56,64},{64,56},{72,... | collective-permute-start | bytes 786440 | tf_op jit(solution)/shard_map/ppermute | solution.py:20
  74.7 1.5 copy_bitcast_fusion.half
  77.5 1.6 fusion.10
  79.6 4.7 %cot.1 = (f32[6,128,512]{2,1,0:T(8,128)S(1)}, bf16[512,768]{1,0:T(8,128)(2,1)S(1)}) custom-call(bf16[4,8,128,128]{3,2,1,0:T(8,128)(2,1)S(1)} %copy_bitcast_fusion.half, bf16[2,8,128,128]{3,2,1,0:T(8,128)(2,1)S(1)} %collective-permute-done.10.near, bf16[27,128,128]{2,1,0:T(8,128)(2,1)S(1)} %get-tuple-element.54.k3, s32[1]{0:T(128)} %bitcast.21.core), custom_call_target="tpu_custom_call" | custom-call | flops 3600000000 | bytes 4816900 | tf_op jit(solution)/shard_map/cot/pallas_call | solution.py:72
  84.3 11.0 %mid.1 = (f32[2,8,64,8,128]{4,3,2,1,0:T(8,128)S(1)}, bf16[6,128,512]{2,1,0:T(8,128)(2,1)S(1)}) custom-call(bf16[2,4,128,128]{3,2,1,0:T(8,128)(2,1)S(1)} %get-tuple-element.18.own, bf16[2,4,128,128]{3,2,1,0:T(8,128)(2,1)S(1)} %collective-permute-done.4.near, bf16[2,4,128,128]{3,2,1,0:T(8,128)(2,1)S(1)} %collective-permute-done.5.far, ...), custom_call_target="tpu_custom_call" | custom-call | flops 7000000000 | bytes 10682388 | tf_op jit(solution)/shard_map/mid/pallas_call | solution.py:72
  95.7 7.6 %last.1 = f32[2,1024,128]{2,1,0:T(8,128)S(1)} custom-call(bf16[6,128,512]{2,1,0:T(8,128)(2,1)S(1)} %get-tuple-element.22.spg, bf16[27,128,128]{2,1,0:T(8,128)(2,1)S(1)} %get-tuple-element.53.k2, bf16[7,256,1280]{2,1,0:T(8,128)(2,1)S(1)} %bitcast.72, s32[1]{0:T(128)} %bitcast.21.core), custom_call_target="tpu_custom_call" | custom-call | flops 6000000000 | bytes 7307268 | tf_op jit(solution)/shard_map/last/pallas_call | solution.py:72
  104.0 1.0 collective-permute-done.12
  105.6 23.2 %all_to_all.30 = bf16[8,88,8,128]{3,2,1,0:T(8,128)(2,1)S(1)} all-to-all(bf16[8,88,8,128]{3,2,1,0:T(8,128)(2,1)S(1)} %pad_maximum_fusion), channel_id=1, replica_groups={{0,16,32,48,64,80,96,112},{8,24,40,56,72,88,104,120},{1,17,33,49,65,81,..., dimensions={0} | all-to-all | bytes 2883584 | tf_op jit(solution)/shard_map/all_to_all | solution.py:37
  129.0 15.3 %all_to_all.31 = bf16[8,25,8,128]{3,2,1,0:T(8,128)(2,1)S(1)} all-to-all(bf16[8,25,8,128]{3,2,1,0:T(8,128)(2,1)S(1)} %pad_maximum_fusion.2), channel_id=1, replica_groups=mesh['sx'=16,'sy'=8] {'sy'}, dimensions={0} | all-to-all | bytes 819200 | tf_op jit(solution)/shard_map/all_to_all | solution.py:41
  144.3 9.4 %all_to_all.32 = bf16[8,9,8,128]{3,2,1,0:T(8,128)(2,1)S(1)} all-to-all(bf16[8,9,8,128]{3,2,1,0:T(8,128)(2,1)S(1)} %broadcast_in_dim.17), channel_id=1, replica_groups=mesh['sx'=16,'sy'=8] {'sy'}, dimensions={0} | all-to-all | bytes 294912 | tf_op jit(solution)/shard_map/all_to_all | solution.py:41
  154.7 8.0 %all-to-all-start.5 = ((bf16[16,128,128]{2,1,0:T(8,128)(2,1)}), bf16[16,128,128]{2,1,0:T(8,128)(2,1)S(1)}, u32[]{:S(2)}, u32[]{:S(2)}) async-start(bf16[16,128,128]{2,1,0:T(8,128)(2,1)} %broadcast_in_dim.19), calls=%async_computation.5 | async-start | bytes 1048576 | tf_op jit(solution)/shard_map/all_to_all | solution.py:469
  164.1 8.2 %all-to-all-done.5 = bf16[16,128,128]{2,1,0:T(8,128)(2,1)S(1)} async-done(((bf16[16,128,128]{2,1,0:T(8,128)(2,1)}), bf16[16,128,128]{2,1,0:T(8,128)(2,1)S(1)}, u32[]{:S(2)}, u32[]{:S(2)}) %all-to-all-start.5) | async-done | bytes 524320 | tf_op jit(solution)/shard_map/all_to_all | solution.py:469
  172.3 1.0 convert.16
  (69 shorter events, 9.2 us)
Async XLA Ops:
  7.2 70.4 %all-gather.2.cloned.1.call-start = ((), (), s32[]{:S(2)}) async-start(), calls=%async_computation.6 | async-start | bytes 1880064 | tf_op jit(solution)/shard_map/all_gather | solution.py:415
  9.8 15.4 %collective-permute-start = (bf16[1,8,64,256]{3,2,1,0:T(8,128)(2,1)S(1)}, bf16[1,8,64,256]{3,2,1,0:T(8,128)(2,1)S(1)}, u32[]{:S(2)}, u32[]{:S(2)}) collective-permute-start(bf16[1,8,64,256]{3,2,1,0:T(8,128)(2,1)S(1)} %get-tuple-element.14), channel_id=1, source_target_pairs={{8,16},{16,8},{24,32},{32,24},{40,48},{48,40},{56,64},{64,56},{72,... | collective-permute-start | bytes 786440 | tf_op jit(solution)/shard_map/ppermute | solution.py:20
  14.8 1.4 copy-start.3
  14.8 2.4 %collective-permute-start.1 = (bf16[1,8,64,256]{3,2,1,0:T(8,128)(2,1)S(1)}, bf16[1,8,64,256]{3,2,1,0:T(8,128)(2,1)S(1)}, u32[]{:S(2)}, u32[]{:S(2)}) collective-permute-start(bf16[1,8,64,256]{3,2,1,0:T(8,128)(2,1)S(1)} %get-tuple-element.15), channel_id=1, source_target_pairs={{0,8},{8,0},{16,24},{24,16},{32,40},{40,32},{48,56},{56,48},{64,72... | collective-permute-start | bytes 786440 | tf_op jit(solution)/shard_map/ppermute | solution.py:19
  16.0 1.2 copy-start
  18.1 17.9 %all-to-all-start = ((bf16[8,4,8,8,128]{4,3,2,1,0:T(8,128)(2,1)}), bf16[8,4,8,8,128]{4,3,2,1,0:T(8,128)(2,1)}, u32[]{:S(2)}, u32[]{:S(2)}) async-start(bf16[8,4,8,8,128]{4,3,2,1,0:T(8,128)(2,1)} %copy.24), calls=%async_computation | async-start | bytes 1048576 | tf_op jit(solution)/shard_map/all_to_all | solution.py:41
  26.0 18.1 %collective-permute-start.2 = (bf16[6,1,64,256]{3,2,1,0:T(8,128)(2,1)}, bf16[6,1,64,256]{3,2,1,0:T(8,128)(2,1)S(1)}, u32[]{:S(2)}, u32[]{:S(2)}) collective-permute-start(bf16[6,1,64,256]{3,2,1,0:T(8,128)(2,1)} %pad_maximum_fusion.3), channel_id=1, source_target_pairs={{0,1},{1,2},{2,3},{3,4},{4,5},{5,6},{6,7},{8,9},{9,10},{10,11},{11... | collective-permute-start | bytes 589832 | tf_op jit(solution)/shard_map/ppermute | solution.py:27
  31.6 12.5 %collective-permute-start.3 = (bf16[6,1,64,256]{3,2,1,0:T(8,128)(2,1)}, bf16[6,1,64,256]{3,2,1,0:T(8,128)(2,1)S(1)}, u32[]{:S(2)}, u32[]{:S(2)}) collective-permute-start(bf16[6,1,64,256]{3,2,1,0:T(8,128)(2,1)} %pad_maximum_fusion.4), channel_id=1, source_target_pairs={{1,0},{2,1},{3,2},{4,3},{5,4},{6,5},{7,6},{9,8},{10,9},{11,10},{12... | collective-permute-start | bytes 589832 | tf_op jit(solution)/shard_map/ppermute | solution.py:28
  38.5 36.1 %all-to-all-start.1 = ((bf16[16,4,8,8,128]{4,3,2,1,0:T(8,128)(2,1)}), bf16[16,4,8,8,128]{4,3,2,1,0:T(8,128)(2,1)}, u32[]{:S(2)}, u32[]{:S(2)}) async-start(bf16[16,4,8,8,128]{4,3,2,1,0:T(8,128)(2,1)} %bitcast.73), calls=%async_computation.1 | async-start | bytes 2097152 | tf_op jit(solution)/shard_map/all_to_all | solution.py:422
  44.1 1.0 copy-start.1
  52.4 2.1 %copy-start.2 = (bf16[7,256,1280]{2,1,0:T(8,128)(2,1)}, bf16[7,256,1280]{2,1,0:T(8,128)(2,1)S(1)}, u32[]{:S(2)}) copy-start(bf16[7,256,1280]{2,1,0:T(8,128)(2,1)S(1)} %get-tuple-element.23.xt) | copy-start | bytes 13762564
  54.5 10.2 %collective-permute-start.6 = (bf16[2,2,128,128]{3,2,1,0:T(8,128)(2,1)S(1)}, bf16[2,2,128,128]{3,2,1,0:T(8,128)(2,1)S(1)}, u32[]{:S(2)}, u32[]{:S(2)}) collective-permute-start(bf16[2,2,128,128]{3,2,1,0:T(8,128)(2,1)S(1)} %get-tuple-element.42), channel_id=1, source_target_pairs={{0,1},{1,2},{2,3},{3,4},{4,5},{5,6},{6,7},{8,9},{9,10},{10,11},{11... | collective-permute-start | bytes 393224 | tf_op jit(solution)/shard_map/ppermute | solution.py:27
  59.5 10.9 %collective-permute-start.7 = (bf16[2,2,128,128]{3,2,1,0:T(8,128)(2,1)S(1)}, bf16[2,2,128,128]{3,2,1,0:T(8,128)(2,1)S(1)}, u32[]{:S(2)}, u32[]{:S(2)}) collective-permute-start(bf16[2,2,128,128]{3,2,1,0:T(8,128)(2,1)S(1)} %get-tuple-element.41), channel_id=1, source_target_pairs={{1,0},{2,1},{3,2},{4,3},{5,4},{6,5},{7,6},{9,8},{10,9},{11,10},{12... | collective-permute-start | bytes 393224 | tf_op jit(solution)/shard_map/ppermute | solution.py:28
  60.9 23.4 %collective-permute-start.5 = (bf16[2,4,128,128]{3,2,1,0:T(8,128)(2,1)S(1)}, bf16[2,4,128,128]{3,2,1,0:T(8,128)(2,1)S(1)}, u32[]{:S(2)}, u32[]{:S(2)}) collective-permute-start(bf16[2,4,128,128]{3,2,1,0:T(8,128)(2,1)S(1)} %get-tuple-element.18.own), channel_id=1, source_target_pairs={{8,16},{16,8},{24,32},{32,24},{40,48},{48,40},{56,64},{64,56},{72,... | collective-permute-start | bytes 786440 | tf_op jit(solution)/shard_map/ppermute | solution.py:20
  64.7 19.6 %collective-permute-start.4 = (bf16[2,4,128,128]{3,2,1,0:T(8,128)(2,1)S(1)}, bf16[2,4,128,128]{3,2,1,0:T(8,128)(2,1)S(1)}, u32[]{:S(2)}, u32[]{:S(2)}) collective-permute-start(bf16[2,4,128,128]{3,2,1,0:T(8,128)(2,1)S(1)} %get-tuple-element.18.own), channel_id=1, source_target_pairs={{0,8},{8,0},{16,24},{24,16},{32,40},{40,32},{48,56},{56,48},{64,72... | collective-permute-start | bytes 786440 | tf_op jit(solution)/shard_map/ppermute | solution.py:19
  70.4 13.9 %collective-permute-start.9 = (bf16[2,4,128,128]{3,2,1,0:T(8,128)(2,1)S(1)}, bf16[2,4,128,128]{3,2,1,0:T(8,128)(2,1)S(1)}, u32[]{:S(2)}, u32[]{:S(2)}) collective-permute-start(bf16[2,4,128,128]{3,2,1,0:T(8,128)(2,1)S(1)} %constant_dynamic-update-slice_fusion.ends), channel_id=1, source_target_pairs={{8,16},{16,8},{24,32},{32,24},{40,48},{48,40},{56,64},{64,56},{72,... | collective-permute-start | bytes 786440 | tf_op jit(solution)/shard_map/ppermute | solution.py:20
  74.6 9.7 %collective-permute-start.8 = (bf16[2,4,128,128]{3,2,1,0:T(8,128)(2,1)S(1)}, bf16[2,4,128,128]{3,2,1,0:T(8,128)(2,1)S(1)}, u32[]{:S(2)}, u32[]{:S(2)}) collective-permute-start(bf16[2,4,128,128]{3,2,1,0:T(8,128)(2,1)S(1)} %constant_dynamic-update-slice_fusion.ends), channel_id=1, source_target_pairs={{0,8},{8,0},{16,24},{24,16},{32,40},{40,32},{48,56},{56,48},{64,72... | collective-permute-start | bytes 786440 | tf_op jit(solution)/shard_map/ppermute | solution.py:19
  77.0 2.5 %collective-permute-start.10 = (bf16[2,8,128,128]{3,2,1,0:T(8,128)(2,1)}, bf16[2,8,128,128]{3,2,1,0:T(8,128)(2,1)S(1)}, u32[]{:S(2)}, u32[]{:S(2)}) collective-permute-start(bf16[2,8,128,128]{3,2,1,0:T(8,128)(2,1)} %slice_select_fusion), channel_id=1, source_target_pairs={{0,8},{8,0},{16,24},{24,16},{32,40},{40,32},{48,56},{56,48},{64,72... | collective-permute-start | bytes 1572872 | tf_op jit(solution)/shard_map/ppermute | solution.py:33
  79.6 16.1 %slice-start = ((s8[4587520]{0:T(1024)(128)(4,1)}), s8[4194304]{0:T(1024)(128)(4,1)S(1)}, s32[]{:S(2)}) async-start(s8[4587520]{0:T(1024)(128)(4,1)} %bitcast.71), calls=%async_computation.7 | async-start | bytes 8388608
  84.3 11.4 %slice-start.1 = ((s8[4587520]{0:T(1024)(128)(4,1)}), s8[393216]{0:T(1024)(128)(4,1)S(1)}, s32[]{:S(2)}) async-start(s8[4587520]{0:T(1024)(128)(4,1)} %bitcast.71), calls=%async_computation.8 | async-start | bytes 786432
  95.5 9.6 %collective-permute-start.11 = (bf16[8,64,8,128]{3,2,1,0:T(8,128)(2,1)S(1)}, bf16[8,64,8,128]{3,2,1,0:T(8,128)(2,1)S(1)}, u32[]{:S(2)}, u32[]{:S(2)}) collective-permute-start(bf16[8,64,8,128]{3,2,1,0:T(8,128)(2,1)S(1)} %fusion.1), channel_id=1, source_target_pairs={{0,8},{8,0},{16,24},{24,16},{32,40},{40,32},{48,56},{56,48},{64,72... | collective-permute-start | bytes 3145736 | tf_op jit(solution)/shard_map/ppermute | solution.py:33
  103.3 1.7 collective-permute-start.12
  154.7 17.6 %all-to-all-start.5 = ((bf16[16,128,128]{2,1,0:T(8,128)(2,1)}), bf16[16,128,128]{2,1,0:T(8,128)(2,1)S(1)}, u32[]{:S(2)}, u32[]{:S(2)}) async-start(bf16[16,128,128]{2,1,0:T(8,128)(2,1)} %broadcast_in_dim.19), calls=%async_computation.5 | async-start | bytes 1048576 | tf_op jit(solution)/shard_map/all_to_all | solution.py:469
Sparse Core Ops, SparseCore 0:
  10.3 48.5 all-gather.1

commit v7 on v6

--- a/solution.py
+++ b/solution.py
@@ -82,12 +82,11 @@
 
 
 def pair_select():
-    sel = np.zeros((256, 4, 128), np.float32)
-    for k, offset in enumerate((0, 1, -1, 2)):
-        for p in range(128):
-            if 0 <= 2 * p + offset < 256:
-                sel[2 * p + offset, k, p] = 1
-    return jnp.asarray(sel.reshape(256, 512), jnp.bfloat16)
+    cell = lax.broadcasted_iota(jnp.int32, (256, 512), 0)
+    lane = lax.broadcasted_iota(jnp.int32, (256, 512), 1)
+    k = lane // 128
+    offset = jnp.where(k == 2, -1, jnp.where(k == 3, 2, k))
+    return jnp.where(cell == lane % 128 * 2 + offset, 1.0, 0.0).astype(jnp.bfloat16)
 
 
 def pair_filters(kernel):
@@ -98,7 +97,8 @@
     return jnp.concatenate([even, odd], axis=2)
 
 
-def first_body(vc, vzl, vzh, vyl, vyh, w1, sel, pooled, xt, xc, acc):
+def first_body(vc, vzl, vzh, vyl, vyh, w1, pooled, xt, xc, acc, sel):
+    sel[...] = pair_select()
     for z in range(6):
         rows = vzl[0] if z == 0 else vzh[0] if z == 5 else vc[z - 1]
         got = dot(rows.reshape(512, 256), sel[...]).astype(jnp.bfloat16)
@@ -146,8 +146,12 @@
             ((2, 4, 128, 128), jnp.bfloat16),
             ((7, 256, 1280), jnp.bfloat16),
         ],
-        [((6, 1280, 256), jnp.bfloat16), ((2, 1024, 256), jnp.float32)],
-        [vc, vzl, vzh, vyl, vyh, w1, pair_select()],
+        [
+            ((6, 1280, 256), jnp.bfloat16),
+            ((2, 1024, 256), jnp.float32),
+            ((256, 512), jnp.bfloat16),
+        ],
+        [vc, vzl, vzh, vyl, vyh, w1],
         flops=5_000_000_000,
         vmem=18,
         name="first",
@@ -396,9 +400,11 @@
 
 
 def cot_deep(values):
-    wide = jnp.pad(values.reshape(32, 8, 8, 128), ((2, 2), (0, 0), (0, 0), (0, 0)))
-    wide = wide.reshape(9, 4, 8, 8, 128)
-    return jnp.stack([wide[:8], wide[1:]], axis=1).reshape(16, 4, 8, 8, 128)
+    own = values.reshape(8, 4, 8, 8, 128)
+    ends = ((0, 0),) * 4
+    below = jnp.pad(own[:7, 2:], ((1, 0),) + ends)
+    above = jnp.pad(own[1:, :2], ((0, 1),) + ends)
+    return jnp.concatenate([below, own, above], axis=1).reshape(16, 4, 8, 8, 128)
 
 
 def after(values, *done):

time: 181 us -> 181 us (level)
  local copies, waits for them, and re-layouts: 14.8 us -> 12.4 us
  other arithmetic: 7.04 us -> 9.09 us
    concatenate x0 -> x1, other arithmetic: none -> 2.15 us  [cot_deep(): jnp.concatenate([below, own, above], axis=1).reshape(16, 4, 8, 8, 128)]
    unnamed x14 -> x12, local copies, waits for them, and re-layouts: 5.06 us -> 4.08 us
  transfers between devices with their start and end apart: 17 -> 17, of which waited for: 4 -> 4; matrix products, arithmetic and copies ran while one was open for 7% -> 8% of each run, Pallas kernels for 11% -> 11%
where the time goes in v7:
time: 181 us; the launch traced here: 180 us
  blocking collectives  47.7 us (26%)
  starting transfers between devices  47 us (26%)
  Pallas kernels  30.6 us (17%)
  waiting for transfers between devices  18.6 us (10%)
  between operations  14.5 us (8%)
  local copies, waits for them, and re-layouts  12.4 us (7%)
  other arithmetic  9.09 us (5%)
    pallas_call x4, Pallas kernels, call(): pl.pallas_call(body, out_shape=[jax.ShapeDtypeStruct(shape, kind) for sha...  30.6 us
    all_to_all x2, blocking collectives, to_sy(): return lax.all_to_all(parts, 'sy', 0, 0, tiled=True)  24.5 us
    all_to_all x1, blocking collectives, to_chips(): lax.all_to_all(parts, 'sx', 0, 0, axis_index_groups=same_core, tiled=True)  23.2 us
    ppermute x3, starting transfers between devices, partners(): lax.ppermute(to_far, 'sx', [(i, i - 1 + 2 * (i % 2)) for i in range(1, 15)])  12.4 us
    ppermute x2, starting transfers between devices, neighbours(): lax.ppermute(last, axis, [(i, i + 1) for i in range(ends)])  9.8 us
    all_to_all x1, waiting for transfers between devices, on_device(): lax.all_to_all(first_grad, 'sx', 0, 0, tiled=True).reshape(2048, 128)[:1728]  8.21 us
    all_to_all x1, starting transfers between devices, on_device(): lax.all_to_all(first_grad, 'sx', 0, 0, tiled=True).reshape(2048, 128)[:1728]  7.96 us
    all_to_all x1, starting transfers between devices, to_sy(): return lax.all_to_all(parts, 'sy', 0, 0, tiled=True)  7.21 us
  transfers between devices with their start and end apart: 17, of which 4 were waited for; matrix products, arithmetic and copies ran while one was open for 8% of the time, Pallas kernels for 11%

profile of v7, /device:TPU:1, one launch (start us, length us, event | category | flops | bytes accessed | tf_op | source)
XLA Modules:
  0.0 179.8 jit_solution(3793235853203730702)
XLA Ops:
  7.2 1.5 pad_maximum_fusion.4
  8.7 1.1 broadcast_select_fusion.2
  9.8 5.1 %collective-permute-start = (bf16[1,8,64,256]{3,2,1,0:T(8,128)(2,1)S(1)}, bf16[1,8,64,256]{3,2,1,0:T(8,128)(2,1)S(1)}, u32[]{:S(2)}, u32[]{:S(2)}) collective-permute-start(bf16[1,8,64,256]{3,2,1,0:T(8,128)(2,1)S(1)} %get-tuple-element.14), channel_id=1, source_target_pairs={{8,16},{16,8},{24,32},{32,24},{40,48},{48,40},{56,64},{64,56},{72,... | collective-permute-start | bytes 786440 | tf_op jit(solution)/shard_map/ppermute | solution.py:20
  15.0 1.0 copy.22
  16.4 0.9 copy-done
  18.1 7.2 %all-to-all-start = ((bf16[8,4,8,8,128]{4,3,2,1,0:T(8,128)(2,1)}), bf16[8,4,8,8,128]{4,3,2,1,0:T(8,128)(2,1)}, u32[]{:S(2)}, u32[]{:S(2)}) async-start(bf16[8,4,8,8,128]{4,3,2,1,0:T(8,128)(2,1)} %copy.23), calls=%async_computation | async-start | bytes 1048576 | tf_op jit(solution)/shard_map/all_to_all | solution.py:41
  26.1 4.9 %collective-permute-start.2 = (bf16[6,1,64,256]{3,2,1,0:T(8,128)(2,1)}, bf16[6,1,64,256]{3,2,1,0:T(8,128)(2,1)S(1)}, u32[]{:S(2)}, u32[]{:S(2)}) collective-permute-start(bf16[6,1,64,256]{3,2,1,0:T(8,128)(2,1)} %pad_maximum_fusion.2), channel_id=1, source_target_pairs={{0,1},{1,2},{2,3},{3,4},{4,5},{5,6},{6,7},{8,9},{9,10},{10,11},{11... | collective-permute-start | bytes 589832 | tf_op jit(solution)/shard_map/ppermute | solution.py:27
  31.7 1.3 collective-permute-start.3
  33.0 3.0 %all-to-all-done = bf16[8,4,8,8,128]{4,3,2,1,0:T(8,128)(2,1)} async-done(((bf16[8,4,8,8,128]{4,3,2,1,0:T(8,128)(2,1)}), bf16[8,4,8,8,128]{4,3,2,1,0:T(8,128)(2,1)}, u32[]{:S(2)}, u32[]{:S(2)}) %all-to-all-start) | async-done | bytes 524320 | tf_op jit(solution)/shard_map/all_to_all | solution.py:41
  36.0 1.1 fusion.16
  37.1 2.2 %fusion.3 = bf16[8,8,8,8,128]{4,3,2,1,0:T(8,128)(2,1)} fusion(bf16[7,2,8,8,128]{4,3,2,1,0:T(8,128)(2,1)S(1)} %get-tuple-element.35, bf16[7,2,8,8,128]{4,3,2,1,0:T(8,128)(2,1)S(1)} %get-tuple-element.34, bf16[8,4,8,8,128]{4,3,2,1,0:T(8,128)(2,1)} %all-to-all-done), kind=kLoop, calls=%fused_computation.10 | loop fusion | flops 5242880 | bytes 2031616 | tf_op jit(solution)/shard_map/concatenate | solution.py:407
  39.3 5.6 %all-to-all-start.1 = ((bf16[16,4,8,8,128]{4,3,2,1,0:T(8,128)(2,1)}), bf16[16,4,8,8,128]{4,3,2,1,0:T(8,128)(2,1)}, u32[]{:S(2)}, u32[]{:S(2)}) async-start(bf16[16,4,8,8,128]{4,3,2,1,0:T(8,128)(2,1)} %bitcast.70), calls=%async_computation.1 | async-start | bytes 2097152 | tf_op jit(solution)/shard_map/all_to_all | solution.py:428
  44.9 7.3 %first.1 = (bf16[2,4,128,128]{3,2,1,0:T(8,128)(2,1)S(1)}, bf16[7,256,1280]{2,1,0:T(8,128)(2,1)S(1)}) custom-call(bf16[4,8,64,256]{3,2,1,0:T(8,128)(2,1)S(1)} %bitcast.67, bf16[1,8,64,256]{3,2,1,0:T(8,128)(2,1)S(1)} %get-tuple-element.37.vzl, bf16[1,8,64,256]{3,2,1,0:T(8,128)(2,1)S(1)} %get-tuple-element.36.vzh, ...), custom_call_target="tpu_custom_call" | custom-call | flops 5000000000 | bytes 7995392 | tf_op jit(solution)/shard_map/first/pallas_call | solution.py:72
  52.2 2.1 %copy-done.1 = bf16[7,256,1280]{2,1,0:T(8,128)(2,1)} copy-done((bf16[7,256,1280]{2,1,0:T(8,128)(2,1)}, bf16[7,256,1280]{2,1,0:T(8,128)(2,1)S(1)}, u32[]{:S(2)}) %copy-start.1) | copy-done | bytes 4587544
  54.3 4.9 %collective-permute-start.6 = (bf16[2,2,128,128]{3,2,1,0:T(8,128)(2,1)S(1)}, bf16[2,2,128,128]{3,2,1,0:T(8,128)(2,1)S(1)}, u32[]{:S(2)}, u32[]{:S(2)}) collective-permute-start(bf16[2,2,128,128]{3,2,1,0:T(8,128)(2,1)S(1)} %get-tuple-element.42), channel_id=1, source_target_pairs={{0,1},{1,2},{2,3},{3,4},{4,5},{5,6},{6,7},{8,9},{9,10},{10,11},{11... | collective-permute-start | bytes 393224 | tf_op jit(solution)/shard_map/ppermute | solution.py:27
  59.3 1.3 collective-permute-start.7
  60.6 3.2 %collective-permute-start.5 = (bf16[2,4,128,128]{3,2,1,0:T(8,128)(2,1)S(1)}, bf16[2,4,128,128]{3,2,1,0:T(8,128)(2,1)S(1)}, u32[]{:S(2)}, u32[]{:S(2)}) collective-permute-start(bf16[2,4,128,128]{3,2,1,0:T(8,128)(2,1)S(1)} %get-tuple-element.18.own), channel_id=1, source_target_pairs={{8,16},{16,8},{24,32},{32,24},{40,48},{48,40},{56,64},{64,56},{72,... | collective-permute-start | bytes 786440 | tf_op jit(solution)/shard_map/ppermute | solution.py:20
  64.0 6.3 %collective-permute-done.7 = bf16[2,2,128,128]{3,2,1,0:T(8,128)(2,1)S(1)} collective-permute-done((bf16[2,2,128,128]{3,2,1,0:T(8,128)(2,1)S(1)}, bf16[2,2,128,128]{3,2,1,0:T(8,128)(2,1)S(1)}, u32[]{:S(2)}, u32[]{:S(2)}) %collective-permute-start.7) | collective-permute-done | bytes 131104 | tf_op jit(solution)/shard_map/ppermute | solution.py:28
  70.3 4.1 %collective-permute-start.9 = (bf16[2,4,128,128]{3,2,1,0:T(8,128)(2,1)S(1)}, bf16[2,4,128,128]{3,2,1,0:T(8,128)(2,1)S(1)}, u32[]{:S(2)}, u32[]{:S(2)}) collective-permute-start(bf16[2,4,128,128]{3,2,1,0:T(8,128)(2,1)S(1)} %constant_dynamic-update-slice_fusion.ends), channel_id=1, source_target_pairs={{8,16},{16,8},{24,32},{32,24},{40,48},{48,40},{56,64},{64,56},{72,... | collective-permute-start | bytes 786440 | tf_op jit(solution)/shard_map/ppermute | solution.py:20
  74.6 1.5 copy_bitcast_fusion.half
  77.4 1.6 fusion.14
  79.5 4.6 %cot.1 = (f32[6,128,512]{2,1,0:T(8,128)S(1)}, bf16[512,768]{1,0:T(8,128)(2,1)S(1)}) custom-call(bf16[4,8,128,128]{3,2,1,0:T(8,128)(2,1)S(1)} %copy_bitcast_fusion.half, bf16[2,8,128,128]{3,2,1,0:T(8,128)(2,1)S(1)} %collective-permute-done.10.near, bf16[27,128,128]{2,1,0:T(8,128)(2,1)S(1)} %get-tuple-element.54.k3, s32[1]{0:T(128)} %bitcast.18.core), custom_call_target="tpu_custom_call" | custom-call | flops 3600000000 | bytes 4816900 | tf_op jit(solution)/shard_map/cot/pallas_call | solution.py:72
  84.2 11.0 %mid.1 = (f32[2,8,64,8,128]{4,3,2,1,0:T(8,128)S(1)}, bf16[6,128,512]{2,1,0:T(8,128)(2,1)S(1)}) custom-call(bf16[2,4,128,128]{3,2,1,0:T(8,128)(2,1)S(1)} %get-tuple-element.18.own, bf16[2,4,128,128]{3,2,1,0:T(8,128)(2,1)S(1)} %collective-permute-done.4.near, bf16[2,4,128,128]{3,2,1,0:T(8,128)(2,1)S(1)} %collective-permute-done.5.far, ...), custom_call_target="tpu_custom_call" | custom-call | flops 7000000000 | bytes 10682388 | tf_op jit(solution)/shard_map/mid/pallas_call | solution.py:72
  95.5 7.6 %last.1 = f32[2,1024,128]{2,1,0:T(8,128)S(1)} custom-call(bf16[6,128,512]{2,1,0:T(8,128)(2,1)S(1)} %get-tuple-element.22.spg, bf16[27,128,128]{2,1,0:T(8,128)(2,1)S(1)} %get-tuple-element.53.k2, bf16[7,256,1280]{2,1,0:T(8,128)(2,1)S(1)} %bitcast.69, s32[1]{0:T(128)} %bitcast.18.core), custom_call_target="tpu_custom_call" | custom-call | flops 6000000000 | bytes 7307268 | tf_op jit(solution)/shard_map/last/pallas_call | solution.py:72
  103.9 1.0 collective-permute-done.12
  105.4 23.2 %all_to_all.30 = bf16[8,88,8,128]{3,2,1,0:T(8,128)(2,1)S(1)} all-to-all(bf16[8,88,8,128]{3,2,1,0:T(8,128)(2,1)S(1)} %pad_maximum_fusion), channel_id=1, replica_groups={{0,16,32,48,64,80,96,112},{8,24,40,56,72,88,104,120},{1,17,33,49,65,81,..., dimensions={0} | all-to-all | bytes 2883584 | tf_op jit(solution)/shard_map/all_to_all | solution.py:37
  128.9 15.1 %all_to_all.31 = bf16[8,25,8,128]{3,2,1,0:T(8,128)(2,1)S(1)} all-to-all(bf16[8,25,8,128]{3,2,1,0:T(8,128)(2,1)S(1)} %pad_maximum_fusion.1), channel_id=1, replica_groups=mesh['sx'=16,'sy'=8] {'sy'}, dimensions={0} | all-to-all | bytes 819200 | tf_op jit(solution)/shard_map/all_to_all | solution.py:41
  144.0 9.4 %all_to_all.32 = bf16[8,9,8,128]{3,2,1,0:T(8,128)(2,1)S(1)} all-to-all(bf16[8,9,8,128]{3,2,1,0:T(8,128)(2,1)S(1)} %broadcast_in_dim.17), channel_id=1, replica_groups=mesh['sx'=16,'sy'=8] {'sy'}, dimensions={0} | all-to-all | bytes 294912 | tf_op jit(solution)/shard_map/all_to_all | solution.py:41
  153.4 0.9 broadcast_in_dim.19
  154.3 8.0 %all-to-all-start.5 = ((bf16[16,128,128]{2,1,0:T(8,128)(2,1)}), bf16[16,128,128]{2,1,0:T(8,128)(2,1)S(1)}, u32[]{:S(2)}, u32[]{:S(2)}) async-start(bf16[16,128,128]{2,1,0:T(8,128)(2,1)} %broadcast_in_dim.19), calls=%async_computation.5 | async-start | bytes 1048576 | tf_op jit(solution)/shard_map/all_to_all | solution.py:475
  163.7 8.2 %all-to-all-done.5 = bf16[16,128,128]{2,1,0:T(8,128)(2,1)S(1)} async-done(((bf16[16,128,128]{2,1,0:T(8,128)(2,1)}), bf16[16,128,128]{2,1,0:T(8,128)(2,1)S(1)}, u32[]{:S(2)}, u32[]{:S(2)}) %all-to-all-start.5) | async-done | bytes 524320 | tf_op jit(solution)/shard_map/all_to_all | solution.py:475
  172.0 1.0 convert.16
  (66 shorter events, 8.2 us)
Async XLA Ops:
  7.2 70.2 %all-gather.2.cloned.1.call-start = ((), (), s32[]{:S(2)}) async-start(), calls=%async_computation.6 | async-start | bytes 1880064 | tf_op jit(solution)/shard_map/all_gather | solution.py:421
  9.8 6.5 %copy-start.2 = (bf16[4,32,128,8]{2,3,1,0:T(8,128)(2,1)S(1)}, bf16[4,32,128,8]{2,3,1,0:T(8,128)(2,1)}, u32[]{:S(2)}) copy-start(bf16[4,32,128,8]{2,3,1,0:T(8,128)(2,1)} %param.9) | copy-start | bytes 786436
  9.8 15.5 %collective-permute-start = (bf16[1,8,64,256]{3,2,1,0:T(8,128)(2,1)S(1)}, bf16[1,8,64,256]{3,2,1,0:T(8,128)(2,1)S(1)}, u32[]{:S(2)}, u32[]{:S(2)}) collective-permute-start(bf16[1,8,64,256]{3,2,1,0:T(8,128)(2,1)S(1)} %get-tuple-element.14), channel_id=1, source_target_pairs={{8,16},{16,8},{24,32},{32,24},{40,48},{48,40},{56,64},{64,56},{72,... | collective-permute-start | bytes 786440 | tf_op jit(solution)/shard_map/ppermute | solution.py:20
  14.9 2.4 %collective-permute-start.1 = (bf16[1,8,64,256]{3,2,1,0:T(8,128)(2,1)S(1)}, bf16[1,8,64,256]{3,2,1,0:T(8,128)(2,1)S(1)}, u32[]{:S(2)}, u32[]{:S(2)}) collective-permute-start(bf16[1,8,64,256]{3,2,1,0:T(8,128)(2,1)S(1)} %get-tuple-element.15), channel_id=1, source_target_pairs={{0,8},{8,0},{16,24},{24,16},{32,40},{40,32},{48,56},{56,48},{64,72... | collective-permute-start | bytes 786440 | tf_op jit(solution)/shard_map/ppermute | solution.py:19
  16.0 1.2 copy-start
  18.1 17.9 %all-to-all-start = ((bf16[8,4,8,8,128]{4,3,2,1,0:T(8,128)(2,1)}), bf16[8,4,8,8,128]{4,3,2,1,0:T(8,128)(2,1)}, u32[]{:S(2)}, u32[]{:S(2)}) async-start(bf16[8,4,8,8,128]{4,3,2,1,0:T(8,128)(2,1)} %copy.23), calls=%async_computation | async-start | bytes 1048576 | tf_op jit(solution)/shard_map/all_to_all | solution.py:41
  26.1 18.7 %collective-permute-start.2 = (bf16[6,1,64,256]{3,2,1,0:T(8,128)(2,1)}, bf16[6,1,64,256]{3,2,1,0:T(8,128)(2,1)S(1)}, u32[]{:S(2)}, u32[]{:S(2)}) collective-permute-start(bf16[6,1,64,256]{3,2,1,0:T(8,128)(2,1)} %pad_maximum_fusion.2), channel_id=1, source_target_pairs={{0,1},{1,2},{2,3},{3,4},{4,5},{5,6},{6,7},{8,9},{9,10},{10,11},{11... | collective-permute-start | bytes 589832 | tf_op jit(solution)/shard_map/ppermute | solution.py:27
  31.7 13.2 %collective-permute-start.3 = (bf16[6,1,64,256]{3,2,1,0:T(8,128)(2,1)}, bf16[6,1,64,256]{3,2,1,0:T(8,128)(2,1)S(1)}, u32[]{:S(2)}, u32[]{:S(2)}) collective-permute-start(bf16[6,1,64,256]{3,2,1,0:T(8,128)(2,1)} %pad_maximum_fusion.3), channel_id=1, source_target_pairs={{1,0},{2,1},{3,2},{4,3},{5,4},{6,5},{7,6},{9,8},{10,9},{11,10},{12... | collective-permute-start | bytes 589832 | tf_op jit(solution)/shard_map/ppermute | solution.py:28
  39.3 35.3 %all-to-all-start.1 = ((bf16[16,4,8,8,128]{4,3,2,1,0:T(8,128)(2,1)}), bf16[16,4,8,8,128]{4,3,2,1,0:T(8,128)(2,1)}, u32[]{:S(2)}, u32[]{:S(2)}) async-start(bf16[16,4,8,8,128]{4,3,2,1,0:T(8,128)(2,1)} %bitcast.70), calls=%async_computation.1 | async-start | bytes 2097152 | tf_op jit(solution)/shard_map/all_to_all | solution.py:428
  52.2 2.1 %copy-start.1 = (bf16[7,256,1280]{2,1,0:T(8,128)(2,1)}, bf16[7,256,1280]{2,1,0:T(8,128)(2,1)S(1)}, u32[]{:S(2)}) copy-start(bf16[7,256,1280]{2,1,0:T(8,128)(2,1)S(1)} %get-tuple-element.23.xt) | copy-start | bytes 13762564
  54.3 9.6 %collective-permute-start.6 = (bf16[2,2,128,128]{3,2,1,0:T(8,128)(2,1)S(1)}, bf16[2,2,128,128]{3,2,1,0:T(8,128)(2,1)S(1)}, u32[]{:S(2)}, u32[]{:S(2)}) collective-permute-start(bf16[2,2,128,128]{3,2,1,0:T(8,128)(2,1)S(1)} %get-tuple-element.42), channel_id=1, source_target_pairs={{0,1},{1,2},{2,3},{3,4},{4,5},{5,6},{6,7},{8,9},{9,10},{10,11},{11... | collective-permute-start | bytes 393224 | tf_op jit(solution)/shard_map/ppermute | solution.py:27
  59.3 11.0 %collective-permute-start.7 = (bf16[2,2,128,128]{3,2,1,0:T(8,128)(2,1)S(1)}, bf16[2,2,128,128]{3,2,1,0:T(8,128)(2,1)S(1)}, u32[]{:S(2)}, u32[]{:S(2)}) collective-permute-start(bf16[2,2,128,128]{3,2,1,0:T(8,128)(2,1)S(1)} %get-tuple-element.41), channel_id=1, source_target_pairs={{1,0},{2,1},{3,2},{4,3},{5,4},{6,5},{7,6},{9,8},{10,9},{11,10},{12... | collective-permute-start | bytes 393224 | tf_op jit(solution)/shard_map/ppermute | solution.py:28
  60.6 23.5 %collective-permute-start.5 = (bf16[2,4,128,128]{3,2,1,0:T(8,128)(2,1)S(1)}, bf16[2,4,128,128]{3,2,1,0:T(8,128)(2,1)S(1)}, u32[]{:S(2)}, u32[]{:S(2)}) collective-permute-start(bf16[2,4,128,128]{3,2,1,0:T(8,128)(2,1)S(1)} %get-tuple-element.18.own), channel_id=1, source_target_pairs={{8,16},{16,8},{24,32},{32,24},{40,48},{48,40},{56,64},{64,56},{72,... | collective-permute-start | bytes 786440 | tf_op jit(solution)/shard_map/ppermute | solution.py:20
  63.9 20.3 %collective-permute-start.4 = (bf16[2,4,128,128]{3,2,1,0:T(8,128)(2,1)S(1)}, bf16[2,4,128,128]{3,2,1,0:T(8,128)(2,1)S(1)}, u32[]{:S(2)}, u32[]{:S(2)}) collective-permute-start(bf16[2,4,128,128]{3,2,1,0:T(8,128)(2,1)S(1)} %get-tuple-element.18.own), channel_id=1, source_target_pairs={{0,8},{8,0},{16,24},{24,16},{32,40},{40,32},{48,56},{56,48},{64,72... | collective-permute-start | bytes 786440 | tf_op jit(solution)/shard_map/ppermute | solution.py:19
  70.3 13.8 %collective-permute-start.9 = (bf16[2,4,128,128]{3,2,1,0:T(8,128)(2,1)S(1)}, bf16[2,4,128,128]{3,2,1,0:T(8,128)(2,1)S(1)}, u32[]{:S(2)}, u32[]{:S(2)}) collective-permute-start(bf16[2,4,128,128]{3,2,1,0:T(8,128)(2,1)S(1)} %constant_dynamic-update-slice_fusion.ends), channel_id=1, source_target_pairs={{8,16},{16,8},{24,32},{32,24},{40,48},{48,40},{56,64},{64,56},{72,... | collective-permute-start | bytes 786440 | tf_op jit(solution)/shard_map/ppermute | solution.py:20
  74.4 9.7 %collective-permute-start.8 = (bf16[2,4,128,128]{3,2,1,0:T(8,128)(2,1)S(1)}, bf16[2,4,128,128]{3,2,1,0:T(8,128)(2,1)S(1)}, u32[]{:S(2)}, u32[]{:S(2)}) collective-permute-start(bf16[2,4,128,128]{3,2,1,0:T(8,128)(2,1)S(1)} %constant_dynamic-update-slice_fusion.ends), channel_id=1, source_target_pairs={{0,8},{8,0},{16,24},{24,16},{32,40},{40,32},{48,56},{56,48},{64,72... | collective-permute-start | bytes 786440 | tf_op jit(solution)/shard_map/ppermute | solution.py:19
  76.9 2.5 %collective-permute-start.10 = (bf16[2,8,128,128]{3,2,1,0:T(8,128)(2,1)}, bf16[2,8,128,128]{3,2,1,0:T(8,128)(2,1)S(1)}, u32[]{:S(2)}, u32[]{:S(2)}) collective-permute-start(bf16[2,8,128,128]{3,2,1,0:T(8,128)(2,1)} %slice_select_fusion), channel_id=1, source_target_pairs={{0,8},{8,0},{16,24},{24,16},{32,40},{40,32},{48,56},{56,48},{64,72... | collective-permute-start | bytes 1572872 | tf_op jit(solution)/shard_map/ppermute | solution.py:33
  79.5 16.1 %slice-start = ((s8[4587520]{0:T(1024)(128)(4,1)}), s8[4194304]{0:T(1024)(128)(4,1)S(1)}, s32[]{:S(2)}) async-start(s8[4587520]{0:T(1024)(128)(4,1)} %bitcast.68), calls=%async_computation.7 | async-start | bytes 8388608
  84.2 11.4 %slice-start.1 = ((s8[4587520]{0:T(1024)(128)(4,1)}), s8[393216]{0:T(1024)(128)(4,1)S(1)}, s32[]{:S(2)}) async-start(s8[4587520]{0:T(1024)(128)(4,1)} %bitcast.68), calls=%async_computation.8 | async-start | bytes 786432
  95.4 9.6 %collective-permute-start.11 = (bf16[8,64,8,128]{3,2,1,0:T(8,128)(2,1)S(1)}, bf16[8,64,8,128]{3,2,1,0:T(8,128)(2,1)S(1)}, u32[]{:S(2)}, u32[]{:S(2)}) collective-permute-start(bf16[8,64,8,128]{3,2,1,0:T(8,128)(2,1)S(1)} %fusion.5), channel_id=1, source_target_pairs={{0,8},{8,0},{16,24},{24,16},{32,40},{40,32},{48,56},{56,48},{64,72... | collective-permute-start | bytes 3145736 | tf_op jit(solution)/shard_map/ppermute | solution.py:33
  103.2 1.7 collective-permute-start.12
  154.3 17.6 %all-to-all-start.5 = ((bf16[16,128,128]{2,1,0:T(8,128)(2,1)}), bf16[16,128,128]{2,1,0:T(8,128)(2,1)S(1)}, u32[]{:S(2)}, u32[]{:S(2)}) async-start(bf16[16,128,128]{2,1,0:T(8,128)(2,1)} %broadcast_in_dim.19), calls=%async_computation.5 | async-start | bytes 1048576 | tf_op jit(solution)/shard_map/all_to_all | solution.py:475
Sparse Core Ops, SparseCore 0:
  10.3 48.7 all-gather.1
